TPU v7x, 32 devices: a whole 2x2x4 slice. The times are simulated.
32 devices in a mesh: parts: 2 (over y), gz: 4 (over z), gy: 4 (over x, core).
Axes of the slice: x: 2, y: 2, z: 4, core: 2. Of those that a mesh axis runs over, the one named last changes fastest.
Arguments:
- initial_class_tags: int32 [64, 64, 384], P(('parts', 'gz'), 'gy'), parts along dimension 0, may hold values from 0 to 15
- depth_affinity: int32 [64, 64, 384], P(('parts', 'gz'), 'gy'), parts along dimension 0, may hold values from 0 to 255
- row_affinity: int32 [64, 64, 384], P(('parts', 'gz'), 'gy'), parts along dimension 0, may hold values from 0 to 255
- column_affinity: int32 [64, 64, 384], P(('parts', 'gz'), 'gy'), parts along dimension 0, may hold values from 0 to 255
Outputs:
- potentials: float32 [4, 64, 64, 384], P(None, ('parts', 'gz'), 'gy'), parts along dimension 1
There are 2 independent parts, one for each index of `parts`. A program takes and returns all parts, laid end to end along the dimension named above; each array names one. Nothing has to cross between parts.
All inputs are finite; a program needn't handle non-finite values.
Results may differ from a plain program's by a relative error of at most 0.00025.
Values sent between devices are 32-bit elements; how exact they have to be, the bound alone decides.
No kernel may reach another device: no remote copies, remote signals or barrier semaphores. Data moves between devices by JAX's collectives and lax.ppermute only.
A program may use at most 64 MiB of HBM per device.

v0:
```python
import functools

import jax
import jax.numpy as jnp
from jax import lax
from jax.experimental import pallas as pl
from jax.experimental.pallas import tpu as pltpu
from jax.sharding import PartitionSpec as P

LABELS = 4
PIVOT_FLOOR = 1e-7
LO, HI = 3, 4
VMEM = pltpu.VMEM


def even_partner(i, count):
    return i ^ 1 if (i ^ 1) < count else i


def odd_partner(i, count):
    j = ((i + 1) ^ 1) - 1
    return j if 0 <= j < count else i


def exchanged(array, axes, counts, pair):
    nz, ny = counts
    route = []
    for z in range(nz):
        for y in range(ny):
            pz, py = pair(z, y)
            if (pz, py) != (z, y):
                route.append((z * ny + y, pz * ny + py))
    return lax.ppermute(array, axes, route)


def pack_kernel(tags, wz, wy, wx, z_even, z_odd, y_even, y_odd, *corners):
    zi, yi = lax.axis_index("gz"), lax.axis_index("gy")
    depth, rows, cols = tags.shape
    z_is_odd, y_is_odd = zi % 2, yi % 2
    row = lax.broadcasted_iota(jnp.int32, (8, cols), 0)
    for up, out in ((1 - z_is_odd, z_even), (z_is_odd, z_odd)):
        start = up * (depth - 4)
        for i in range(4):
            out[i] = tags[start + i]
        start = up * (depth - 3)
        for a, ref in enumerate((wz, wy, wx)):
            for i in range(3):
                out[4 + 3 * a + i] = ref[start + i]

    def strips(sources, up, out):
        tile = pl.multiple_of(up * (rows - 8), 8)
        first = (row >= 4) == (up == 1)
        for k in range(0, len(sources), 2):
            (ra, pa), (rb, pb) = sources[k], sources[k + 1]
            a = ra[pa, pl.ds(tile, 8), :]
            b = rb[pb, pl.ds(tile, 8), :]
            out[k // 2] = jnp.where(first, a, pltpu.roll(b, 4, 0))

    y_ups = (1 - y_is_odd, y_is_odd)
    z_ups = (1 - z_is_odd, z_is_odd)
    for up, out in zip(y_ups, (y_even, y_odd)):
        strips([(ref, p) for ref in (tags, wz, wy, wx) for p in range(depth)], up, out)
    for n, out in enumerate(corners):
        z_up, y_up = z_ups[n // 2], y_ups[n % 2]
        sources = []
        for ref, width in ((tags, 3), (wz, 3), (wy, 2), (wx, 2)):
            start = z_up * (depth - width)
            sources += [(ref, start + i) for i in range(width)]
        strips(sources, y_up, out)


def pack(tags, wz, wy, wx):
    depth, rows, cols = tags.shape
    i32 = jnp.int32
    return pl.pallas_call(
        pack_kernel,
        out_shape=[jax.ShapeDtypeStruct((13, rows, cols), i32)] * 2
        + [jax.ShapeDtypeStruct((2 * depth, 8, cols), i32)] * 2
        + [jax.ShapeDtypeStruct((5, 8, cols), i32)] * 4,
        in_specs=[pl.BlockSpec(memory_space=VMEM)] * 4,
        out_specs=[pl.BlockSpec(memory_space=VMEM)] * 8,
        compiler_params=pltpu.CompilerParams(vmem_limit_bytes=16 * 2**20),
    )(tags, wz, wy, wx)


def krylov_kernel(
    counts, tags, wz, wy, wx, z_even, z_odd, y_even, y_odd, c_ee, c_eo, c_oe, c_oo,
    fields, moments,
    t_pad, w_pad, coef, b_pad, v1, v2, sums,
):
    nz, ny = counts
    zi, yi = lax.axis_index("gz"), lax.axis_index("gy")
    depth, rows, cols = tags.shape
    z_is_even, y_is_even = zi % 2 == 0, yi % 2 == 0
    wide = rows + 8
    f32 = jnp.float32
    half = lax.broadcasted_iota(jnp.int32, (8, cols), 0) < 4
    row = lax.broadcasted_iota(jnp.int32, (wide, cols), 0)
    col = lax.broadcasted_iota(jnp.int32, (wide, cols), 1)
    own = slice(0, rows)
    ring = slice(rows, wide)

    def weight(values):
        return (values.astype(f32) + 1.0) * (1.0 / 256.0)

    def put(a, plane, where, values):
        if a == 0:
            t_pad[plane, where, :] = values
        else:
            w_pad[a - 1, plane, where, :] = weight(values)

    def strip_pair(from_next, from_prev):
        first = jnp.where(half, from_next, from_prev)
        second = pltpu.roll(jnp.where(half, from_prev, from_next), 4, 0)
        return first, second

    arrays = (tags, wz, wy, wx)
    for a, ref in enumerate(arrays):
        for p in range(depth):
            put(a, LO + p, own, ref[p])
    for i in range(13):
        e, o = z_even[i], z_odd[i]
        after = jnp.where(z_is_even, e, o)
        before = jnp.where(z_is_even, o, e)
        if i < 4:
            put(0, LO + depth + i, own, after)
            if i >= 1:
                put(0, i - 1, own, before)
        else:
            a, k = 1 + (i - 4) // 3, (i - 4) % 3
            put(a, LO + depth + k, own, after)
            put(a, k, own, before)
    for k in range(2 * depth):
        e, o = y_even[k], y_odd[k]
        pair = strip_pair(jnp.where(y_is_even, e, o), jnp.where(y_is_even, o, e))
        for j in range(2):
            a, p = divmod(2 * k + j, depth)
            put(a, LO + p, ring, pair[j])
    places = [(0, 0), (0, 1), (0, 2), (1, 0), (1, 1), (1, 2), (2, 0), (2, 1), (3, 0), (3, 1)]
    for k in range(5):
        ee, eo, oe, oo = c_ee[k], c_eo[k], c_oe[k], c_oo[k]
        e_next, e_prev = jnp.where(y_is_even, ee, eo), jnp.where(y_is_even, eo, ee)
        o_next, o_prev = jnp.where(y_is_even, oe, oo), jnp.where(y_is_even, oo, oe)
        after = strip_pair(
            jnp.where(z_is_even, e_next, o_next), jnp.where(z_is_even, e_prev, o_prev)
        )
        before = strip_pair(
            jnp.where(z_is_even, o_next, e_next), jnp.where(z_is_even, o_prev, e_prev)
        )
        for j in range(2):
            a, i = places[2 * k + j]
            put(a, LO + depth + i, ring, after[j])
            put(a, i + (1 if a >= 2 else 0), ring, before[j])
    zero_tile = jnp.zeros((8, cols), jnp.int32)
    put(0, LO + depth + 3, ring, zero_tile)
    put(1, LO + depth + 2, ring, zero_tile)
    for a in (2, 3):
        put(a, LO + depth + 2, ring, zero_tile)
        put(a, 0, ring, zero_tile)

    w_pad[0, LO + depth - 1] = jnp.where(zi == nz - 1, 0.0, w_pad[0, LO + depth - 1])
    w_pad[0, LO - 1] = jnp.where(zi == 0, 0.0, w_pad[0, LO - 1])
    last_row = jnp.where(yi == ny - 1, rows - 1, -1)
    first_row = jnp.where(yi == 0, wide - 1, -1)
    y_cut = (row == last_row) | (row == first_row)
    x_cut = col == cols - 1

    def prepare(p, _):
        tag = t_pad[p]
        w_z, w_zb = w_pad[0, p], w_pad[0, p - 1]
        w_y = jnp.where(y_cut, 0.0, w_pad[1, p])
        w_x = jnp.where(x_cut, 0.0, w_pad[2, p])
        w_yb, w_xb = pltpu.roll(w_y, 1, 0), pltpu.roll(w_x, 1, 1)
        free = tag >= 4
        degree = (w_z + w_zb) + (w_y + w_yb) + (w_x + w_xb)
        weights = [jnp.where(free, w, 0.0) for w in (w_z, w_zb, w_y, w_yb, w_x, w_xb, degree)]
        for i, w in enumerate(weights):
            coef[i, p] = w
        near = (
            t_pad[p + 1], t_pad[p - 1],
            pltpu.roll(tag, wide - 1, 0), pltpu.roll(tag, 1, 0),
            pltpu.roll(tag, cols - 1, 1), pltpu.roll(tag, 1, 1),
        )
        for c in range(LABELS):
            terms = [jnp.where(n == c, w, 0.0) for n, w in zip(near, weights)]
            b_pad[c, p] = (terms[0] + terms[1]) + (terms[2] + terms[3]) + (terms[4] + terms[5])
        return 0

    lax.fori_loop(1, LO + depth + 3, prepare, 0)

    def apply(source, target):
        def body(p, _):
            for c in range(LABELS):
                v = source[c, p]
                z = coef[0, p] * source[c, p + 1] + coef[1, p] * source[c, p - 1]
                y = coef[2, p] * pltpu.roll(v, wide - 1, 0) + coef[3, p] * pltpu.roll(v, 1, 0)
                x = coef[4, p] * pltpu.roll(v, cols - 1, 1) + coef[5, p] * pltpu.roll(v, 1, 1)
                target[c, p] = coef[6, p] * v - (z + y + x)
            return 0
        return body

    lax.fori_loop(2, LO + depth + 2, apply(b_pad, v1), 0)
    lax.fori_loop(3, LO + depth + 1, apply(v1, v2), 0)

    spots = [(r, l) for r in range(0, rows, 8) for l in range(0, cols, 128)]
    half_pairs = [(a, b) for a in range(LABELS) for b in range(a, LABELS)]
    all_pairs = [(a, b) for a in range(LABELS) for b in range(LABELS)]

    def block(ref, c, p, spot):
        return ref[c, p, spot[0] : spot[0] + 8, spot[1] : spot[1] + 128]

    def total(products):
        while len(products) > 1:
            products = [x + y for x, y in zip(products[::2], products[1::2])] + (
                [products[-1]] if len(products) % 2 else []
            )
        return products[0]

    def accumulate(p, acc):
        parts = [[] for _ in acc]
        for spot in spots:
            b = [block(b_pad, c, p, spot) for c in range(LABELS)]
            ab = [block(v1, c, p, spot) for c in range(LABELS)]
            products = [b[i] * b[j] for i, j in half_pairs]
            products += [b[i] * ab[j] for i, j in half_pairs]
            products += [ab[i] * ab[j] for i, j in half_pairs]
            for part, product in zip(parts, products):
                part.append(product)
            for c in range(LABELS):
                where = (p - LO, slice(spot[0], spot[0] + 8), slice(spot[1], spot[1] + 128))
                fields[(0, c) + where] = b[c]
                fields[(1, c) + where] = ab[c]
        return tuple(x + total(part) for x, part in zip(acc, parts))

    def accumulate_last(p, acc):
        parts = [[] for _ in acc]
        ahead = []
        for c in range(LABELS):
            v = v2[c, p]
            n = coef[0, p] * v2[c, p + 1] + coef[2, p] * pltpu.roll(v, wide - 1, 0)
            n = n + coef[4, p] * pltpu.roll(v, cols - 1, 1)
            ahead.append(coef[6, p] * v - 2.0 * n)
        for spot in spots:
            cut = (slice(spot[0], spot[0] + 8), slice(spot[1], spot[1] + 128))
            ab = [block(v1, c, p, spot) for c in range(LABELS)]
            aab = [block(v2, c, p, spot) for c in range(LABELS)]
            q = [x[cut] for x in ahead]
            products = [ab[i] * aab[j] for i, j in half_pairs]
            products += [aab[i] * aab[j] for i, j in half_pairs]
            products += [aab[i] * q[j] for i, j in all_pairs]
            for part, product in zip(parts, products):
                part.append(product)
            for c in range(LABELS):
                fields[(2, c, p - LO) + cut] = aab[c]
        return tuple(x + total(part) for x, part in zip(acc, parts))

    zero = jnp.zeros((8, 128), f32)
    low = lax.fori_loop(LO, LO + depth, accumulate, (zero,) * 30)
    high = lax.fori_loop(LO, LO + depth, accumulate_last, (zero,) * 36)
    kept = {}
    for k in range(5):
        part = low[10 * k : 10 * k + 10] if k < 3 else high[10 * (k - 3) : 10 * (k - 3) + 10]
        for (a, b), x in zip(half_pairs, part):
            kept[k, a, b] = kept[k, b, a] = x
    last = dict(zip(all_pairs, high[20:]))
    for a, b in half_pairs:
        kept[5, a, b] = kept[5, b, a] = 0.5 * (last[a, b] + last[b, a])
    for k in range(6):
        for a, b in half_pairs:
            x = jnp.sum(kept[k, a, b], axis=0, keepdims=True)
            for i, j in {(a, b), (b, a)}:
                at = (2 * k + j // 2) * 8 + (j % 2) * 4 + i
                sums[at : at + 1, :] = x
    lane = lax.broadcasted_iota(jnp.int32, (8, 128), 1)
    packed = zero
    for g in range(12):
        x = jnp.sum(sums[8 * g : 8 * g + 8, :], axis=1, keepdims=True)
        packed = jnp.where(lane == g, x, packed)
    moments[...] = packed


def krylov(counts, arrays, halos):
    depth, rows, cols = arrays[0].shape
    planes, wide = depth + LO + HI, rows + 8
    f32 = jnp.float32
    return pl.pallas_call(
        functools.partial(krylov_kernel, counts),
        out_shape=[
            jax.ShapeDtypeStruct((3, LABELS, depth, rows, cols), f32),
            jax.ShapeDtypeStruct((8, 128), f32),
        ],
        in_specs=[pl.BlockSpec(memory_space=VMEM)] * 12,
        out_specs=[pl.BlockSpec(memory_space=VMEM)] * 2,
        scratch_shapes=[
            VMEM((planes, wide, cols), jnp.int32),
            VMEM((3, planes, wide, cols), f32),
            VMEM((7, planes, wide, cols), f32),
            VMEM((LABELS, planes, wide, cols), f32),
            VMEM((LABELS, planes, wide, cols), f32),
            VMEM((LABELS, planes, wide, cols), f32),
            VMEM((96, 128), f32),
        ],
        compiler_params=pltpu.CompilerParams(vmem_limit_bytes=48 * 2**20),
    )(*arrays, *halos)


def combine_kernel(mine, theirs, fields, tags, out, coeffs):
    f32 = jnp.float32
    depth, rows, cols = tags.shape
    sums = mine[...] + theirs[...]
    lane = lax.broadcasted_iota(jnp.int32, (8, 128), 1)
    row = lax.broadcasted_iota(jnp.int32, (8, 128), 0)

    def splat(column):
        return jnp.broadcast_to(column, (8, 128))

    columns = {}
    for k in range(6):
        for h in range(2):
            x = splat(sums[:, 2 * k + h : 2 * k + h + 1])
            columns[k, 2 * h] = x
            columns[k, 2 * h + 1] = pltpu.roll(x, 4, 0)
    blocks = []
    for i in range(3):
        x = jnp.zeros((8, 128), f32)
        for j, k in enumerate((i + 1, i + 2, i + 3, i)):
            for b in range(LABELS):
                x = jnp.where(lane == 4 * j + b, columns[k, b], x)
        blocks.append(x)
    system = [
        jnp.where(row < 4, blocks[0], pltpu.roll(blocks[1], 4, 0)),
        jnp.where(row < 4, blocks[2], 0.0),
    ]
    start = list(system)
    for k in range(3 * LABELS):
        n, r = divmod(k, 8)
        pivot_row = system[n][r : r + 1, :]
        pivot = pivot_row[:, k : k + 1]
        sound = pivot > PIVOT_FLOOR * start[n][r : r + 1, k : k + 1]
        scale = jnp.where(sound, 1.0 / jnp.where(sound, pivot, 1.0), 0.0)
        pivot_row = pivot_row * scale
        for m in range(2):
            x = system[m] - system[m][:, k : k + 1] * pivot_row
            system[m] = jnp.where(row == r, pivot_row, x) if m == n else x
    for c in range(LABELS):
        for m in range(2):
            at = 3 * LABELS + c
            coeffs[c, 8 * m : 8 * m + 8, :] = splat(system[m][:, at : at + 1])

    for first in range(0, LABELS, 2):
        weights = {
            (c, k): jnp.broadcast_to(coeffs[c, k : k + 1, :], (8, 128))
            for c in (first, first + 1)
            for k in range(3 * LABELS)
        }

        def body(p, _):
            for r in range(0, rows, 8):
                for l in range(0, cols, 128):
                    cut = (p, slice(r, r + 8), slice(l, l + 128))
                    v = [fields[(k // LABELS, k % LABELS) + cut] for k in range(3 * LABELS)]
                    tag = tags[cut]
                    for c in (first, first + 1):
                        s = [v[k] * weights[c, k] for k in range(3 * LABELS)]
                        while len(s) > 1:
                            s = [x + y for x, y in zip(s[::2], s[1::2])] + (
                                [s[-1]] if len(s) % 2 else []
                            )
                        out[(c,) + cut] = jnp.where(tag == c, 1.0, s[0])
            return 0

        lax.fori_loop(0, depth, body, 0)


def combined(mine, theirs, fields, tags):
    return pl.pallas_call(
        combine_kernel,
        out_shape=jax.ShapeDtypeStruct((LABELS,) + tags.shape, jnp.float32),
        in_specs=[pl.BlockSpec(memory_space=VMEM)] * 4,
        out_specs=pl.BlockSpec(memory_space=VMEM),
        scratch_shapes=[VMEM((LABELS, 16, 128), jnp.float32)],
        compiler_params=pltpu.CompilerParams(vmem_limit_bytes=32 * 2**20),
    )(mine, theirs, fields, tags)


def per_device(counts, tags, depth_affinity, row_affinity, column_affinity):
    nz, ny = counts
    arrays = (tags, depth_affinity, row_affinity, column_affinity)
    axes = ("gz", "gy")
    packed = pack(*arrays)
    ze, zo = (lambda z: even_partner(z, nz)), (lambda z: odd_partner(z, nz))
    ye, yo = (lambda y: even_partner(y, ny)), (lambda y: odd_partner(y, ny))

    def z_pair(pz):
        return lambda z, y: (pz(z), y) if pz(z) != z else (z, ye(y))

    def y_pair(py):
        return lambda z, y: (z, py(y)) if py(y) != y else (ze(z), y)

    def corner(pz, py):
        def pair(z, y):
            if pz(z) != z and py(y) != y:
                return pz(z), py(y)
            return (pz(z), y) if pz(z) != z else (z, ye(y))
        return pair

    pairs = [z_pair(ze), z_pair(zo), y_pair(ye), y_pair(yo)]
    pairs += [corner(a, b) for a in (ze, zo) for b in (ye, yo)]
    halos = [exchanged(x, axes, counts, pair) for x, pair in zip(packed, pairs)]
    fields, moments = krylov(counts, arrays, halos)

    steps = [lambda z, y, d=d: (z, y ^ d) for d in powers(ny)]
    steps += [lambda z, y, d=d: (z ^ d, y) for d in powers(nz)]
    for n, pair in enumerate(steps):
        theirs = exchanged(moments, axes, counts, pair)
        if n < len(steps) - 1:
            moments = moments + theirs
    return combined(moments, theirs, fields, tags)


def powers(count):
    return [1 << n for n in range(count.bit_length() - 1)]


def solution(mesh):
    counts = (mesh.shape["gz"], mesh.shape["gy"])
    placed = P(("parts", "gz"), "gy", None)
    return jax.shard_map(
        functools.partial(per_device, counts),
        mesh=mesh,
        in_specs=(placed,) * 4,
        out_specs=P(None, ("parts", "gz"), "gy", None),
        check_vma=False,
    )
```

profile of v0, /device:TPU:0, one launch (start us, length us, event | category | flops | bytes accessed | tf_op | source)
XLA Modules:
  0.0 55.8 jit_solution(16119498424838228095)
XLA Ops:
  0.0 0.9 %copy-done = s32[8,16,384]{2,1,0:T(8,128)S(1)} copy-done((s32[8,16,384]{2,1,0:T(8,128)S(1)}, s32[8,16,384]{2,1,0:T(8,128)}, u32[]{:S(2)}) %copy-start) | copy-done | bytes 196632
  0.9 0.9 %copy-done.2 = s32[8,16,384]{2,1,0:T(8,128)S(1)} copy-done((s32[8,16,384]{2,1,0:T(8,128)S(1)}, s32[8,16,384]{2,1,0:T(8,128)}, u32[]{:S(2)}) %copy-start.2) | copy-done | bytes 196632
  1.9 0.9 %copy-done.4 = s32[8,16,384]{2,1,0:T(8,128)S(1)} copy-done((s32[8,16,384]{2,1,0:T(8,128)S(1)}, s32[8,16,384]{2,1,0:T(8,128)}, u32[]{:S(2)}) %copy-start.4) | copy-done | bytes 196632
  2.8 0.9 %copy-done.6 = s32[8,16,384]{2,1,0:T(8,128)S(1)} copy-done((s32[8,16,384]{2,1,0:T(8,128)S(1)}, s32[8,16,384]{2,1,0:T(8,128)}, u32[]{:S(2)}) %copy-start.6) | copy-done | bytes 196632
  3.8 3.1 %collective-permute-start = (s32[13,16,384]{2,1,0:T(8,128)S(1)}, s32[13,16,384]{2,1,0:T(8,128)S(1)}, u32[]{:S(2)}, u32[]{:S(2)}) collective-permute-start(s32[13,16,384]{2,1,0:T(8,128)S(1)} %get-tuple-element.15), channel_id=1, source_target_pairs={{0,4},{1,5},{2,6},{3,7},{4,0},{5,1},{6,2},{7,3},{8,12},{9,13},{10,... | collective-permute-start | bytes 958472 | tf_op jit(solution)/shard_map/ppermute | solution.py:33
  6.9 2.0 %collective-permute-start.4 = (s32[5,8,384]{2,1,0:T(8,128)S(1)}, s32[5,8,384]{2,1,0:T(8,128)S(1)}, u32[]{:S(2)}, u32[]{:S(2)}) collective-permute-start(s32[5,8,384]{2,1,0:T(8,128)S(1)} %get-tuple-element.19), channel_id=1, source_target_pairs={{0,5},{1,4},{2,7},{3,6},{4,1},{5,0},{6,3},{7,2},{8,13},{9,12},{10,... | collective-permute-start | bytes 184328 | tf_op jit(solution)/shard_map/ppermute | solution.py:33
  8.9 1.2 %collective-permute-start.2 = (s32[16,8,384]{2,1,0:T(8,128)S(1)}, s32[16,8,384]{2,1,0:T(8,128)S(1)}, u32[]{:S(2)}, u32[]{:S(2)}) collective-permute-start(s32[16,8,384]{2,1,0:T(8,128)S(1)} %get-tuple-element.17), channel_id=1, source_target_pairs={{0,1},{1,0},{2,3},{3,2},{4,5},{5,4},{6,7},{7,6},{8,9},{9,8},{10,11... | collective-permute-start | bytes 589832 | tf_op jit(solution)/shard_map/ppermute | solution.py:33
  10.2 4.8 %collective-permute-done.4.c_ee = s32[5,8,384]{2,1,0:T(8,128)S(1)} collective-permute-done((s32[5,8,384]{2,1,0:T(8,128)S(1)}, s32[5,8,384]{2,1,0:T(8,128)S(1)}, u32[]{:S(2)}, u32[]{:S(2)}) %collective-permute-start.4) | collective-permute-done | bytes 61472 | tf_op jit(solution)/shard_map/ppermute | solution.py:33
  15.0 1.3 %collective-permute-start.5 = (s32[5,8,384]{2,1,0:T(8,128)S(1)}, s32[5,8,384]{2,1,0:T(8,128)S(1)}, u32[]{:S(2)}, u32[]{:S(2)}) collective-permute-start(s32[5,8,384]{2,1,0:T(8,128)S(1)} %get-tuple-element.20), channel_id=1, source_target_pairs={{0,4},{1,6},{2,5},{3,7},{4,0},{5,2},{6,1},{7,3},{8,12},{9,14},{10,... | collective-permute-start | bytes 184328 | tf_op jit(solution)/shard_map/ppermute | solution.py:33
  16.3 2.9 %collective-permute-done.5.c_eo = s32[5,8,384]{2,1,0:T(8,128)S(1)} collective-permute-done((s32[5,8,384]{2,1,0:T(8,128)S(1)}, s32[5,8,384]{2,1,0:T(8,128)S(1)}, u32[]{:S(2)}, u32[]{:S(2)}) %collective-permute-start.5) | collective-permute-done | bytes 61472 | tf_op jit(solution)/shard_map/ppermute | solution.py:33
  20.1 0.9 %collective-permute-done.6.c_oe = s32[5,8,384]{2,1,0:T(8,128)S(1)} collective-permute-done((s32[5,8,384]{2,1,0:T(8,128)S(1)}, s32[5,8,384]{2,1,0:T(8,128)S(1)}, u32[]{:S(2)}, u32[]{:S(2)}) %collective-permute-start.6) | collective-permute-done | bytes 61472 | tf_op jit(solution)/shard_map/ppermute | solution.py:33
  21.4 0.9 %collective-permute-done.7.c_oo = s32[5,8,384]{2,1,0:T(8,128)S(1)} collective-permute-done((s32[5,8,384]{2,1,0:T(8,128)S(1)}, s32[5,8,384]{2,1,0:T(8,128)S(1)}, u32[]{:S(2)}, u32[]{:S(2)}) %collective-permute-start.7) | collective-permute-done | bytes 61472 | tf_op jit(solution)/shard_map/ppermute | solution.py:33
  22.3 0.9 %copy-done.1 = s32[8,16,384]{2,1,0:T(8,128)S(1)} copy-done((s32[8,16,384]{2,1,0:T(8,128)S(1)}, s32[8,16,384]{2,1,0:T(8,128)}, u32[]{:S(2)}) %copy-start.1) | copy-done | bytes 196632
  23.2 0.9 %copy-done.3 = s32[8,16,384]{2,1,0:T(8,128)S(1)} copy-done((s32[8,16,384]{2,1,0:T(8,128)S(1)}, s32[8,16,384]{2,1,0:T(8,128)}, u32[]{:S(2)}) %copy-start.3) | copy-done | bytes 196632
  24.2 0.9 %copy-done.5 = s32[8,16,384]{2,1,0:T(8,128)S(1)} copy-done((s32[8,16,384]{2,1,0:T(8,128)S(1)}, s32[8,16,384]{2,1,0:T(8,128)}, u32[]{:S(2)}) %copy-start.5) | copy-done | bytes 196632
  25.1 0.9 %copy-done.7 = s32[8,16,384]{2,1,0:T(8,128)S(1)} copy-done((s32[8,16,384]{2,1,0:T(8,128)S(1)}, s32[8,16,384]{2,1,0:T(8,128)}, u32[]{:S(2)}) %copy-start.7) | copy-done | bytes 196632
  26.0 7.3 %shard_map.47 = (f32[3,4,8,16,384]{4,3,2,1,0:T(8,128)S(1)}, f32[8,128]{1,0:T(8,128)S(1)}) custom-call(s32[8,16,384]{2,1,0:T(8,128)S(1)} %copy-done.1, s32[8,16,384]{2,1,0:T(8,128)S(1)} %copy-done.3, s32[8,16,384]{2,1,0:T(8,128)S(1)} %copy-done.5, s32[8,16,384]{2,1,0:T(8,128)S(1)} %copy-done.7, s32[13,16,384]{2,1,0:T(8,128)S(1)} %collective-permute-done.z_even, ...), custom_call_target="tpu_custom_call" | custom-call | tf_op jit(solution)/shard_map/pallas_call | solution.py:286
  34.5 2.4 %collective-permute-start.9 = (f32[8,128]{1,0:T(8,128)S(1)}, f32[8,128]{1,0:T(8,128)S(1)}, u32[]{:S(2)}, u32[]{:S(2)}) collective-permute-start(f32[8,128]{1,0:T(8,128)S(1)} %add.9), channel_id=1, source_target_pairs={{0,2},{1,3},{2,0},{3,1},{4,6},{5,7},{6,4},{7,5},{8,10},{9,11},{10,... | collective-permute-start | bytes 12296 | tf_op jit(solution)/shard_map/ppermute | solution.py:33
  36.9 1.6 %collective-permute-done.9 = f32[8,128]{1,0:T(8,128)S(1)} collective-permute-done((f32[8,128]{1,0:T(8,128)S(1)}, f32[8,128]{1,0:T(8,128)S(1)}, u32[]{:S(2)}, u32[]{:S(2)}) %collective-permute-start.9) | collective-permute-done | bytes 4128 | tf_op jit(solution)/shard_map/ppermute | solution.py:33
  38.5 8.1 %collective-permute-start.10 = (f32[8,128]{1,0:T(8,128)S(1)}, f32[8,128]{1,0:T(8,128)S(1)}, u32[]{:S(2)}, u32[]{:S(2)}) collective-permute-start(f32[8,128]{1,0:T(8,128)S(1)} %add.10), channel_id=1, source_target_pairs={{0,4},{1,5},{2,6},{3,7},{4,0},{5,1},{6,2},{7,3},{8,12},{9,13},{10,... | collective-permute-start | bytes 12296 | tf_op jit(solution)/shard_map/ppermute | solution.py:33
  46.6 1.6 %collective-permute-done.10 = f32[8,128]{1,0:T(8,128)S(1)} collective-permute-done((f32[8,128]{1,0:T(8,128)S(1)}, f32[8,128]{1,0:T(8,128)S(1)}, u32[]{:S(2)}, u32[]{:S(2)}) %collective-permute-start.10) | collective-permute-done | bytes 4128 | tf_op jit(solution)/shard_map/ppermute | solution.py:33
  48.2 3.2 %collective-permute-start.11 = (f32[8,128]{1,0:T(8,128)S(1)}, f32[8,128]{1,0:T(8,128)S(1)}, u32[]{:S(2)}, u32[]{:S(2)}) collective-permute-start(f32[8,128]{1,0:T(8,128)S(1)} %add.11.mine), channel_id=1, source_target_pairs={{0,8},{1,9},{2,10},{3,11},{4,12},{5,13},{6,14},{7,15},{8,0},{9,1},... | collective-permute-start | bytes 12296 | tf_op jit(solution)/shard_map/ppermute | solution.py:33
  51.4 1.6 %collective-permute-done.11.theirs = f32[8,128]{1,0:T(8,128)S(1)} collective-permute-done((f32[8,128]{1,0:T(8,128)S(1)}, f32[8,128]{1,0:T(8,128)S(1)}, u32[]{:S(2)}, u32[]{:S(2)}) %collective-permute-start.11) | collective-permute-done | bytes 4128 | tf_op jit(solution)/shard_map/ppermute | solution.py:33
  53.0 2.7 %shard_map.48 = f32[4,8,16,384]{3,2,1,0:T(8,128)} custom-call(f32[8,128]{1,0:T(8,128)S(1)} %add.11.mine, f32[8,128]{1,0:T(8,128)S(1)} %collective-permute-done.11.theirs, f32[3,4,8,16,384]{4,3,2,1,0:T(8,128)S(1)} %get-tuple-element.24.fields, s32[8,16,384]{2,1,0:T(8,128)S(1)} %copy-done.1), custom_call_target="tpu_custom_call" | custom-call | tf_op jit(solution)/shard_map/pallas_call | solution.py:376
  (22 shorter events, 2.6 us)
Async XLA Ops:
  0.0 0.9 %copy-start = (s32[8,16,384]{2,1,0:T(8,128)S(1)}, s32[8,16,384]{2,1,0:T(8,128)}, u32[]{:S(2)}) copy-start(s32[8,16,384]{2,1,0:T(8,128)} %tags.5) | copy-start | bytes 589828
  0.9 0.9 %copy-start.2 = (s32[8,16,384]{2,1,0:T(8,128)S(1)}, s32[8,16,384]{2,1,0:T(8,128)}, u32[]{:S(2)}) copy-start(s32[8,16,384]{2,1,0:T(8,128)} %wz.3) | copy-start | bytes 589828
  1.9 0.9 %copy-start.4 = (s32[8,16,384]{2,1,0:T(8,128)S(1)}, s32[8,16,384]{2,1,0:T(8,128)}, u32[]{:S(2)}) copy-start(s32[8,16,384]{2,1,0:T(8,128)} %wy.3) | copy-start | bytes 589828
  2.8 0.9 %copy-start.6 = (s32[8,16,384]{2,1,0:T(8,128)S(1)}, s32[8,16,384]{2,1,0:T(8,128)}, u32[]{:S(2)}) copy-start(s32[8,16,384]{2,1,0:T(8,128)} %wx.3) | copy-start | bytes 589828
  3.8 18.5 %collective-permute-start = (s32[13,16,384]{2,1,0:T(8,128)S(1)}, s32[13,16,384]{2,1,0:T(8,128)S(1)}, u32[]{:S(2)}, u32[]{:S(2)}) collective-permute-start(s32[13,16,384]{2,1,0:T(8,128)S(1)} %get-tuple-element.15), channel_id=1, source_target_pairs={{0,4},{1,5},{2,6},{3,7},{4,0},{5,1},{6,2},{7,3},{8,12},{9,13},{10,... | collective-permute-start | bytes 958472 | tf_op jit(solution)/shard_map/ppermute | solution.py:33
  6.9 15.4 %collective-permute-start.1 = (s32[13,16,384]{2,1,0:T(8,128)S(1)}, s32[13,16,384]{2,1,0:T(8,128)S(1)}, u32[]{:S(2)}, u32[]{:S(2)}) collective-permute-start(s32[13,16,384]{2,1,0:T(8,128)S(1)} %get-tuple-element.16), channel_id=1, source_target_pairs={{0,1},{1,0},{2,3},{3,2},{4,8},{5,9},{6,10},{7,11},{8,4},{9,5},{10,... | collective-permute-start | bytes 958472 | tf_op jit(solution)/shard_map/ppermute | solution.py:33
  6.9 8.1 %collective-permute-start.4 = (s32[5,8,384]{2,1,0:T(8,128)S(1)}, s32[5,8,384]{2,1,0:T(8,128)S(1)}, u32[]{:S(2)}, u32[]{:S(2)}) collective-permute-start(s32[5,8,384]{2,1,0:T(8,128)S(1)} %get-tuple-element.19), channel_id=1, source_target_pairs={{0,5},{1,4},{2,7},{3,6},{4,1},{5,0},{6,3},{7,2},{8,13},{9,12},{10,... | collective-permute-start | bytes 184328 | tf_op jit(solution)/shard_map/ppermute | solution.py:33
  8.9 13.3 %collective-permute-start.2 = (s32[16,8,384]{2,1,0:T(8,128)S(1)}, s32[16,8,384]{2,1,0:T(8,128)S(1)}, u32[]{:S(2)}, u32[]{:S(2)}) collective-permute-start(s32[16,8,384]{2,1,0:T(8,128)S(1)} %get-tuple-element.17), channel_id=1, source_target_pairs={{0,1},{1,0},{2,3},{3,2},{4,5},{5,4},{6,7},{7,6},{8,9},{9,8},{10,11... | collective-permute-start | bytes 589832 | tf_op jit(solution)/shard_map/ppermute | solution.py:33
  10.2 12.1 %collective-permute-start.3 = (s32[16,8,384]{2,1,0:T(8,128)S(1)}, s32[16,8,384]{2,1,0:T(8,128)S(1)}, u32[]{:S(2)}, u32[]{:S(2)}) collective-permute-start(s32[16,8,384]{2,1,0:T(8,128)S(1)} %get-tuple-element.18), channel_id=1, source_target_pairs={{0,4},{1,2},{2,1},{3,7},{4,0},{5,6},{6,5},{7,3},{8,12},{9,10},{10,... | collective-permute-start | bytes 589832 | tf_op jit(solution)/shard_map/ppermute | solution.py:33
  15.0 4.2 %collective-permute-start.5 = (s32[5,8,384]{2,1,0:T(8,128)S(1)}, s32[5,8,384]{2,1,0:T(8,128)S(1)}, u32[]{:S(2)}, u32[]{:S(2)}) collective-permute-start(s32[5,8,384]{2,1,0:T(8,128)S(1)} %get-tuple-element.20), channel_id=1, source_target_pairs={{0,4},{1,6},{2,5},{3,7},{4,0},{5,2},{6,1},{7,3},{8,12},{9,14},{10,... | collective-permute-start | bytes 184328 | tf_op jit(solution)/shard_map/ppermute | solution.py:33
  19.2 1.8 %collective-permute-start.6 = (s32[5,8,384]{2,1,0:T(8,128)S(1)}, s32[5,8,384]{2,1,0:T(8,128)S(1)}, u32[]{:S(2)}, u32[]{:S(2)}) collective-permute-start(s32[5,8,384]{2,1,0:T(8,128)S(1)} %get-tuple-element.21), channel_id=1, source_target_pairs={{0,1},{1,0},{2,3},{3,2},{4,9},{5,8},{6,11},{7,10},{8,5},{9,4},{10,... | collective-permute-start | bytes 184328 | tf_op jit(solution)/shard_map/ppermute | solution.py:33
  21.0 1.2 %collective-permute-start.7 = (s32[5,8,384]{2,1,0:T(8,128)S(1)}, s32[5,8,384]{2,1,0:T(8,128)S(1)}, u32[]{:S(2)}, u32[]{:S(2)}) collective-permute-start(s32[5,8,384]{2,1,0:T(8,128)S(1)} %get-tuple-element.22), channel_id=1, source_target_pairs={{0,1},{1,0},{2,3},{3,2},{4,8},{5,10},{6,9},{7,11},{8,4},{9,6},{10,... | collective-permute-start | bytes 184328 | tf_op jit(solution)/shard_map/ppermute | solution.py:33
  22.3 0.9 %copy-start.1 = (s32[8,16,384]{2,1,0:T(8,128)S(1)}, s32[8,16,384]{2,1,0:T(8,128)}, u32[]{:S(2)}) copy-start(s32[8,16,384]{2,1,0:T(8,128)} %tags.5) | copy-start | bytes 589828
  23.2 0.9 %copy-start.3 = (s32[8,16,384]{2,1,0:T(8,128)S(1)}, s32[8,16,384]{2,1,0:T(8,128)}, u32[]{:S(2)}) copy-start(s32[8,16,384]{2,1,0:T(8,128)} %wz.3) | copy-start | bytes 589828
  24.2 0.9 %copy-start.5 = (s32[8,16,384]{2,1,0:T(8,128)S(1)}, s32[8,16,384]{2,1,0:T(8,128)}, u32[]{:S(2)}) copy-start(s32[8,16,384]{2,1,0:T(8,128)} %wy.3) | copy-start | bytes 589828
  25.1 0.9 %copy-start.7 = (s32[8,16,384]{2,1,0:T(8,128)S(1)}, s32[8,16,384]{2,1,0:T(8,128)}, u32[]{:S(2)}) copy-start(s32[8,16,384]{2,1,0:T(8,128)} %wx.3) | copy-start | bytes 589828
  33.3 1.2 %collective-permute-start.8 = (f32[8,128]{1,0:T(8,128)S(1)}, f32[8,128]{1,0:T(8,128)S(1)}, u32[]{:S(2)}, u32[]{:S(2)}) collective-permute-start(f32[8,128]{1,0:T(8,128)S(1)} %get-tuple-element.23), channel_id=1, source_target_pairs={{0,1},{1,0},{2,3},{3,2},{4,5},{5,4},{6,7},{7,6},{8,9},{9,8},{10,11... | collective-permute-start | bytes 12296 | tf_op jit(solution)/shard_map/ppermute | solution.py:33
  34.5 4.0 %collective-permute-start.9 = (f32[8,128]{1,0:T(8,128)S(1)}, f32[8,128]{1,0:T(8,128)S(1)}, u32[]{:S(2)}, u32[]{:S(2)}) collective-permute-start(f32[8,128]{1,0:T(8,128)S(1)} %add.9), channel_id=1, source_target_pairs={{0,2},{1,3},{2,0},{3,1},{4,6},{5,7},{6,4},{7,5},{8,10},{9,11},{10,... | collective-permute-start | bytes 12296 | tf_op jit(solution)/shard_map/ppermute | solution.py:33
  38.5 9.7 %collective-permute-start.10 = (f32[8,128]{1,0:T(8,128)S(1)}, f32[8,128]{1,0:T(8,128)S(1)}, u32[]{:S(2)}, u32[]{:S(2)}) collective-permute-start(f32[8,128]{1,0:T(8,128)S(1)} %add.10), channel_id=1, source_target_pairs={{0,4},{1,5},{2,6},{3,7},{4,0},{5,1},{6,2},{7,3},{8,12},{9,13},{10,... | collective-permute-start | bytes 12296 | tf_op jit(solution)/shard_map/ppermute | solution.py:33
  48.2 4.8 %collective-permute-start.11 = (f32[8,128]{1,0:T(8,128)S(1)}, f32[8,128]{1,0:T(8,128)S(1)}, u32[]{:S(2)}, u32[]{:S(2)}) collective-permute-start(f32[8,128]{1,0:T(8,128)S(1)} %add.11.mine), channel_id=1, source_target_pairs={{0,8},{1,9},{2,10},{3,11},{4,12},{5,13},{6,14},{7,15},{8,0},{9,1},... | collective-permute-start | bytes 12296 | tf_op jit(solution)/shard_map/ppermute | solution.py:33
where the time goes:
time: 56.1 us; the launch traced here: 55.8 us
  starting transfers between devices  23.1 us (41%)
  waiting for transfers between devices  15.1 us (27%)
  Pallas kernels  10.1 us (18%)
  local copies, waits for them, and re-layouts  7.41 us (13%)
    ppermute x12, starting transfers between devices, exchanged(): return lax.ppermute(array, axes, route)  23.1 us
    ppermute x12, waiting for transfers between devices, exchanged(): return lax.ppermute(array, axes, route)  15.1 us
    unnamed x16, local copies, waits for them, and re-layouts  7.41 us
    pallas_call x1, Pallas kernels, krylov(): pl.pallas_call(functools.partial(krylov_kernel, counts), out_shape=[jax.S...  7.28 us
    pallas_call x1, Pallas kernels, combined(): pl.pallas_call(combine_kernel, out_shape=jax.ShapeDtypeStruct((LABELS,) +...  2.74 us
  transfers between devices with their start and end apart: 12, of which 8 were waited for; matrix products, arithmetic and copies ran while one was open for 0% of the time, Pallas kernels for 0%

commit v1 on v0

--- a/solution.py
+++ b/solution.py
@@ -10,6 +10,8 @@
 LABELS = 4
 PIVOT_FLOOR = 1e-7
 LO, HI = 3, 4
+CORNER_WIDTHS = (3, 3, 2, 2)
+CORNERS = [(a, i) for a, width in enumerate(CORNER_WIDTHS) for i in range(width)]
 VMEM = pltpu.VMEM
 
 
@@ -33,9 +35,15 @@
     return lax.ppermute(array, axes, route)
 
 
-def pack_kernel(tags, wz, wy, wx, z_even, z_odd, y_even, y_odd, *corners):
+def pack_kernel(tags_hbm, wz_hbm, wy_hbm, wx_hbm, tags, wz, wy, wx, z_even, z_odd, y_even, y_odd, sems):
     zi, yi = lax.axis_index("gz"), lax.axis_index("gy")
     depth, rows, cols = tags.shape
+    hbm, own = (tags_hbm, wz_hbm, wy_hbm, wx_hbm), (tags, wz, wy, wx)
+    copies = [pltpu.make_async_copy(h, o, sems.at[n]) for n, (h, o) in enumerate(zip(hbm, own))]
+    for copy in copies:
+        copy.start()
+    for copy in copies:
+        copy.wait()
     z_is_odd, y_is_odd = zi % 2, yi % 2
     row = lax.broadcasted_iota(jnp.int32, (8, cols), 0)
     for up, out in ((1 - z_is_odd, z_even), (z_is_odd, z_odd)):
@@ -46,55 +54,70 @@
         for a, ref in enumerate((wz, wy, wx)):
             for i in range(3):
                 out[4 + 3 * a + i] = ref[start + i]
-
-    def strips(sources, up, out):
+    for up, out in ((1 - y_is_odd, y_even), (y_is_odd, y_odd)):
         tile = pl.multiple_of(up * (rows - 8), 8)
         first = (row >= 4) == (up == 1)
-        for k in range(0, len(sources), 2):
-            (ra, pa), (rb, pb) = sources[k], sources[k + 1]
-            a = ra[pa, pl.ds(tile, 8), :]
-            b = rb[pb, pl.ds(tile, 8), :]
-            out[k // 2] = jnp.where(first, a, pltpu.roll(b, 4, 0))
-
-    y_ups = (1 - y_is_odd, y_is_odd)
-    z_ups = (1 - z_is_odd, z_is_odd)
-    for up, out in zip(y_ups, (y_even, y_odd)):
-        strips([(ref, p) for ref in (tags, wz, wy, wx) for p in range(depth)], up, out)
-    for n, out in enumerate(corners):
-        z_up, y_up = z_ups[n // 2], y_ups[n % 2]
-        sources = []
-        for ref, width in ((tags, 3), (wz, 3), (wy, 2), (wx, 2)):
-            start = z_up * (depth - width)
-            sources += [(ref, start + i) for i in range(width)]
-        strips(sources, y_up, out)
-
-
-def pack(tags, wz, wy, wx):
-    depth, rows, cols = tags.shape
+        for k in range(2 * depth):
+            ref, p = own[2 * k // depth], 2 * k % depth
+            a, b = ref[p, pl.ds(tile, 8), :], ref[p + 1, pl.ds(tile, 8), :]
+            out[k] = jnp.where(first, a, pltpu.roll(b, 4, 0))
+
+
+def pack(*arrays):
+    depth, rows, cols = arrays[0].shape
     i32 = jnp.int32
     return pl.pallas_call(
         pack_kernel,
-        out_shape=[jax.ShapeDtypeStruct((13, rows, cols), i32)] * 2
-        + [jax.ShapeDtypeStruct((2 * depth, 8, cols), i32)] * 2
-        + [jax.ShapeDtypeStruct((5, 8, cols), i32)] * 4,
-        in_specs=[pl.BlockSpec(memory_space=VMEM)] * 4,
+        out_shape=[jax.ShapeDtypeStruct((depth, rows, cols), i32)] * 4
+        + [jax.ShapeDtypeStruct((13, rows, cols), i32)] * 2
+        + [jax.ShapeDtypeStruct((2 * depth, 8, cols), i32)] * 2,
+        in_specs=[pl.BlockSpec(memory_space=pltpu.HBM)] * 4,
         out_specs=[pl.BlockSpec(memory_space=VMEM)] * 8,
+        scratch_shapes=[pltpu.SemaphoreType.DMA((4,))],
         compiler_params=pltpu.CompilerParams(vmem_limit_bytes=16 * 2**20),
-    )(tags, wz, wy, wx)
+    )(*arrays)
+
+
+def ring_kernel(y_even, y_odd, rings, z_even, z_odd):
+    zi, yi = lax.axis_index("gz"), lax.axis_index("gy")
+    cols = rings.shape[2]
+    depth = rings.shape[0] // 4
+    half = lax.broadcasted_iota(jnp.int32, (8, cols), 0) < 4
+    from_next = half == (yi % 2 == 0)
+    for k in range(2 * depth):
+        e, o = y_even[k], y_odd[k]
+        rings[2 * k] = jnp.where(from_next, e, o)
+        rings[2 * k + 1] = pltpu.roll(jnp.where(from_next, o, e), 4, 0)
+    z_is_odd = zi % 2
+    for up, out in ((1 - z_is_odd, z_even), (z_is_odd, z_odd)):
+        for n, (a, i) in enumerate(CORNERS):
+            out[n] = rings[a * depth + up * (depth - CORNER_WIDTHS[a]) + i]
+
+
+def make_rings(y_even, y_odd):
+    tiles, _, cols = y_even.shape
+    i32 = jnp.int32
+    return pl.pallas_call(
+        ring_kernel,
+        out_shape=[jax.ShapeDtypeStruct((2 * tiles, 8, cols), i32)]
+        + [jax.ShapeDtypeStruct((len(CORNERS), 8, cols), i32)] * 2,
+        in_specs=[pl.BlockSpec(memory_space=VMEM)] * 2,
+        out_specs=[pl.BlockSpec(memory_space=VMEM)] * 3,
+        compiler_params=pltpu.CompilerParams(vmem_limit_bytes=16 * 2**20),
+    )(y_even, y_odd)
 
 
 def krylov_kernel(
-    counts, tags, wz, wy, wx, z_even, z_odd, y_even, y_odd, c_ee, c_eo, c_oe, c_oo,
+    counts, tags, wz, wy, wx, z_even, z_odd, rings, c_even, c_odd,
     fields, moments,
     t_pad, w_pad, coef, b_pad, v1, v2, sums,
 ):
     nz, ny = counts
     zi, yi = lax.axis_index("gz"), lax.axis_index("gy")
     depth, rows, cols = tags.shape
-    z_is_even, y_is_even = zi % 2 == 0, yi % 2 == 0
+    z_is_even = zi % 2 == 0
     wide = rows + 8
     f32 = jnp.float32
-    half = lax.broadcasted_iota(jnp.int32, (8, cols), 0) < 4
     row = lax.broadcasted_iota(jnp.int32, (wide, cols), 0)
     col = lax.broadcasted_iota(jnp.int32, (wide, cols), 1)
     own = slice(0, rows)
@@ -108,11 +131,6 @@
             t_pad[plane, where, :] = values
         else:
             w_pad[a - 1, plane, where, :] = weight(values)
-
-    def strip_pair(from_next, from_prev):
-        first = jnp.where(half, from_next, from_prev)
-        second = pltpu.roll(jnp.where(half, from_prev, from_next), 4, 0)
-        return first, second
 
     arrays = (tags, wz, wy, wx)
     for a, ref in enumerate(arrays):
@@ -130,27 +148,13 @@
             a, k = 1 + (i - 4) // 3, (i - 4) % 3
             put(a, LO + depth + k, own, after)
             put(a, k, own, before)
-    for k in range(2 * depth):
-        e, o = y_even[k], y_odd[k]
-        pair = strip_pair(jnp.where(y_is_even, e, o), jnp.where(y_is_even, o, e))
-        for j in range(2):
-            a, p = divmod(2 * k + j, depth)
-            put(a, LO + p, ring, pair[j])
-    places = [(0, 0), (0, 1), (0, 2), (1, 0), (1, 1), (1, 2), (2, 0), (2, 1), (3, 0), (3, 1)]
-    for k in range(5):
-        ee, eo, oe, oo = c_ee[k], c_eo[k], c_oe[k], c_oo[k]
-        e_next, e_prev = jnp.where(y_is_even, ee, eo), jnp.where(y_is_even, eo, ee)
-        o_next, o_prev = jnp.where(y_is_even, oe, oo), jnp.where(y_is_even, oo, oe)
-        after = strip_pair(
-            jnp.where(z_is_even, e_next, o_next), jnp.where(z_is_even, e_prev, o_prev)
-        )
-        before = strip_pair(
-            jnp.where(z_is_even, o_next, e_next), jnp.where(z_is_even, o_prev, e_prev)
-        )
-        for j in range(2):
-            a, i = places[2 * k + j]
-            put(a, LO + depth + i, ring, after[j])
-            put(a, i + (1 if a >= 2 else 0), ring, before[j])
+    for a in range(4):
+        for p in range(depth):
+            put(a, LO + p, ring, rings[a * depth + p])
+    for n, (a, i) in enumerate(CORNERS):
+        e, o = c_even[n], c_odd[n]
+        put(a, LO + depth + i, ring, jnp.where(z_is_even, e, o))
+        put(a, LO - CORNER_WIDTHS[a] + i, ring, jnp.where(z_is_even, o, e))
     zero_tile = jnp.zeros((8, cols), jnp.int32)
     put(0, LO + depth + 3, ring, zero_tile)
     put(1, LO + depth + 2, ring, zero_tile)
@@ -289,7 +293,7 @@
             jax.ShapeDtypeStruct((3, LABELS, depth, rows, cols), f32),
             jax.ShapeDtypeStruct((8, 128), f32),
         ],
-        in_specs=[pl.BlockSpec(memory_space=VMEM)] * 12,
+        in_specs=[pl.BlockSpec(memory_space=VMEM)] * 9,
         out_specs=[pl.BlockSpec(memory_space=VMEM)] * 2,
         scratch_shapes=[
             VMEM((planes, wide, cols), jnp.int32),
@@ -387,7 +391,7 @@
     nz, ny = counts
     arrays = (tags, depth_affinity, row_affinity, column_affinity)
     axes = ("gz", "gy")
-    packed = pack(*arrays)
+    *own, z_even, z_odd, y_even, y_odd = pack(*arrays)
     ze, zo = (lambda z: even_partner(z, nz)), (lambda z: odd_partner(z, nz))
     ye, yo = (lambda y: even_partner(y, ny)), (lambda y: odd_partner(y, ny))
 
@@ -397,25 +401,22 @@
     def y_pair(py):
         return lambda z, y: (z, py(y)) if py(y) != y else (ze(z), y)
 
-    def corner(pz, py):
-        def pair(z, y):
-            if pz(z) != z and py(y) != y:
-                return pz(z), py(y)
-            return (pz(z), y) if pz(z) != z else (z, ye(y))
-        return pair
-
-    pairs = [z_pair(ze), z_pair(zo), y_pair(ye), y_pair(yo)]
-    pairs += [corner(a, b) for a in (ze, zo) for b in (ye, yo)]
-    halos = [exchanged(x, axes, counts, pair) for x, pair in zip(packed, pairs)]
-    fields, moments = krylov(counts, arrays, halos)
-
-    steps = [lambda z, y, d=d: (z, y ^ d) for d in powers(ny)]
-    steps += [lambda z, y, d=d: (z ^ d, y) for d in powers(nz)]
+    def swap(array, pair):
+        return exchanged(array, axes, counts, pair)
+
+    z_halos = [swap(z_even, z_pair(ze)), swap(z_odd, z_pair(zo))]
+    rings, c_even, c_odd = make_rings(swap(y_even, y_pair(ye)), swap(y_odd, y_pair(yo)))
+    corners = [swap(c_even, z_pair(ze)), swap(c_odd, z_pair(zo))]
+    fields, moments = krylov(counts, own, [*z_halos, rings, *corners])
+
+    steps = [lambda z, y: (z, y ^ 1)]
+    steps += [lambda z, y, d=d: (z, y ^ d ^ 1) for d in powers(ny)[1:]]
+    steps += [lambda z, y, d=d: (z ^ d, y ^ 1) for d in powers(nz)]
     for n, pair in enumerate(steps):
-        theirs = exchanged(moments, axes, counts, pair)
+        theirs = swap(moments, pair)
         if n < len(steps) - 1:
             moments = moments + theirs
-    return combined(moments, theirs, fields, tags)
+    return combined(moments, theirs, fields, own[0])
 
 
 def powers(count):

time: 56.1 us -> 42.7 us (0.76)
  starting transfers between devices: 23.1 us -> 12.4 us
  local copies, waits for them, and re-layouts: 7.41 us -> 3.71 us
  Pallas kernels: 10.1 us -> 11.1 us
    ppermute x12 -> x10, starting transfers between devices: 23.1 us -> 12.4 us  [exchanged(): return lax.ppermute(array, axes, route)]
    unnamed x16 -> x8, local copies, waits for them, and re-layouts: 7.41 us -> 3.71 us
    pallas_call x1 -> x2, Pallas kernels: 0.11 us -> 1.17 us  [the longest x1 1.1 us: pack(): pl.pallas_call(pack_kernel, out_shape=[jax.ShapeDtypeStruct((depth, rows,...]
    ppermute x12 -> x10, waiting for transfers between devices: 15.1 us -> 15.2 us  [exchanged(): return lax.ppermute(array, axes, route)]
  transfers between devices with their start and end apart: 12 -> 10, of which waited for: 8 -> 6; matrix products, arithmetic and copies ran while one was open for 0% -> 0% of each run, Pallas kernels for 0% -> 0%
where the time goes in v1:
time: 42.7 us; the launch traced here: 42.5 us
  waiting for transfers between devices  15.2 us (36%)
  starting transfers between devices  12.4 us (29%)
  Pallas kernels  11.1 us (26%)
  local copies, waits for them, and re-layouts  3.71 us (9%)
    ppermute x10, waiting for transfers between devices, exchanged(): return lax.ppermute(array, axes, route)  15.2 us
    ppermute x10, starting transfers between devices, exchanged(): return lax.ppermute(array, axes, route)  12.4 us
    pallas_call x1, Pallas kernels, krylov(): pl.pallas_call(functools.partial(krylov_kernel, counts), out_shape=[jax.S...  7.23 us
    unnamed x8, local copies, waits for them, and re-layouts  3.71 us
    pallas_call x1, Pallas kernels, combined(): pl.pallas_call(combine_kernel, out_shape=jax.ShapeDtypeStruct((LABELS,) +...  2.74 us
    pallas_call x1, Pallas kernels, pack(): pl.pallas_call(pack_kernel, out_shape=[jax.ShapeDtypeStruct((depth, rows,...  1.1 us
  transfers between devices with their start and end apart: 10, of which 6 were waited for; matrix products, arithmetic and copies ran while one was open for 0% of the time, Pallas kernels for 0%

profile of v1, /device:TPU:0, one launch (start us, length us, event | category | flops | bytes accessed | tf_op | source)
XLA Modules:
  0.0 42.5 jit_solution(5985781477488812772)
XLA Ops:
  0.0 0.9 %copy-done = s32[8,16,384]{2,1,0:T(8,128)S(1)} copy-done((s32[8,16,384]{2,1,0:T(8,128)S(1)}, s32[8,16,384]{2,1,0:T(8,128)}, u32[]{:S(2)}) %copy-start) | copy-done | bytes 196632
  0.9 0.9 %copy-done.1 = s32[8,16,384]{2,1,0:T(8,128)S(1)} copy-done((s32[8,16,384]{2,1,0:T(8,128)S(1)}, s32[8,16,384]{2,1,0:T(8,128)}, u32[]{:S(2)}) %copy-start.1) | copy-done | bytes 196632
  1.9 0.9 %copy-done.2 = s32[8,16,384]{2,1,0:T(8,128)S(1)} copy-done((s32[8,16,384]{2,1,0:T(8,128)S(1)}, s32[8,16,384]{2,1,0:T(8,128)}, u32[]{:S(2)}) %copy-start.2) | copy-done | bytes 196632
  2.8 0.9 %copy-done.3 = s32[8,16,384]{2,1,0:T(8,128)S(1)} copy-done((s32[8,16,384]{2,1,0:T(8,128)S(1)}, s32[8,16,384]{2,1,0:T(8,128)}, u32[]{:S(2)}) %copy-start.3) | copy-done | bytes 196632
  3.7 1.1 %shard_map.46 = (s32[8,16,384]{2,1,0:T(8,128)S(1)}, s32[8,16,384]{2,1,0:T(8,128)S(1)}, s32[8,16,384]{2,1,0:T(8,128)S(1)}, s32[8,16,384]{2,1,0:T(8,128)S(1)}, s32...) custom-call(s32[8,16,384]{2,1,0:T(8,128)S(1)} %copy-done, ...), custom_call_target="tpu_custom_call" | custom-call | tf_op jit(solution)/shard_map/pallas_call | solution.py:69
  4.8 0.5 %collective-permute-start.2 = (s32[16,8,384]{2,1,0:T(8,128)S(1)}, s32[16,8,384]{2,1,0:T(8,128)S(1)}, u32[]{:S(2)}, u32[]{:S(2)}) collective-permute-start(s32[16,8,384]{2,1,0:T(8,128)S(1)} %get-tuple-element.24), channel_id=1, source_target_pairs={{0,1},{1,0},{2,3},{3,2},{4,5},{5,4},{6,7},{7,6},{8,9},{9,8},{10,11... | collective-permute-start | bytes 589832 | tf_op jit(solution)/shard_map/ppermute | solution.py:35
  5.3 2.6 %collective-permute-start.3 = (s32[16,8,384]{2,1,0:T(8,128)S(1)}, s32[16,8,384]{2,1,0:T(8,128)S(1)}, u32[]{:S(2)}, u32[]{:S(2)}) collective-permute-start(s32[16,8,384]{2,1,0:T(8,128)S(1)} %get-tuple-element.25), channel_id=1, source_target_pairs={{0,4},{1,2},{2,1},{3,7},{4,0},{5,6},{6,5},{7,3},{8,12},{9,10},{10,... | collective-permute-start | bytes 589832 | tf_op jit(solution)/shard_map/ppermute | solution.py:35
  8.0 0.1 collective-permute-start
  8.1 1.2 %collective-permute-start.1 = (s32[13,16,384]{2,1,0:T(8,128)S(1)}, s32[13,16,384]{2,1,0:T(8,128)S(1)}, u32[]{:S(2)}, u32[]{:S(2)}) collective-permute-start(s32[13,16,384]{2,1,0:T(8,128)S(1)} %get-tuple-element.23), channel_id=1, source_target_pairs={{0,1},{1,0},{2,3},{3,2},{4,8},{5,9},{6,10},{7,11},{8,4},{9,5},{10,... | collective-permute-start | bytes 958472 | tf_op jit(solution)/shard_map/ppermute | solution.py:35
  9.3 0.0 collective-permute-done.2.y_even
  9.3 3.4 %collective-permute-done.3.y_odd = s32[16,8,384]{2,1,0:T(8,128)S(1)} collective-permute-done((s32[16,8,384]{2,1,0:T(8,128)S(1)}, s32[16,8,384]{2,1,0:T(8,128)S(1)}, u32[]{:S(2)}, u32[]{:S(2)}) %collective-permute-start.3) | collective-permute-done | bytes 196640 | tf_op jit(solution)/shard_map/ppermute | solution.py:35
  12.7 0.1 shard_map.47
  12.8 2.5 %collective-permute-start.4 = (s32[10,8,384]{2,1,0:T(8,128)S(1)}, s32[10,8,384]{2,1,0:T(8,128)S(1)}, u32[]{:S(2)}, u32[]{:S(2)}) collective-permute-start(s32[10,8,384]{2,1,0:T(8,128)S(1)} %get-tuple-element.27), channel_id=1, source_target_pairs={{0,4},{1,5},{2,6},{3,7},{4,0},{5,1},{6,2},{7,3},{8,12},{9,13},{10,... | collective-permute-start | bytes 368648 | tf_op jit(solution)/shard_map/ppermute | solution.py:35
  15.3 5.8 %collective-permute-done.4.c_even = s32[10,8,384]{2,1,0:T(8,128)S(1)} collective-permute-done((s32[10,8,384]{2,1,0:T(8,128)S(1)}, s32[10,8,384]{2,1,0:T(8,128)S(1)}, u32[]{:S(2)}, u32[]{:S(2)}) %collective-permute-start.4) | collective-permute-done | bytes 122912 | tf_op jit(solution)/shard_map/ppermute | solution.py:35
  21.1 7.2 %shard_map.48 = (f32[3,4,8,16,384]{4,3,2,1,0:T(8,128)S(1)}, f32[8,128]{1,0:T(8,128)S(1)}) custom-call(s32[8,16,384]{2,1,0:T(8,128)S(1)} %get-tuple-element.18.tags, s32[8,16,384]{2,1,0:T(8,128)S(1)} %get-tuple-element.19.wz, s32[8,16,384]{2,1,0:T(8,128)S(1)} %get-tuple-element.20.wy, s32[8,16,384]{2,1,0:T(8,128)S(1)} %get-tuple-element.21.wx, ...), custom_call_target="tpu_custom_call" | custom-call | tf_op jit(solution)/shard_map/pallas_call | solution.py:290
  28.4 0.1 collective-permute-start.6
  28.4 1.2 %collective-permute-done.6 = f32[8,128]{1,0:T(8,128)S(1)} collective-permute-done((f32[8,128]{1,0:T(8,128)S(1)}, f32[8,128]{1,0:T(8,128)S(1)}, u32[]{:S(2)}, u32[]{:S(2)}) %collective-permute-start.6) | collective-permute-done | bytes 4128 | tf_op jit(solution)/shard_map/ppermute | solution.py:35
  29.6 0.8 %collective-permute-start.7 = (f32[8,128]{1,0:T(8,128)S(1)}, f32[8,128]{1,0:T(8,128)S(1)}, u32[]{:S(2)}, u32[]{:S(2)}) collective-permute-start(f32[8,128]{1,0:T(8,128)S(1)} %add.9), channel_id=1, source_target_pairs={{0,3},{1,2},{2,1},{3,0},{4,7},{5,6},{6,5},{7,4},{8,11},{9,10},{10,... | collective-permute-start | bytes 12296 | tf_op jit(solution)/shard_map/ppermute | solution.py:35
  30.4 2.2 %collective-permute-done.7 = f32[8,128]{1,0:T(8,128)S(1)} collective-permute-done((f32[8,128]{1,0:T(8,128)S(1)}, f32[8,128]{1,0:T(8,128)S(1)}, u32[]{:S(2)}, u32[]{:S(2)}) %collective-permute-start.7) | collective-permute-done | bytes 4128 | tf_op jit(solution)/shard_map/ppermute | solution.py:35
  32.6 1.8 %collective-permute-start.8 = (f32[8,128]{1,0:T(8,128)S(1)}, f32[8,128]{1,0:T(8,128)S(1)}, u32[]{:S(2)}, u32[]{:S(2)}) collective-permute-start(f32[8,128]{1,0:T(8,128)S(1)} %add.10), channel_id=1, source_target_pairs={{0,5},{1,4},{2,7},{3,6},{4,1},{5,0},{6,3},{7,2},{8,13},{9,12},{10,... | collective-permute-start | bytes 12296 | tf_op jit(solution)/shard_map/ppermute | solution.py:35
  34.4 1.3 %collective-permute-done.8 = f32[8,128]{1,0:T(8,128)S(1)} collective-permute-done((f32[8,128]{1,0:T(8,128)S(1)}, f32[8,128]{1,0:T(8,128)S(1)}, u32[]{:S(2)}, u32[]{:S(2)}) %collective-permute-start.8) | collective-permute-done | bytes 4128 | tf_op jit(solution)/shard_map/ppermute | solution.py:35
  35.7 2.7 %collective-permute-start.9 = (f32[8,128]{1,0:T(8,128)S(1)}, f32[8,128]{1,0:T(8,128)S(1)}, u32[]{:S(2)}, u32[]{:S(2)}) collective-permute-start(f32[8,128]{1,0:T(8,128)S(1)} %add.11.mine), channel_id=1, source_target_pairs={{0,9},{1,8},{2,11},{3,10},{4,13},{5,12},{6,15},{7,14},{8,1},{9,0},... | collective-permute-start | bytes 12296 | tf_op jit(solution)/shard_map/ppermute | solution.py:35
  38.5 1.3 %collective-permute-done.9.theirs = f32[8,128]{1,0:T(8,128)S(1)} collective-permute-done((f32[8,128]{1,0:T(8,128)S(1)}, f32[8,128]{1,0:T(8,128)S(1)}, u32[]{:S(2)}, u32[]{:S(2)}) %collective-permute-start.9) | collective-permute-done | bytes 4128 | tf_op jit(solution)/shard_map/ppermute | solution.py:35
  39.8 2.7 %shard_map.49 = f32[4,8,16,384]{3,2,1,0:T(8,128)} custom-call(f32[8,128]{1,0:T(8,128)S(1)} %add.11.mine, f32[8,128]{1,0:T(8,128)S(1)} %collective-permute-done.9.theirs, f32[3,4,8,16,384]{4,3,2,1,0:T(8,128)S(1)} %get-tuple-element.30.fields, s32[8,16,384]{2,1,0:T(8,128)S(1)} %get-tuple-element.18.tags), custom_call_target="tpu_custom_call" | custom-call | tf_op jit(solution)/shard_map/pallas_call | solution.py:380
  (11 shorter events, 0.0 us)
Async XLA Ops:
  0.0 0.9 %copy-start = (s32[8,16,384]{2,1,0:T(8,128)S(1)}, s32[8,16,384]{2,1,0:T(8,128)}, u32[]{:S(2)}) copy-start(s32[8,16,384]{2,1,0:T(8,128)} %tags_hbm.1) | copy-start | bytes 589828
  0.9 0.9 %copy-start.1 = (s32[8,16,384]{2,1,0:T(8,128)S(1)}, s32[8,16,384]{2,1,0:T(8,128)}, u32[]{:S(2)}) copy-start(s32[8,16,384]{2,1,0:T(8,128)} %wz_hbm.1) | copy-start | bytes 589828
  1.9 0.9 %copy-start.2 = (s32[8,16,384]{2,1,0:T(8,128)S(1)}, s32[8,16,384]{2,1,0:T(8,128)}, u32[]{:S(2)}) copy-start(s32[8,16,384]{2,1,0:T(8,128)} %wy_hbm.1) | copy-start | bytes 589828
  2.8 0.9 %copy-start.3 = (s32[8,16,384]{2,1,0:T(8,128)S(1)}, s32[8,16,384]{2,1,0:T(8,128)}, u32[]{:S(2)}) copy-start(s32[8,16,384]{2,1,0:T(8,128)} %wx_hbm.1) | copy-start | bytes 589828
  4.8 4.5 %collective-permute-start.2 = (s32[16,8,384]{2,1,0:T(8,128)S(1)}, s32[16,8,384]{2,1,0:T(8,128)S(1)}, u32[]{:S(2)}, u32[]{:S(2)}) collective-permute-start(s32[16,8,384]{2,1,0:T(8,128)S(1)} %get-tuple-element.24), channel_id=1, source_target_pairs={{0,1},{1,0},{2,3},{3,2},{4,5},{5,4},{6,7},{7,6},{8,9},{9,8},{10,11... | collective-permute-start | bytes 589832 | tf_op jit(solution)/shard_map/ppermute | solution.py:35
  5.3 7.4 %collective-permute-start.3 = (s32[16,8,384]{2,1,0:T(8,128)S(1)}, s32[16,8,384]{2,1,0:T(8,128)S(1)}, u32[]{:S(2)}, u32[]{:S(2)}) collective-permute-start(s32[16,8,384]{2,1,0:T(8,128)S(1)} %get-tuple-element.25), channel_id=1, source_target_pairs={{0,4},{1,2},{2,1},{3,7},{4,0},{5,6},{6,5},{7,3},{8,12},{9,10},{10,... | collective-permute-start | bytes 589832 | tf_op jit(solution)/shard_map/ppermute | solution.py:35
  8.0 13.1 %collective-permute-start = (s32[13,16,384]{2,1,0:T(8,128)S(1)}, s32[13,16,384]{2,1,0:T(8,128)S(1)}, u32[]{:S(2)}, u32[]{:S(2)}) collective-permute-start(s32[13,16,384]{2,1,0:T(8,128)S(1)} %get-tuple-element.22), channel_id=1, source_target_pairs={{0,4},{1,5},{2,6},{3,7},{4,0},{5,1},{6,2},{7,3},{8,12},{9,13},{10,... | collective-permute-start | bytes 958472 | tf_op jit(solution)/shard_map/ppermute | solution.py:35
  8.1 13.1 %collective-permute-start.1 = (s32[13,16,384]{2,1,0:T(8,128)S(1)}, s32[13,16,384]{2,1,0:T(8,128)S(1)}, u32[]{:S(2)}, u32[]{:S(2)}) collective-permute-start(s32[13,16,384]{2,1,0:T(8,128)S(1)} %get-tuple-element.23), channel_id=1, source_target_pairs={{0,1},{1,0},{2,3},{3,2},{4,8},{5,9},{6,10},{7,11},{8,4},{9,5},{10,... | collective-permute-start | bytes 958472 | tf_op jit(solution)/shard_map/ppermute | solution.py:35
  12.8 8.4 %collective-permute-start.4 = (s32[10,8,384]{2,1,0:T(8,128)S(1)}, s32[10,8,384]{2,1,0:T(8,128)S(1)}, u32[]{:S(2)}, u32[]{:S(2)}) collective-permute-start(s32[10,8,384]{2,1,0:T(8,128)S(1)} %get-tuple-element.27), channel_id=1, source_target_pairs={{0,4},{1,5},{2,6},{3,7},{4,0},{5,1},{6,2},{7,3},{8,12},{9,13},{10,... | collective-permute-start | bytes 368648 | tf_op jit(solution)/shard_map/ppermute | solution.py:35
  15.3 5.8 %collective-permute-start.5 = (s32[10,8,384]{2,1,0:T(8,128)S(1)}, s32[10,8,384]{2,1,0:T(8,128)S(1)}, u32[]{:S(2)}, u32[]{:S(2)}) collective-permute-start(s32[10,8,384]{2,1,0:T(8,128)S(1)} %get-tuple-element.28), channel_id=1, source_target_pairs={{0,1},{1,0},{2,3},{3,2},{4,8},{5,9},{6,10},{7,11},{8,4},{9,5},{10,... | collective-permute-start | bytes 368648 | tf_op jit(solution)/shard_map/ppermute | solution.py:35
  28.4 1.2 %collective-permute-start.6 = (f32[8,128]{1,0:T(8,128)S(1)}, f32[8,128]{1,0:T(8,128)S(1)}, u32[]{:S(2)}, u32[]{:S(2)}) collective-permute-start(f32[8,128]{1,0:T(8,128)S(1)} %get-tuple-element.29), channel_id=1, source_target_pairs={{0,1},{1,0},{2,3},{3,2},{4,5},{5,4},{6,7},{7,6},{8,9},{9,8},{10,11... | collective-permute-start | bytes 12296 | tf_op jit(solution)/shard_map/ppermute | solution.py:35
  29.6 3.0 %collective-permute-start.7 = (f32[8,128]{1,0:T(8,128)S(1)}, f32[8,128]{1,0:T(8,128)S(1)}, u32[]{:S(2)}, u32[]{:S(2)}) collective-permute-start(f32[8,128]{1,0:T(8,128)S(1)} %add.9), channel_id=1, source_target_pairs={{0,3},{1,2},{2,1},{3,0},{4,7},{5,6},{6,5},{7,4},{8,11},{9,10},{10,... | collective-permute-start | bytes 12296 | tf_op jit(solution)/shard_map/ppermute | solution.py:35
  32.6 3.1 %collective-permute-start.8 = (f32[8,128]{1,0:T(8,128)S(1)}, f32[8,128]{1,0:T(8,128)S(1)}, u32[]{:S(2)}, u32[]{:S(2)}) collective-permute-start(f32[8,128]{1,0:T(8,128)S(1)} %add.10), channel_id=1, source_target_pairs={{0,5},{1,4},{2,7},{3,6},{4,1},{5,0},{6,3},{7,2},{8,13},{9,12},{10,... | collective-permute-start | bytes 12296 | tf_op jit(solution)/shard_map/ppermute | solution.py:35
  35.7 4.0 %collective-permute-start.9 = (f32[8,128]{1,0:T(8,128)S(1)}, f32[8,128]{1,0:T(8,128)S(1)}, u32[]{:S(2)}, u32[]{:S(2)}) collective-permute-start(f32[8,128]{1,0:T(8,128)S(1)} %add.11.mine), channel_id=1, source_target_pairs={{0,9},{1,8},{2,11},{3,10},{4,13},{5,12},{6,15},{7,14},{8,1},{9,0},... | collective-permute-start | bytes 12296 | tf_op jit(solution)/shard_map/ppermute | solution.py:35

commit v2 on v1

v2 whole, which is shorter than its diff:
```python
import functools

import jax
import jax.numpy as jnp
from jax import lax
from jax.experimental import pallas as pl
from jax.experimental.pallas import tpu as pltpu
from jax.sharding import PartitionSpec as P

LABELS = 4
PIVOT_FLOOR = 1e-7
LO, HI = 3, 4
Z_WIDTHS = (4, 3, 3, 3)
Z_PLANES = [(a, i) for a, width in enumerate(Z_WIDTHS) for i in range(width)]
CORNER_WIDTHS = (3, 3, 3, 2)
CORNERS = [(a, i) for a, width in enumerate(CORNER_WIDTHS) for i in range(width)]
PAIR = 4096.0
VMEM = pltpu.VMEM


def even_partner(i, count):
    return i ^ 1 if (i ^ 1) < count else i


def odd_partner(i, count):
    j = ((i + 1) ^ 1) - 1
    return j if 0 <= j < count else i


def exchanged(array, axes, counts, pair):
    parts, nz, ny = counts
    route = []
    for p in range(parts):
        for z in range(nz):
            for y in range(ny):
                q = (p,) + pair(z, y)
                if q == (p, z, y):
                    q = (even_partner(p, parts), z, y)
                source, target = ((a * nz + b) * ny + c for a, b, c in ((p, z, y), q))
                if source != target:
                    route.append((source, target))
    return lax.ppermute(array, axes, route)


def tile_pairs(sources, up, out):
    rows, cols = sources[0][0].shape[-2:]
    row = lax.broadcasted_iota(jnp.int32, (8, cols), 0)
    tile = pl.multiple_of(up * (rows - 8), 8)
    first = (row >= 4) == (up == 1)
    for k in range(0, len(sources), 2):
        (ra, *pa), (rb, *pb) = sources[k], sources[min(k + 1, len(sources) - 1)]
        a = ra[(*pa, pl.ds(tile, 8), slice(None))]
        b = rb[(*pb, pl.ds(tile, 8), slice(None))]
        out[k // 2] = jnp.where(first, a, pltpu.roll(b, 4, 0))


def pack_kernel(arrays, z_even, z_odd, y_odd, d_even, d_odd):
    z_is_odd, y_is_odd = lax.axis_index("gz") % 2, lax.axis_index("gy") % 2
    depth = arrays.shape[1]
    z_ups, y_ups = (1 - z_is_odd, z_is_odd), (1 - y_is_odd, y_is_odd)
    for up, out in zip(z_ups, (z_even, z_odd)):
        for n, (a, i) in enumerate(Z_PLANES):
            out[n] = arrays[a, up * (depth - Z_WIDTHS[a]) + i]
    planes = [(arrays, a, p) for a in range(4) for p in range(depth)]
    tile_pairs(planes, y_ups[1], y_odd)
    for up, out in zip(z_ups, (d_even, d_odd)):
        corners = [(arrays, a, up * (depth - CORNER_WIDTHS[a]) + i) for a, i in CORNERS]
        tile_pairs(corners, y_ups[1], out)


def pack(arrays):
    _, depth, rows, cols = arrays.shape
    sizes = [(len(Z_PLANES), rows)] * 2 + [(2 * depth, 8)] + [(len(CORNERS) // 2 + 1, 8)] * 2
    return pl.pallas_call(
        pack_kernel,
        out_shape=[jax.ShapeDtypeStruct((*size, cols), jnp.int32) for size in sizes],
        in_specs=[pl.BlockSpec(memory_space=VMEM)],
        out_specs=[pl.BlockSpec(memory_space=VMEM)] * 5,
        compiler_params=pltpu.CompilerParams(vmem_limit_bytes=16 * 2**20),
    )(arrays)


def relay_kernel(
    arrays, z_even, z_odd, y_odd, d_even, d_odd, before, after, ring, d_before, d_after, relay
):
    z_is_even = lax.axis_index("gz") % 2 == 0
    y_is_odd = lax.axis_index("gy") % 2
    for n in range(len(Z_PLANES)):
        e, o = z_even[n], z_odd[n]
        before[n] = jnp.where(z_is_even, o, e)
        after[n] = jnp.where(z_is_even, e, o)
    sources = [(arrays, a, p) for a in range(4) for p in range(arrays.shape[1])]
    for a, i in CORNERS:
        n = Z_PLANES.index((a, 0))
        sources += [(before, n + Z_WIDTHS[a] - CORNER_WIDTHS[a] + i), (after, n + i)]
    tile_pairs(sources, 1 - y_is_odd, relay)

    def unpack(out, n, pair):
        out[n] = pair
        if n + 1 < out.shape[0]:
            out[n + 1] = pltpu.roll(pair, 4, 0)

    for k in range(y_odd.shape[0]):
        unpack(ring, 2 * k, y_odd[k])
    for k in range(d_even.shape[0]):
        e, o = d_even[k], d_odd[k]
        unpack(d_before, 2 * k, jnp.where(z_is_even, o, e))
        unpack(d_after, 2 * k, jnp.where(z_is_even, e, o))


def relayed(arrays, z_even, z_odd, y_odd, d_even, d_odd):
    cols = z_even.shape[2]
    own = 2 * y_odd.shape[0]
    shapes = [z_even.shape] * 2 + [
        (n, 8, cols) for n in (own, len(CORNERS), len(CORNERS), own // 2 + len(CORNERS))
    ]
    return pl.pallas_call(
        relay_kernel,
        out_shape=[jax.ShapeDtypeStruct(shape, jnp.int32) for shape in shapes],
        in_specs=[pl.BlockSpec(memory_space=VMEM)] * 6,
        out_specs=[pl.BlockSpec(memory_space=VMEM)] * 6,
        compiler_params=pltpu.CompilerParams(vmem_limit_bytes=16 * 2**20),
    )(arrays, z_even, z_odd, y_odd, d_even, d_odd)


def krylov_kernel(
    counts, arrays, before, after, ring_odd, d_before, d_after, relay,
    fields, moments,
    m_pad, w_pad, coef, b_pad, v1, v2, sums,
):
    _, nz, ny = counts
    zi, yi = lax.axis_index("gz"), lax.axis_index("gy")
    _, depth, rows, cols = arrays.shape
    z_is_even, y_is_even = zi % 2 == 0, yi % 2 == 0
    wide = rows + 8
    f32 = jnp.float32
    ring_row = lax.broadcasted_iota(jnp.int32, (8, cols), 0)
    half = ring_row < 4
    own = slice(0, rows)
    ring = slice(rows, wide)

    def put(a, plane, where, values):
        if a == 0:
            m_pad[0, plane, where, :] = jnp.where(
                values == 0, 1.0, jnp.where(values == 1, PAIR, 0.0)
            )
            m_pad[1, plane, where, :] = jnp.where(
                values == 2, 1.0, jnp.where(values == 3, PAIR, 0.0)
            )
        else:
            w_pad[a - 1, plane, where, :] = values.astype(f32) + 1.0

    for a in range(4):
        for p in range(depth):
            put(a, LO + p, own, arrays[a, p])
    for n, (a, i) in enumerate(Z_PLANES):
        put(a, LO + depth + i, own, after[n])
        if LO - Z_WIDTHS[a] + i >= 0:
            put(a, LO - Z_WIDTHS[a] + i, own, before[n])

    from_even = half == y_is_even
    for k in range(2 * depth):
        pair = relay[k]
        for j, tile_even in enumerate((pair, pltpu.roll(pair, 4, 0))):
            a, p = divmod(2 * k + j, depth)
            put(a, LO + p, ring, jnp.where(from_even, tile_even, ring_odd[2 * k + j]))
    for n, (a, i) in enumerate(CORNERS):
        pair = relay[2 * depth + n]
        put(a, LO - CORNER_WIDTHS[a] + i, ring, jnp.where(from_even, pair, d_before[n]))
        put(a, LO + depth + i, ring, jnp.where(from_even, pltpu.roll(pair, 4, 0), d_after[n]))
    zero_tile = jnp.zeros((8, cols), jnp.int32)
    put(0, LO + depth + 3, ring, zero_tile)
    put(3, LO + depth + 2, ring, zero_tile)
    put(3, 0, ring, zero_tile)

    w_pad[0, LO + depth - 1] = jnp.where(zi == nz - 1, 0.0, w_pad[0, LO + depth - 1])
    w_pad[0, LO - 1] = jnp.where(zi == 0, 0.0, w_pad[0, LO - 1])
    at_end = (yi == ny - 1) & (ring_row == 7)
    at_start = (yi == 0) & (ring_row == 7)
    for p in range(LO + depth + 3):
        here = slice(rows - 8, rows)
        w_pad[1, p, here, :] = jnp.where(at_end, 0.0, w_pad[1, p, here, :])
        w_pad[1, p, ring, :] = jnp.where(at_start, 0.0, w_pad[1, p, ring, :])

    lanes = [slice(l, l + 128) for l in range(0, cols, 128)]
    lane = lax.broadcasted_iota(jnp.int32, (8, 128), 1)
    row = lax.broadcasted_iota(jnp.int32, (8, 128), 0)

    def tile(ref, index, r):
        return [ref[(*index, slice(r, r + 8), l)] for l in lanes]

    def store(ref, index, r, values):
        for l, x in zip(lanes, values):
            ref[(*index, slice(r, r + 8), l)] = x

    def next_x(v):
        turned = [pltpu.roll(x, 127, 1) for x in v]
        return [jnp.where(lane == 127, b, a) for a, b in zip(turned, turned[1:] + turned[:1])]

    def prev_x(v):
        turned = [pltpu.roll(x, 1, 1) for x in v]
        return [jnp.where(lane == 0, b, a) for a, b in zip(turned, turned[-1:] + turned[:-1])]

    def next_y(ref, index, r, v):
        other = tile(ref, index, (r + 8) % wide)
        return [pltpu.roll(jnp.where(row == 0, b, a), 7, 0) for a, b in zip(v, other)]

    def prev_y(ref, index, r, v):
        other = tile(ref, index, (r - 8) % wide)
        return [pltpu.roll(jnp.where(row == 7, b, a), 1, 0) for a, b in zip(v, other)]

    def near(weights, ref, c, p, r, v):
        neighbours = (
            tile(ref, (c, p + 1), r), tile(ref, (c, p - 1), r),
            next_y(ref, (c, p), r, v), prev_y(ref, (c, p), r, v),
            next_x(v), prev_x(v),
        )
        out = []
        for l in range(len(lanes)):
            t = [w[l] * n[l] for w, n in zip(weights, neighbours)]
            out.append((t[0] + t[1]) + (t[2] + t[3]) + (t[4] + t[5]))
        return out

    def prepare(p, _):
        for r in range(0, wide, 8):
            m = [tile(m_pad, (h, p), r) for h in range(2)]
            w_z, w_zb = tile(w_pad, (0, p), r), tile(w_pad, (0, p - 1), r)
            w_y, w_x = tile(w_pad, (1, p), r), tile(w_pad, (2, p), r)
            w_x = w_x[:-1] + [jnp.where(lane == 127, 0.0, w_x[-1])]
            w_yb, w_xb = prev_y(w_pad, (1, p), r, w_y), prev_x(w_x)
            weights = [[] for _ in range(7)]
            for l in range(len(lanes)):
                free = (m[0][l] + m[1][l]) == 0.0
                edges = [w[l] for w in (w_z, w_zb, w_y, w_yb, w_x, w_xb)]
                edges.append((edges[0] + edges[1]) + (edges[2] + edges[3]) + (edges[4] + edges[5]))
                for kept, w in zip(weights, edges):
                    kept.append(jnp.where(free, w, 0.0))
            for i, w in enumerate(weights):
                store(coef, (i, p), r, w)
            for h in range(2):
                both = near(weights, m_pad, h, p, r, m[h])
                second = [jnp.floor(x * (1.0 / PAIR)) for x in both]
                store(b_pad, (2 * h, p), r, [x - PAIR * y for x, y in zip(both, second)])
                store(b_pad, (2 * h + 1, p), r, second)
        return 0

    lax.fori_loop(1, LO + depth + 3, prepare, 0)

    def apply(source, target):
        def body(p, _):
            for r in range(0, wide, 8):
                weights = [tile(coef, (i, p), r) for i in range(7)]
                results = []
                for c in range(LABELS):
                    v = tile(source, (c, p), r)
                    n = near(weights[:6], source, c, p, r, v)
                    results.append([d * x - y for d, x, y in zip(weights[6], v, n)])
                for c in range(LABELS):
                    store(target, (c, p), r, results[c])
            return 0
        return body

    lax.fori_loop(2, LO + depth + 2, apply(b_pad, v1), 0)
    lax.fori_loop(3, LO + depth + 1, apply(v1, v2), 0)

    half_pairs = [(a, b) for a in range(LABELS) for b in range(a, LABELS)]
    all_pairs = [(a, b) for a in range(LABELS) for b in range(LABELS)]

    def total(products):
        while len(products) > 1:
            products = [x + y for x, y in zip(products[::2], products[1::2])] + (
                [products[-1]] if len(products) % 2 else []
            )
        return products[0]

    def accumulate(p, acc):
        parts = [[] for _ in acc]
        for r in range(0, rows, 8):
            bs = [tile(b_pad, (c, p), r) for c in range(LABELS)]
            abs_ = [tile(v1, (c, p), r) for c in range(LABELS)]
            for l in range(len(lanes)):
                b, ab = [x[l] for x in bs], [x[l] for x in abs_]
                products = [b[i] * b[j] for i, j in half_pairs]
                products += [b[i] * ab[j] for i, j in half_pairs]
                products += [ab[i] * ab[j] for i, j in half_pairs]
                for part, product in zip(parts, products):
                    part.append(product)
            for c in range(LABELS):
                store(fields, (0, c, p - LO), r, bs[c])
                store(fields, (1, c, p - LO), r, abs_[c])
        return tuple(x + total(part) for x, part in zip(acc, parts))

    def accumulate_last(p, acc):
        parts = [[] for _ in acc]
        for r in range(0, rows, 8):
            abs_ = [tile(v1, (c, p), r) for c in range(LABELS)]
            aabs = [tile(v2, (c, p), r) for c in range(LABELS)]
            w = [tile(coef, (i, p), r) for i in (0, 2, 4, 6)]
            qs = []
            for c in range(LABELS):
                v = aabs[c]
                z, y, x = tile(v2, (c, p + 1), r), next_y(v2, (c, p), r, v), next_x(v)
                qs.append([
                    w[3][l] * v[l] - 2.0 * (w[0][l] * z[l] + w[1][l] * y[l] + w[2][l] * x[l])
                    for l in range(len(lanes))
                ])
            for l in range(len(lanes)):
                ab, aab, q = [x[l] for x in abs_], [x[l] for x in aabs], [x[l] for x in qs]
                products = [ab[i] * aab[j] for i, j in half_pairs]
                products += [aab[i] * aab[j] for i, j in half_pairs]
                products += [aab[i] * q[j] for i, j in all_pairs]
                for part, product in zip(parts, products):
                    part.append(product)
            for c in range(LABELS):
                store(fields, (2, c, p - LO), r, aabs[c])
        return tuple(x + total(part) for x, part in zip(acc, parts))

    zero = jnp.zeros((8, 128), f32)
    low = lax.fori_loop(LO, LO + depth, accumulate, (zero,) * 30)
    high = lax.fori_loop(LO, LO + depth, accumulate_last, (zero,) * 36)
    kept = {}
    for k in range(5):
        part = low[10 * k : 10 * k + 10] if k < 3 else high[10 * (k - 3) : 10 * (k - 3) + 10]
        for (a, b), x in zip(half_pairs, part):
            kept[k, a, b] = kept[k, b, a] = x
    last = dict(zip(all_pairs, high[20:]))
    for a, b in half_pairs:
        kept[5, a, b] = kept[5, b, a] = 0.5 * (last[a, b] + last[b, a])
    for k in range(6):
        for a, b in half_pairs:
            x = jnp.sum(kept[k, a, b], axis=0, keepdims=True)
            for i, j in {(a, b), (b, a)}:
                at = (2 * k + j // 2) * 8 + (j % 2) * 4 + i
                sums[at : at + 1, :] = x
    packed = zero
    for g in range(12):
        x = jnp.sum(sums[8 * g : 8 * g + 8, :], axis=1, keepdims=True)
        packed = jnp.where(lane == g, x, packed)
    moments[...] = packed


def krylov(counts, arrays, halos):
    _, depth, rows, cols = arrays.shape
    planes, wide = depth + LO + HI, rows + 8
    f32 = jnp.float32
    return pl.pallas_call(
        functools.partial(krylov_kernel, counts),
        out_shape=[
            jax.ShapeDtypeStruct((3, LABELS, depth, rows, cols), f32),
            jax.ShapeDtypeStruct((8, 128), f32),
        ],
        in_specs=[pl.BlockSpec(memory_space=VMEM)] * 7,
        out_specs=[pl.BlockSpec(memory_space=VMEM)] * 2,
        scratch_shapes=[
            VMEM((2, planes, wide, cols), f32),
            VMEM((3, planes, wide, cols), f32),
            VMEM((7, planes, wide, cols), f32),
            VMEM((LABELS, planes, wide, cols), f32),
            VMEM((LABELS, planes, wide, cols), f32),
            VMEM((LABELS, planes, wide, cols), f32),
            VMEM((96, 128), f32),
        ],
        compiler_params=pltpu.CompilerParams(vmem_limit_bytes=48 * 2**20),
    )(arrays, *halos)


def combine_kernel(mine, theirs, fields, arrays, out, coeffs):
    f32 = jnp.float32
    _, depth, rows, cols = arrays.shape
    sums = mine[...] + theirs[...]
    lane = lax.broadcasted_iota(jnp.int32, (8, 128), 1)
    row = lax.broadcasted_iota(jnp.int32, (8, 128), 0)

    def splat(column):
        return jnp.broadcast_to(column, (8, 128))

    columns = {}
    for k in range(6):
        for h in range(2):
            x = splat(sums[:, 2 * k + h : 2 * k + h + 1])
            columns[k, 2 * h] = x
            columns[k, 2 * h + 1] = pltpu.roll(x, 4, 0)
    blocks = []
    for i in range(3):
        x = jnp.zeros((8, 128), f32)
        for j, k in enumerate((i + 1, i + 2, i + 3, i)):
            for b in range(LABELS):
                x = jnp.where(lane == 4 * j + b, columns[k, b], x)
        blocks.append(x)
    system = [
        jnp.where(row < 4, blocks[0], pltpu.roll(blocks[1], 4, 0)),
        jnp.where(row < 4, blocks[2], 0.0),
    ]
    start = list(system)
    for k in range(3 * LABELS):
        n, r = divmod(k, 8)
        pivot_row = system[n][r : r + 1, :]
        pivot = pivot_row[:, k : k + 1]
        sound = pivot > PIVOT_FLOOR * start[n][r : r + 1, k : k + 1]
        scale = jnp.where(sound, 1.0 / jnp.where(sound, pivot, 1.0), 0.0)
        pivot_row = pivot_row * scale
        for m in range(2):
            x = system[m] - system[m][:, k : k + 1] * pivot_row
            system[m] = jnp.where(row == r, pivot_row, x) if m == n else x
    for c in range(LABELS):
        for m in range(2):
            at = 3 * LABELS + c
            coeffs[c, 8 * m : 8 * m + 8, :] = splat(system[m][:, at : at + 1])

    for first in range(0, LABELS, 2):
        weights = {
            (c, k): jnp.broadcast_to(coeffs[c, k : k + 1, :], (8, 128))
            for c in (first, first + 1)
            for k in range(3 * LABELS)
        }

        def body(p, _):
            for r in range(0, rows, 8):
                for l in range(0, cols, 128):
                    cut = (p, slice(r, r + 8), slice(l, l + 128))
                    v = [fields[(k // LABELS, k % LABELS) + cut] for k in range(3 * LABELS)]
                    tag = arrays[(0,) + cut]
                    for c in (first, first + 1):
                        s = [v[k] * weights[c, k] for k in range(3 * LABELS)]
                        while len(s) > 1:
                            s = [x + y for x, y in zip(s[::2], s[1::2])] + (
                                [s[-1]] if len(s) % 2 else []
                            )
                        out[(c,) + cut] = jnp.where(tag == c, 1.0, s[0])
            return 0

        lax.fori_loop(0, depth, body, 0)


def combined(mine, theirs, fields, arrays):
    return pl.pallas_call(
        combine_kernel,
        out_shape=jax.ShapeDtypeStruct((LABELS,) + arrays.shape[1:], jnp.float32),
        in_specs=[pl.BlockSpec(memory_space=VMEM)] * 4,
        out_specs=pl.BlockSpec(memory_space=VMEM),
        scratch_shapes=[VMEM((LABELS, 16, 128), jnp.float32)],
        compiler_params=pltpu.CompilerParams(vmem_limit_bytes=32 * 2**20),
    )(mine, theirs, fields, arrays)


def per_device(counts, tags, depth_affinity, row_affinity, column_affinity):
    parts, nz, ny = counts
    arrays = jnp.stack([tags, depth_affinity, row_affinity, column_affinity])
    axes = ("parts", "gz", "gy")
    ze, zo = (lambda z: even_partner(z, nz)), (lambda z: odd_partner(z, nz))
    ye, yo = (lambda y: even_partner(y, ny)), (lambda y: odd_partner(y, ny))

    def swap(array, pz, py):
        def pair(z, y):
            if pz and pz(z) == z:
                return z, ye(y)
            if py and py(y) == y:
                return z, y
            return pz(z) if pz else z, py(y) if py else y
        return exchanged(array, axes, counts, pair)

    z_even, z_odd, y_odd, d_even, d_odd = pack(arrays)
    *sorted_halos, relay = relayed(
        arrays, swap(z_even, ze, None), swap(z_odd, zo, None), swap(y_odd, None, yo),
        swap(d_even, ze, yo), swap(d_odd, zo, yo),
    )
    halos = [*sorted_halos, swap(relay, None, ye)]
    fields, moments = krylov(counts, arrays, halos)

    steps = [lambda z, y: (z, y ^ 1)]
    steps += [lambda z, y, d=d: (z, y ^ d ^ 1) for d in powers(ny)[1:]]
    steps += [lambda z, y, d=d: (z ^ d, y ^ 1) for d in powers(nz)]
    for n, pair in enumerate(steps):
        theirs = exchanged(moments, axes, counts, pair)
        if n < len(steps) - 1:
            moments = moments + theirs
    return combined(moments, theirs, fields, arrays)


def powers(count):
    return [1 << n for n in range(count.bit_length() - 1)]


def solution(mesh):
    counts = tuple(mesh.shape[axis] for axis in ("parts", "gz", "gy"))
    placed = P(("parts", "gz"), "gy", None)
    return jax.shard_map(
        functools.partial(per_device, counts),
        mesh=mesh,
        in_specs=(placed,) * 4,
        out_specs=P(None, ("parts", "gz"), "gy", None),
        check_vma=False,
    )
```

time: 42.7 us -> 37.5 us (0.88)
  waiting for transfers between devices: 15.2 us -> 11.3 us
  local copies, waits for them, and re-layouts: 3.71 us -> 0 us
  starting transfers between devices: 12.4 us -> 14.9 us
  other arithmetic: 0.01 us -> 1.29 us
  Pallas kernels: 11.1 us -> 9.91 us
    ppermute x10, waiting for transfers between devices: 15.2 us -> 11.3 us  [exchanged(): return lax.ppermute(array, axes, route)]
    unnamed x8 -> x0, local copies, waits for them, and re-layouts: 3.71 us -> none
    ppermute x10, starting transfers between devices: 12.4 us -> 14.9 us  [exchanged(): return lax.ppermute(array, axes, route)]
    another operation x0 -> x1, other arithmetic: none -> 1.28 us  [per_device(): arrays = jnp.stack([tags, depth_affinity, row_affinity, column_affinity])]
    pallas_call x2, Pallas kernels: 1.17 us -> 0.23 us  [the longest x1 0.13 us: relayed(): pl.pallas_call(relay_kernel, out_shape=[jax.ShapeDtypeStruct(shape, jnp.i...]
  transfers between devices with their start and end apart: 10 -> 10, of which waited for: 6 -> 7; matrix products, arithmetic and copies ran while one was open for 0% -> 0% of each run, Pallas kernels for 0% -> 0%
where the time goes in v2:
time: 37.5 us; the launch traced here: 37.4 us
  starting transfers between devices  14.9 us (40%)
  waiting for transfers between devices  11.3 us (30%)
  Pallas kernels  9.91 us (26%)
  other arithmetic  1.29 us (3%)
    ppermute x10, starting transfers between devices, exchanged(): return lax.ppermute(array, axes, route)  14.9 us
    ppermute x10, waiting for transfers between devices, exchanged(): return lax.ppermute(array, axes, route)  11.3 us
    pallas_call x1, Pallas kernels, krylov(): pl.pallas_call(functools.partial(krylov_kernel, counts), out_shape=[jax.S...  6.93 us
    pallas_call x1, Pallas kernels, combined(): pl.pallas_call(combine_kernel, out_shape=jax.ShapeDtypeStruct((LABELS,) +...  2.75 us
    another operation x1, other arithmetic, per_device(): arrays = jnp.stack([tags, depth_affinity, row_affinity, column_affinity])  1.28 us
  transfers between devices with their start and end apart: 10, of which 7 were waited for; matrix products, arithmetic and copies ran while one was open for 0% of the time, Pallas kernels for 0%

profile of v2, /device:TPU:0, one launch (start us, length us, event | category | flops | bytes accessed | tf_op | source)
XLA Modules:
  0.0 37.4 jit_solution(15187456137035919952)
XLA Ops:
  0.0 1.3 %pad_add_fusion.arrays = s32[4,8,16,384]{3,2,1,0:T(8,128)S(1)} fusion(s32[1,8,16,384]{3,2,1,0:T(8,128)} %bitcast.4, s32[1,8,16,384]{3,2,1,0:T(8,128)} %bitcast.5, s32[1,8,16,384]{3,2,1,0:T(8,128)} %bitcast.6, s32[1,8,16,384]{3,2,1,0:T(8,128)} %bitcast.7), kind=kLoop, calls=%fused_computation | loop fusion | flops 589824 | bytes 1572864 | tf_op jit(solution)/shard_map/stack | solution.py:448
  1.3 0.1 shard_map.46
  1.4 3.1 %collective-permute-start = (s32[13,16,384]{2,1,0:T(8,128)S(1)}, s32[13,16,384]{2,1,0:T(8,128)S(1)}, u32[]{:S(2)}, u32[]{:S(2)}) collective-permute-start(s32[13,16,384]{2,1,0:T(8,128)S(1)} %get-tuple-element.18), channel_id=1, source_target_pairs={{0,4},{1,5},{2,6},{3,7},{4,0},{5,1},{6,2},{7,3},{8,12},{9,13},{10,... | collective-permute-start | bytes 958472 | tf_op jit(solution)/shard_map/ppermute | solution.py:42
  4.5 0.0 collective-permute-start.1
  4.5 1.5 %collective-permute-start.2 = (s32[16,8,384]{2,1,0:T(8,128)S(1)}, s32[16,8,384]{2,1,0:T(8,128)S(1)}, u32[]{:S(2)}, u32[]{:S(2)}) collective-permute-start(s32[16,8,384]{2,1,0:T(8,128)S(1)} %get-tuple-element.20), channel_id=1, source_target_pairs={{0,16},{1,2},{2,1},{3,19},{4,20},{5,6},{6,5},{7,23},{8,24},{9,10},... | collective-permute-start | bytes 589832 | tf_op jit(solution)/shard_map/ppermute | solution.py:42
  6.0 0.5 %collective-permute-start.3 = (s32[6,8,384]{2,1,0:T(8,128)S(1)}, s32[6,8,384]{2,1,0:T(8,128)S(1)}, u32[]{:S(2)}, u32[]{:S(2)}) collective-permute-start(s32[6,8,384]{2,1,0:T(8,128)S(1)} %get-tuple-element.21), channel_id=1, source_target_pairs={{0,16},{1,6},{2,5},{3,19},{4,20},{5,2},{6,1},{7,23},{8,24},{9,14},... | collective-permute-start | bytes 221192 | tf_op jit(solution)/shard_map/ppermute | solution.py:42
  6.5 2.2 %collective-permute-start.4 = (s32[6,8,384]{2,1,0:T(8,128)S(1)}, s32[6,8,384]{2,1,0:T(8,128)S(1)}, u32[]{:S(2)}, u32[]{:S(2)}) collective-permute-start(s32[6,8,384]{2,1,0:T(8,128)S(1)} %get-tuple-element.22), channel_id=1, source_target_pairs={{0,1},{1,0},{2,3},{3,2},{4,20},{5,10},{6,9},{7,23},{8,24},{9,6},{1... | collective-permute-start | bytes 221192 | tf_op jit(solution)/shard_map/ppermute | solution.py:42
  8.7 2.3 %collective-permute-done.3.d_even = s32[6,8,384]{2,1,0:T(8,128)S(1)} collective-permute-done((s32[6,8,384]{2,1,0:T(8,128)S(1)}, s32[6,8,384]{2,1,0:T(8,128)S(1)}, u32[]{:S(2)}, u32[]{:S(2)}) %collective-permute-start.3) | collective-permute-done | bytes 73760 | tf_op jit(solution)/shard_map/ppermute | solution.py:42
  10.9 0.0 collective-permute-done.4.d_odd
  10.9 1.9 %collective-permute-done.z_even = s32[13,16,384]{2,1,0:T(8,128)S(1)} collective-permute-done((s32[13,16,384]{2,1,0:T(8,128)S(1)}, s32[13,16,384]{2,1,0:T(8,128)S(1)}, u32[]{:S(2)}, u32[]{:S(2)}) %collective-permute-start) | collective-permute-done | bytes 319520 | tf_op jit(solution)/shard_map/ppermute | solution.py:42
  12.8 0.0 collective-permute-done.1.z_odd
  12.8 0.1 shard_map.47
  12.9 1.0 %collective-permute-start.5 = (s32[27,8,384]{2,1,0:T(8,128)S(1)}, s32[27,8,384]{2,1,0:T(8,128)S(1)}, u32[]{:S(2)}, u32[]{:S(2)}) collective-permute-start(s32[27,8,384]{2,1,0:T(8,128)S(1)} %get-tuple-element.28), channel_id=1, source_target_pairs={{0,1},{1,0},{2,3},{3,2},{4,5},{5,4},{6,7},{7,6},{8,9},{9,8},{10,11... | collective-permute-start | bytes 995336 | tf_op jit(solution)/shard_map/ppermute | solution.py:42
  13.9 1.3 %collective-permute-done.5.relay = s32[27,8,384]{2,1,0:T(8,128)S(1)} collective-permute-done((s32[27,8,384]{2,1,0:T(8,128)S(1)}, s32[27,8,384]{2,1,0:T(8,128)S(1)}, u32[]{:S(2)}, u32[]{:S(2)}) %collective-permute-start.5) | collective-permute-done | bytes 331808 | tf_op jit(solution)/shard_map/ppermute | solution.py:42
  15.2 6.9 %shard_map.48 = (f32[3,4,8,16,384]{4,3,2,1,0:T(8,128)S(1)}, f32[8,128]{1,0:T(8,128)S(1)}) custom-call(s32[4,8,16,384]{3,2,1,0:T(8,128)S(1)} %pad_add_fusion.arrays, s32[13,16,384]{2,1,0:T(8,128)S(1)} %get-tuple-element.23.before, s32[13,16,384]{2,1,0:T(8,128)S(1)} %get-tuple-element.24.after, s32[32,8,384]{2,1,0:T(8,128)S(1)} %get-tuple-element.25.ring_odd, ...), custom_call_target="tpu_custom_call" | custom-call | tf_op jit(solution)/shard_map/pallas_call | solution.py:346
  22.1 0.4 %collective-permute-start.6 = (f32[8,128]{1,0:T(8,128)S(1)}, f32[8,128]{1,0:T(8,128)S(1)}, u32[]{:S(2)}, u32[]{:S(2)}) collective-permute-start(f32[8,128]{1,0:T(8,128)S(1)} %get-tuple-element.29), channel_id=1, source_target_pairs={{0,1},{1,0},{2,3},{3,2},{4,5},{5,4},{6,7},{7,6},{8,9},{9,8},{10,11... | collective-permute-start | bytes 12296 | tf_op jit(solution)/shard_map/ppermute | solution.py:42
  22.6 0.8 %collective-permute-done.6 = f32[8,128]{1,0:T(8,128)S(1)} collective-permute-done((f32[8,128]{1,0:T(8,128)S(1)}, f32[8,128]{1,0:T(8,128)S(1)}, u32[]{:S(2)}, u32[]{:S(2)}) %collective-permute-start.6) | collective-permute-done | bytes 4128 | tf_op jit(solution)/shard_map/ppermute | solution.py:42
  23.4 0.6 %collective-permute-start.7 = (f32[8,128]{1,0:T(8,128)S(1)}, f32[8,128]{1,0:T(8,128)S(1)}, u32[]{:S(2)}, u32[]{:S(2)}) collective-permute-start(f32[8,128]{1,0:T(8,128)S(1)} %add.9), channel_id=1, source_target_pairs={{0,3},{1,2},{2,1},{3,0},{4,7},{5,6},{6,5},{7,4},{8,11},{9,10},{10,... | collective-permute-start | bytes 12296 | tf_op jit(solution)/shard_map/ppermute | solution.py:42
  24.0 2.4 %collective-permute-done.7 = f32[8,128]{1,0:T(8,128)S(1)} collective-permute-done((f32[8,128]{1,0:T(8,128)S(1)}, f32[8,128]{1,0:T(8,128)S(1)}, u32[]{:S(2)}, u32[]{:S(2)}) %collective-permute-start.7) | collective-permute-done | bytes 4128 | tf_op jit(solution)/shard_map/ppermute | solution.py:42
  26.4 2.6 %collective-permute-start.8 = (f32[8,128]{1,0:T(8,128)S(1)}, f32[8,128]{1,0:T(8,128)S(1)}, u32[]{:S(2)}, u32[]{:S(2)}) collective-permute-start(f32[8,128]{1,0:T(8,128)S(1)} %add.10), channel_id=1, source_target_pairs={{0,5},{1,4},{2,7},{3,6},{4,1},{5,0},{6,3},{7,2},{8,13},{9,12},{10,... | collective-permute-start | bytes 12296 | tf_op jit(solution)/shard_map/ppermute | solution.py:42
  29.1 1.3 %collective-permute-done.8 = f32[8,128]{1,0:T(8,128)S(1)} collective-permute-done((f32[8,128]{1,0:T(8,128)S(1)}, f32[8,128]{1,0:T(8,128)S(1)}, u32[]{:S(2)}, u32[]{:S(2)}) %collective-permute-start.8) | collective-permute-done | bytes 4128 | tf_op jit(solution)/shard_map/ppermute | solution.py:42
  30.4 2.9 %collective-permute-start.9 = (f32[8,128]{1,0:T(8,128)S(1)}, f32[8,128]{1,0:T(8,128)S(1)}, u32[]{:S(2)}, u32[]{:S(2)}) collective-permute-start(f32[8,128]{1,0:T(8,128)S(1)} %add.11.mine), channel_id=1, source_target_pairs={{0,9},{1,8},{2,11},{3,10},{4,13},{5,12},{6,15},{7,14},{8,1},{9,0},... | collective-permute-start | bytes 12296 | tf_op jit(solution)/shard_map/ppermute | solution.py:42
  33.3 1.3 %collective-permute-done.9.theirs = f32[8,128]{1,0:T(8,128)S(1)} collective-permute-done((f32[8,128]{1,0:T(8,128)S(1)}, f32[8,128]{1,0:T(8,128)S(1)}, u32[]{:S(2)}, u32[]{:S(2)}) %collective-permute-start.9) | collective-permute-done | bytes 4128 | tf_op jit(solution)/shard_map/ppermute | solution.py:42
  34.6 2.8 %shard_map.49 = f32[4,8,16,384]{3,2,1,0:T(8,128)} custom-call(f32[8,128]{1,0:T(8,128)S(1)} %add.11.mine, f32[8,128]{1,0:T(8,128)S(1)} %collective-permute-done.9.theirs, f32[3,4,8,16,384]{4,3,2,1,0:T(8,128)S(1)} %get-tuple-element.30.fields, s32[4,8,16,384]{3,2,1,0:T(8,128)S(1)} %pad_add_fusion.arrays), custom_call_target="tpu_custom_call" | custom-call | tf_op jit(solution)/shard_map/pallas_call | solution.py:436
  (4 shorter events, 0.0 us)
Async XLA Ops:
  1.4 11.4 %collective-permute-start = (s32[13,16,384]{2,1,0:T(8,128)S(1)}, s32[13,16,384]{2,1,0:T(8,128)S(1)}, u32[]{:S(2)}, u32[]{:S(2)}) collective-permute-start(s32[13,16,384]{2,1,0:T(8,128)S(1)} %get-tuple-element.18), channel_id=1, source_target_pairs={{0,4},{1,5},{2,6},{3,7},{4,0},{5,1},{6,2},{7,3},{8,12},{9,13},{10,... | collective-permute-start | bytes 958472 | tf_op jit(solution)/shard_map/ppermute | solution.py:42
  4.5 8.3 %collective-permute-start.1 = (s32[13,16,384]{2,1,0:T(8,128)S(1)}, s32[13,16,384]{2,1,0:T(8,128)S(1)}, u32[]{:S(2)}, u32[]{:S(2)}) collective-permute-start(s32[13,16,384]{2,1,0:T(8,128)S(1)} %get-tuple-element.19), channel_id=1, source_target_pairs={{0,1},{1,0},{2,3},{3,2},{4,8},{5,9},{6,10},{7,11},{8,4},{9,5},{10,... | collective-permute-start | bytes 958472 | tf_op jit(solution)/shard_map/ppermute | solution.py:42
  4.5 6.5 %collective-permute-start.2 = (s32[16,8,384]{2,1,0:T(8,128)S(1)}, s32[16,8,384]{2,1,0:T(8,128)S(1)}, u32[]{:S(2)}, u32[]{:S(2)}) collective-permute-start(s32[16,8,384]{2,1,0:T(8,128)S(1)} %get-tuple-element.20), channel_id=1, source_target_pairs={{0,16},{1,2},{2,1},{3,19},{4,20},{5,6},{6,5},{7,23},{8,24},{9,10},... | collective-permute-start | bytes 589832 | tf_op jit(solution)/shard_map/ppermute | solution.py:42
  6.0 4.9 %collective-permute-start.3 = (s32[6,8,384]{2,1,0:T(8,128)S(1)}, s32[6,8,384]{2,1,0:T(8,128)S(1)}, u32[]{:S(2)}, u32[]{:S(2)}) collective-permute-start(s32[6,8,384]{2,1,0:T(8,128)S(1)} %get-tuple-element.21), channel_id=1, source_target_pairs={{0,16},{1,6},{2,5},{3,19},{4,20},{5,2},{6,1},{7,23},{8,24},{9,14},... | collective-permute-start | bytes 221192 | tf_op jit(solution)/shard_map/ppermute | solution.py:42
  6.5 4.4 %collective-permute-start.4 = (s32[6,8,384]{2,1,0:T(8,128)S(1)}, s32[6,8,384]{2,1,0:T(8,128)S(1)}, u32[]{:S(2)}, u32[]{:S(2)}) collective-permute-start(s32[6,8,384]{2,1,0:T(8,128)S(1)} %get-tuple-element.22), channel_id=1, source_target_pairs={{0,1},{1,0},{2,3},{3,2},{4,20},{5,10},{6,9},{7,23},{8,24},{9,6},{1... | collective-permute-start | bytes 221192 | tf_op jit(solution)/shard_map/ppermute | solution.py:42
  12.9 2.3 %collective-permute-start.5 = (s32[27,8,384]{2,1,0:T(8,128)S(1)}, s32[27,8,384]{2,1,0:T(8,128)S(1)}, u32[]{:S(2)}, u32[]{:S(2)}) collective-permute-start(s32[27,8,384]{2,1,0:T(8,128)S(1)} %get-tuple-element.28), channel_id=1, source_target_pairs={{0,1},{1,0},{2,3},{3,2},{4,5},{5,4},{6,7},{7,6},{8,9},{9,8},{10,11... | collective-permute-start | bytes 995336 | tf_op jit(solution)/shard_map/ppermute | solution.py:42
  22.1 1.2 %collective-permute-start.6 = (f32[8,128]{1,0:T(8,128)S(1)}, f32[8,128]{1,0:T(8,128)S(1)}, u32[]{:S(2)}, u32[]{:S(2)}) collective-permute-start(f32[8,128]{1,0:T(8,128)S(1)} %get-tuple-element.29), channel_id=1, source_target_pairs={{0,1},{1,0},{2,3},{3,2},{4,5},{5,4},{6,7},{7,6},{8,9},{9,8},{10,11... | collective-permute-start | bytes 12296 | tf_op jit(solution)/shard_map/ppermute | solution.py:42
  23.4 3.0 %collective-permute-start.7 = (f32[8,128]{1,0:T(8,128)S(1)}, f32[8,128]{1,0:T(8,128)S(1)}, u32[]{:S(2)}, u32[]{:S(2)}) collective-permute-start(f32[8,128]{1,0:T(8,128)S(1)} %add.9), channel_id=1, source_target_pairs={{0,3},{1,2},{2,1},{3,0},{4,7},{5,6},{6,5},{7,4},{8,11},{9,10},{10,... | collective-permute-start | bytes 12296 | tf_op jit(solution)/shard_map/ppermute | solution.py:42
  26.4 4.0 %collective-permute-start.8 = (f32[8,128]{1,0:T(8,128)S(1)}, f32[8,128]{1,0:T(8,128)S(1)}, u32[]{:S(2)}, u32[]{:S(2)}) collective-permute-start(f32[8,128]{1,0:T(8,128)S(1)} %add.10), channel_id=1, source_target_pairs={{0,5},{1,4},{2,7},{3,6},{4,1},{5,0},{6,3},{7,2},{8,13},{9,12},{10,... | collective-permute-start | bytes 12296 | tf_op jit(solution)/shard_map/ppermute | solution.py:42
  30.4 4.2 %collective-permute-start.9 = (f32[8,128]{1,0:T(8,128)S(1)}, f32[8,128]{1,0:T(8,128)S(1)}, u32[]{:S(2)}, u32[]{:S(2)}) collective-permute-start(f32[8,128]{1,0:T(8,128)S(1)} %add.11.mine), channel_id=1, source_target_pairs={{0,9},{1,8},{2,11},{3,10},{4,13},{5,12},{6,15},{7,14},{8,1},{9,0},... | collective-permute-start | bytes 12296 | tf_op jit(solution)/shard_map/ppermute | solution.py:42

commit v3 on v2

--- a/solution.py
+++ b/solution.py
@@ -15,6 +15,7 @@
 CORNER_WIDTHS = (3, 3, 3, 2)
 CORNERS = [(a, i) for a, width in enumerate(CORNER_WIDTHS) for i in range(width)]
 PAIR = 4096.0
+GROUP = 4
 VMEM = pltpu.VMEM
 
 
@@ -54,7 +55,19 @@
         out[k // 2] = jnp.where(first, a, pltpu.roll(b, 4, 0))
 
 
-def pack_kernel(arrays, z_even, z_odd, y_odd, d_even, d_odd):
+def interleave(cols, back=False):
+    tiles = cols // 128
+    i, j = (lax.broadcasted_iota(jnp.int32, (cols, cols), n) for n in ((1, 0) if back else (0, 1)))
+    return (i == tiles * (j % 128) + j // 128).astype(jnp.float32).astype(jnp.bfloat16)
+
+
+def pack_kernel(natural, arrays, z_even, z_odd, y_odd, d_even, d_odd):
+    cols = natural.shape[-1]
+    flat = natural[...].reshape(-1, cols).astype(jnp.float32).astype(jnp.bfloat16)
+    turned = jnp.dot(flat, interleave(cols), preferred_element_type=jnp.float32)
+    turned = turned.reshape(arrays.shape)
+    arrays[0] = turned[0]
+    arrays[1:] = turned[1:] + 1.0
     z_is_odd, y_is_odd = lax.axis_index("gz") % 2, lax.axis_index("gy") % 2
     depth = arrays.shape[1]
     z_ups, y_ups = (1 - z_is_odd, z_is_odd), (1 - y_is_odd, y_is_odd)
@@ -73,9 +86,10 @@
     sizes = [(len(Z_PLANES), rows)] * 2 + [(2 * depth, 8)] + [(len(CORNERS) // 2 + 1, 8)] * 2
     return pl.pallas_call(
         pack_kernel,
-        out_shape=[jax.ShapeDtypeStruct((*size, cols), jnp.int32) for size in sizes],
+        out_shape=[jax.ShapeDtypeStruct(arrays.shape, jnp.float32)]
+        + [jax.ShapeDtypeStruct((*size, cols), jnp.float32) for size in sizes],
         in_specs=[pl.BlockSpec(memory_space=VMEM)],
-        out_specs=[pl.BlockSpec(memory_space=VMEM)] * 5,
+        out_specs=[pl.BlockSpec(memory_space=VMEM)] * 6,
         compiler_params=pltpu.CompilerParams(vmem_limit_bytes=16 * 2**20),
     )(arrays)
 
@@ -116,7 +130,7 @@
     ]
     return pl.pallas_call(
         relay_kernel,
-        out_shape=[jax.ShapeDtypeStruct(shape, jnp.int32) for shape in shapes],
+        out_shape=[jax.ShapeDtypeStruct(shape, jnp.float32) for shape in shapes],
         in_specs=[pl.BlockSpec(memory_space=VMEM)] * 6,
         out_specs=[pl.BlockSpec(memory_space=VMEM)] * 6,
         compiler_params=pltpu.CompilerParams(vmem_limit_bytes=16 * 2**20),
@@ -126,7 +140,7 @@
 def krylov_kernel(
     counts, arrays, before, after, ring_odd, d_before, d_after, relay,
     fields, moments,
-    m_pad, w_pad, coef, b_pad, v1, v2, sums,
+    m_pad, w_pad, free, b_pad, v1, v2, acc, sums,
 ):
     _, nz, ny = counts
     zi, yi = lax.axis_index("gz"), lax.axis_index("gy")
@@ -148,7 +162,7 @@
                 values == 2, 1.0, jnp.where(values == 3, PAIR, 0.0)
             )
         else:
-            w_pad[a - 1, plane, where, :] = values.astype(f32) + 1.0
+            w_pad[a - 1, plane, where, :] = values
 
     for a in range(4):
         for p in range(depth):
@@ -168,100 +182,127 @@
         pair = relay[2 * depth + n]
         put(a, LO - CORNER_WIDTHS[a] + i, ring, jnp.where(from_even, pair, d_before[n]))
         put(a, LO + depth + i, ring, jnp.where(from_even, pltpu.roll(pair, 4, 0), d_after[n]))
-    zero_tile = jnp.zeros((8, cols), jnp.int32)
+    zero_tile = jnp.zeros((8, cols), f32)
     put(0, LO + depth + 3, ring, zero_tile)
     put(3, LO + depth + 2, ring, zero_tile)
     put(3, 0, ring, zero_tile)
 
     w_pad[0, LO + depth - 1] = jnp.where(zi == nz - 1, 0.0, w_pad[0, LO + depth - 1])
     w_pad[0, LO - 1] = jnp.where(zi == 0, 0.0, w_pad[0, LO - 1])
+    x_end = slice(cols - 128, cols)
+    last_x = lax.broadcasted_iota(jnp.int32, (wide, 128), 1) == 127
     at_end = (yi == ny - 1) & (ring_row == 7)
     at_start = (yi == 0) & (ring_row == 7)
     for p in range(LO + depth + 3):
         here = slice(rows - 8, rows)
         w_pad[1, p, here, :] = jnp.where(at_end, 0.0, w_pad[1, p, here, :])
         w_pad[1, p, ring, :] = jnp.where(at_start, 0.0, w_pad[1, p, ring, :])
+        w_pad[2, p, :, x_end] = jnp.where(last_x, 0.0, w_pad[2, p, :, x_end])
 
     lanes = [slice(l, l + 128) for l in range(0, cols, 128)]
     lane = lax.broadcasted_iota(jnp.int32, (8, 128), 1)
     row = lax.broadcasted_iota(jnp.int32, (8, 128), 0)
 
+    row_tiles = range(0, wide, 8)
+
     def tile(ref, index, r):
         return [ref[(*index, slice(r, r + 8), l)] for l in lanes]
+
+    def plane(ref, *index):
+        return [tile(ref, index, r) for r in row_tiles]
 
     def store(ref, index, r, values):
         for l, x in zip(lanes, values):
             ref[(*index, slice(r, r + 8), l)] = x
 
+    def store_plane(ref, index, values):
+        for r, x in zip(row_tiles, values):
+            store(ref, index, r, x)
+
+    def each(f, *planes):
+        return [[f(*x) for x in zip(*rows_)] for rows_ in zip(*planes)]
+
     def next_x(v):
-        turned = [pltpu.roll(x, 127, 1) for x in v]
-        return [jnp.where(lane == 127, b, a) for a, b in zip(turned, turned[1:] + turned[:1])]
+        return [x[1:] + [pltpu.roll(x[0], 127, 1)] for x in v]
 
     def prev_x(v):
-        turned = [pltpu.roll(x, 1, 1) for x in v]
-        return [jnp.where(lane == 0, b, a) for a, b in zip(turned, turned[-1:] + turned[:-1])]
-
-    def next_y(ref, index, r, v):
-        other = tile(ref, index, (r + 8) % wide)
-        return [pltpu.roll(jnp.where(row == 0, b, a), 7, 0) for a, b in zip(v, other)]
-
-    def prev_y(ref, index, r, v):
-        other = tile(ref, index, (r - 8) % wide)
-        return [pltpu.roll(jnp.where(row == 7, b, a), 1, 0) for a, b in zip(v, other)]
-
-    def near(weights, ref, c, p, r, v):
-        neighbours = (
-            tile(ref, (c, p + 1), r), tile(ref, (c, p - 1), r),
-            next_y(ref, (c, p), r, v), prev_y(ref, (c, p), r, v),
-            next_x(v), prev_x(v),
-        )
-        out = []
-        for l in range(len(lanes)):
-            t = [w[l] * n[l] for w, n in zip(weights, neighbours)]
-            out.append((t[0] + t[1]) + (t[2] + t[3]) + (t[4] + t[5]))
-        return out
-
-    def prepare(p, _):
-        for r in range(0, wide, 8):
-            m = [tile(m_pad, (h, p), r) for h in range(2)]
-            w_z, w_zb = tile(w_pad, (0, p), r), tile(w_pad, (0, p - 1), r)
-            w_y, w_x = tile(w_pad, (1, p), r), tile(w_pad, (2, p), r)
-            w_x = w_x[:-1] + [jnp.where(lane == 127, 0.0, w_x[-1])]
-            w_yb, w_xb = prev_y(w_pad, (1, p), r, w_y), prev_x(w_x)
-            weights = [[] for _ in range(7)]
-            for l in range(len(lanes)):
-                free = (m[0][l] + m[1][l]) == 0.0
-                edges = [w[l] for w in (w_z, w_zb, w_y, w_yb, w_x, w_xb)]
-                edges.append((edges[0] + edges[1]) + (edges[2] + edges[3]) + (edges[4] + edges[5]))
-                for kept, w in zip(weights, edges):
-                    kept.append(jnp.where(free, w, 0.0))
-            for i, w in enumerate(weights):
-                store(coef, (i, p), r, w)
-            for h in range(2):
-                both = near(weights, m_pad, h, p, r, m[h])
-                second = [jnp.floor(x * (1.0 / PAIR)) for x in both]
-                store(b_pad, (2 * h, p), r, [x - PAIR * y for x, y in zip(both, second)])
-                store(b_pad, (2 * h + 1, p), r, second)
-        return 0
-
-    lax.fori_loop(1, LO + depth + 3, prepare, 0)
+        return [[pltpu.roll(x[-1], 1, 1)] + x[:-1] for x in v]
+
+    def next_y(v):
+        pair = lambda a, b: pltpu.roll(jnp.where(row == 0, b, a), 7, 0)
+        return each(pair, v, v[1:] + v[:1])
+
+    def prev_y(v):
+        pair = lambda a, b: pltpu.roll(jnp.where(row == 7, b, a), 1, 0)
+        return each(pair, v, v[-1:] + v[:-1])
+
+    def times(x, y):
+        return each(lambda a, b: a * b, x, y)
+
+    def in_groups(first, end, body):
+        steps, rest = divmod(end - first, GROUP)
+
+        def step(i, _):
+            body(first + GROUP * i, GROUP)
+            return 0
+
+        lax.fori_loop(0, steps, step, 0)
+        if rest:
+            body(end - rest, rest)
+
+    def prepare(start, count):
+        for h in range(2):
+            m = [plane(m_pad, h, start + j) for j in (-1, 0)]
+            from_behind = times(plane(w_pad, 0, start - 1), m[0])
+            here = m[1]
+            for j in range(count):
+                p = start + j
+                ahead = plane(m_pad, h, p + 1)
+                w_z, w_y, w_x = (plane(w_pad, i, p) for i in range(3))
+                sums_ = each(
+                    lambda a, b, c, d, e, f: (a + b) + (c + d) + (e + f),
+                    times(w_z, ahead), from_behind,
+                    times(w_y, next_y(here)), prev_y(times(w_y, here)),
+                    times(w_x, next_x(here)), prev_x(times(w_x, here)),
+                )
+                if h == 0:
+                    other = plane(m_pad, 1, p)
+                    u = each(lambda a, b: jnp.where(a + b == 0.0, 1.0, 0.0), here, other)
+                    store_plane(free, (p,), u)
+                else:
+                    u = plane(free, p)
+                sums_ = times(sums_, u)
+                second = each(lambda x: jnp.floor(x * (1.0 / PAIR)), sums_)
+                store_plane(b_pad, (2 * h, p), each(lambda x, y: x - PAIR * y, sums_, second))
+                store_plane(b_pad, (2 * h + 1, p), second)
+                from_behind = times(w_z, here)
+                here = ahead
+
+    in_groups(1, LO + depth + 3, prepare)
+
+    def flow(w, x, y):
+        return each(lambda a, b, c: a * (b - c), w, x, y)
 
     def apply(source, target):
-        def body(p, _):
-            for r in range(0, wide, 8):
-                weights = [tile(coef, (i, p), r) for i in range(7)]
-                results = []
-                for c in range(LABELS):
-                    v = tile(source, (c, p), r)
-                    n = near(weights[:6], source, c, p, r, v)
-                    results.append([d * x - y for d, x, y in zip(weights[6], v, n)])
-                for c in range(LABELS):
-                    store(target, (c, p), r, results[c])
-            return 0
+        def body(start, count):
+            for c in range(LABELS):
+                here = plane(source, c, start)
+                from_behind = flow(plane(w_pad, 0, start - 1), here, plane(source, c, start - 1))
+                for j in range(count):
+                    p = start + j
+                    ahead = plane(source, c, p + 1)
+                    f_z = flow(plane(w_pad, 0, p), ahead, here)
+                    f_y = flow(plane(w_pad, 1, p), next_y(here), here)
+                    f_x = flow(plane(w_pad, 2, p), next_x(here), here)
+                    store_plane(target, (c, p), each(
+                        lambda u, a, b, c, d, e, f: u * ((a - b) + (c - d) + (e - f)),
+                        plane(free, p), from_behind, f_z, prev_y(f_y), f_y, prev_x(f_x), f_x,
+                    ))
+                    from_behind, here = f_z, ahead
         return body
 
-    lax.fori_loop(2, LO + depth + 2, apply(b_pad, v1), 0)
-    lax.fori_loop(3, LO + depth + 1, apply(v1, v2), 0)
+    in_groups(2, LO + depth + 2, apply(b_pad, v1))
+    in_groups(3, LO + depth + 1, apply(v1, v2))
 
     half_pairs = [(a, b) for a in range(LABELS) for b in range(a, LABELS)]
     all_pairs = [(a, b) for a in range(LABELS) for b in range(LABELS)]
@@ -273,9 +314,15 @@
             )
         return products[0]
 
-    def accumulate(p, acc):
-        parts = [[] for _ in acc]
-        for r in range(0, rows, 8):
+    def add_up(first, parts):
+        for n, part in enumerate(parts):
+            acc[first + n] = acc[first + n] + total(part)
+
+    own_tiles = range(0, rows, 8)
+
+    def accumulate(p, _):
+        parts = [[] for _ in range(30)]
+        for r in own_tiles:
             bs = [tile(b_pad, (c, p), r) for c in range(LABELS)]
             abs_ = [tile(v1, (c, p), r) for c in range(LABELS)]
             for l in range(len(lanes)):
@@ -288,36 +335,45 @@
             for c in range(LABELS):
                 store(fields, (0, c, p - LO), r, bs[c])
                 store(fields, (1, c, p - LO), r, abs_[c])
-        return tuple(x + total(part) for x, part in zip(acc, parts))
-
-    def accumulate_last(p, acc):
-        parts = [[] for _ in acc]
-        for r in range(0, rows, 8):
+        add_up(0, parts)
+        return 0
+
+    def accumulate_last(p, _):
+        parts = [[] for _ in range(36)]
+        w_z, w_y, w_x = (plane(w_pad, i, p) for i in range(3))
+        degree = each(
+            lambda a, b, c, d, e, f: (a + b) + (c + d) + (e + f),
+            w_z, plane(w_pad, 0, p - 1), w_y, prev_y(w_y), w_x, prev_x(w_x),
+        )
+        qs, aabs_ = [], []
+        for c in range(LABELS):
+            v = plane(v2, c, p)
+            qs.append(each(
+                lambda d, x, a, b, e: d * x - 2.0 * (a + b + e),
+                degree, v, times(w_z, plane(v2, c, p + 1)), times(w_y, next_y(v)),
+                times(w_x, next_x(v)),
+            ))
+            aabs_.append(v)
+        for t, r in enumerate(own_tiles):
             abs_ = [tile(v1, (c, p), r) for c in range(LABELS)]
-            aabs = [tile(v2, (c, p), r) for c in range(LABELS)]
-            w = [tile(coef, (i, p), r) for i in (0, 2, 4, 6)]
-            qs = []
-            for c in range(LABELS):
-                v = aabs[c]
-                z, y, x = tile(v2, (c, p + 1), r), next_y(v2, (c, p), r, v), next_x(v)
-                qs.append([
-                    w[3][l] * v[l] - 2.0 * (w[0][l] * z[l] + w[1][l] * y[l] + w[2][l] * x[l])
-                    for l in range(len(lanes))
-                ])
             for l in range(len(lanes)):
-                ab, aab, q = [x[l] for x in abs_], [x[l] for x in aabs], [x[l] for x in qs]
+                ab, aab, q = [x[l] for x in abs_], [x[t][l] for x in aabs_], [x[t][l] for x in qs]
                 products = [ab[i] * aab[j] for i, j in half_pairs]
                 products += [aab[i] * aab[j] for i, j in half_pairs]
                 products += [aab[i] * q[j] for i, j in all_pairs]
                 for part, product in zip(parts, products):
                     part.append(product)
             for c in range(LABELS):
-                store(fields, (2, c, p - LO), r, aabs[c])
-        return tuple(x + total(part) for x, part in zip(acc, parts))
+                store(fields, (2, c, p - LO), r, aabs_[c][t])
+        add_up(30, parts)
+        return 0
 
     zero = jnp.zeros((8, 128), f32)
-    low = lax.fori_loop(LO, LO + depth, accumulate, (zero,) * 30)
-    high = lax.fori_loop(LO, LO + depth, accumulate_last, (zero,) * 36)
+    for n in range(66):
+        acc[n] = zero
+    lax.fori_loop(LO, LO + depth, accumulate, 0)
+    lax.fori_loop(LO, LO + depth, accumulate_last, 0)
+    low, high = [acc[n] for n in range(30)], [acc[30 + n] for n in range(36)]
     kept = {}
     for k in range(5):
         part = low[10 * k : 10 * k + 10] if k < 3 else high[10 * (k - 3) : 10 * (k - 3) + 10]
@@ -354,19 +410,20 @@
         scratch_shapes=[
             VMEM((2, planes, wide, cols), f32),
             VMEM((3, planes, wide, cols), f32),
-            VMEM((7, planes, wide, cols), f32),
+            VMEM((planes, wide, cols), f32),
             VMEM((LABELS, planes, wide, cols), f32),
             VMEM((LABELS, planes, wide, cols), f32),
             VMEM((LABELS, planes, wide, cols), f32),
+            VMEM((66, 8, 128), f32),
             VMEM((96, 128), f32),
         ],
         compiler_params=pltpu.CompilerParams(vmem_limit_bytes=48 * 2**20),
     )(arrays, *halos)
 
 
-def combine_kernel(mine, theirs, fields, arrays, out, coeffs):
+def combine_kernel(mine, theirs, fields, natural, out, coeffs, mixed):
     f32 = jnp.float32
-    _, depth, rows, cols = arrays.shape
+    _, depth, rows, cols = natural.shape
     sums = mine[...] + theirs[...]
     lane = lax.broadcasted_iota(jnp.int32, (8, 128), 1)
     row = lax.broadcasted_iota(jnp.int32, (8, 128), 0)
@@ -419,33 +476,44 @@
                 for l in range(0, cols, 128):
                     cut = (p, slice(r, r + 8), slice(l, l + 128))
                     v = [fields[(k // LABELS, k % LABELS) + cut] for k in range(3 * LABELS)]
-                    tag = arrays[(0,) + cut]
                     for c in (first, first + 1):
                         s = [v[k] * weights[c, k] for k in range(3 * LABELS)]
                         while len(s) > 1:
                             s = [x + y for x, y in zip(s[::2], s[1::2])] + (
                                 [s[-1]] if len(s) % 2 else []
                             )
-                        out[(c,) + cut] = jnp.where(tag == c, 1.0, s[0])
+                        mixed[(c,) + cut] = s[0]
             return 0
 
         lax.fori_loop(0, depth, body, 0)
 
-
-def combined(mine, theirs, fields, arrays):
+    back = interleave(cols, back=True)
+    for c in range(LABELS):
+        x = mixed[c].reshape(depth * rows, cols)
+        high = x.astype(jnp.bfloat16)
+        low = (x - high.astype(f32)).astype(jnp.bfloat16)
+        x = jnp.dot(high, back, preferred_element_type=f32)
+        x = x + jnp.dot(low, back, preferred_element_type=f32)
+        out[c] = jnp.where(natural[0] == c, 1.0, x.reshape(depth, rows, cols))
+
+
+def combined(mine, theirs, fields, natural):
     return pl.pallas_call(
         combine_kernel,
-        out_shape=jax.ShapeDtypeStruct((LABELS,) + arrays.shape[1:], jnp.float32),
+        out_shape=jax.ShapeDtypeStruct((LABELS,) + natural.shape[1:], jnp.float32),
         in_specs=[pl.BlockSpec(memory_space=VMEM)] * 4,
         out_specs=pl.BlockSpec(memory_space=VMEM),
-        scratch_shapes=[VMEM((LABELS, 16, 128), jnp.float32)],
+        scratch_shapes=[
+            VMEM((LABELS, 16, 128), jnp.float32),
+            VMEM((LABELS,) + natural.shape[1:], jnp.float32),
+        ],
         compiler_params=pltpu.CompilerParams(vmem_limit_bytes=32 * 2**20),
-    )(mine, theirs, fields, arrays)
+    )(mine, theirs, fields, natural)
 
 
 def per_device(counts, tags, depth_affinity, row_affinity, column_affinity):
     parts, nz, ny = counts
-    arrays = jnp.stack([tags, depth_affinity, row_affinity, column_affinity])
+    natural = jnp.stack([tags, depth_affinity, row_affinity, column_affinity])
     axes = ("parts", "gz", "gy")
     ze, zo = (lambda z: even_partner(z, nz)), (lambda z: odd_partner(z, nz))
     ye, yo = (lambda y: even_partner(y, ny)), (lambda y: odd_partner(y, ny))
@@ -459,7 +527,7 @@
             return pz(z) if pz else z, py(y) if py else y
         return exchanged(array, axes, counts, pair)
 
-    z_even, z_odd, y_odd, d_even, d_odd = pack(arrays)
+    arrays, z_even, z_odd, y_odd, d_even, d_odd = pack(natural)
     *sorted_halos, relay = relayed(
         arrays, swap(z_even, ze, None), swap(z_odd, zo, None), swap(y_odd, None, yo),
         swap(d_even, ze, yo), swap(d_odd, zo, yo),
@@ -474,7 +542,7 @@
         theirs = exchanged(moments, axes, counts, pair)
         if n < len(steps) - 1:
             moments = moments + theirs
-    return combined(moments, theirs, fields, arrays)
+    return combined(moments, theirs, fields, natural)
 
 
 def powers(count):

time: 37.5 us -> 36.1 us (0.963)
  Pallas kernels: 9.91 us -> 8.55 us
    pallas_call x1, Pallas kernels: 6.93 us -> 4.49 us  [krylov(): pl.pallas_call(functools.partial(krylov_kernel, counts), out_shape=[jax.S...]
    pallas_call x1, Pallas kernels: 2.75 us -> 3.38 us  [combined(): pl.pallas_call(combine_kernel, out_shape=jax.ShapeDtypeStruct((LABELS,) +...]
    pallas_call x2, Pallas kernels: 0.23 us -> 0.68 us  [the longest x1 0.55 us: pack(): pl.pallas_call(pack_kernel, out_shape=[jax.ShapeDtypeStruct(arrays.shape,...]
where the time goes in v3:
time: 36.1 us; the launch traced here: 36 us
  starting transfers between devices  14.9 us (41%)
  waiting for transfers between devices  11.3 us (31%)
  Pallas kernels  8.55 us (24%)
  other arithmetic  1.29 us (4%)
    ppermute x10, starting transfers between devices, exchanged(): return lax.ppermute(array, axes, route)  14.9 us
    ppermute x10, waiting for transfers between devices, exchanged(): return lax.ppermute(array, axes, route)  11.3 us
    pallas_call x1, Pallas kernels, krylov(): pl.pallas_call(functools.partial(krylov_kernel, counts), out_shape=[jax.S...  4.49 us
    pallas_call x1, Pallas kernels, combined(): pl.pallas_call(combine_kernel, out_shape=jax.ShapeDtypeStruct((LABELS,) +...  3.38 us
    another operation x1, other arithmetic, per_device(): natural = jnp.stack([tags, depth_affinity, row_affinity, column_affinity])  1.28 us
  transfers between devices with their start and end apart: 10, of which 7 were waited for; matrix products, arithmetic and copies ran while one was open for 0% of the time, Pallas kernels for 0%

profile of v3, /device:TPU:0, one launch (start us, length us, event | category | flops | bytes accessed | tf_op | source)
XLA Modules:
  0.0 36.0 jit_solution(14056780499700116451)
XLA Ops:
  0.0 1.3 %pad_add_fusion.natural = s32[4,8,16,384]{3,2,1,0:T(8,128)S(1)} fusion(s32[1,8,16,384]{3,2,1,0:T(8,128)} %bitcast.4, s32[1,8,16,384]{3,2,1,0:T(8,128)} %bitcast.5, s32[1,8,16,384]{3,2,1,0:T(8,128)} %bitcast.6, s32[1,8,16,384]{3,2,1,0:T(8,128)} %bitcast.7), kind=kLoop, calls=%fused_computation | loop fusion | flops 589824 | bytes 1572864 | tf_op jit(solution)/shard_map/stack | solution.py:516
  1.3 0.5 %shard_map.46 = (f32[4,8,16,384]{3,2,1,0:T(8,128)S(1)}, f32[13,16,384]{2,1,0:T(8,128)S(1)}, f32[13,16,384]{2,1,0:T(8,128)S(1)}, f32[16,8,384]{2,1,0:T(8,128)S(1)...) custom-call(s32[4,8,16,384]{3,2,1,0:T(8,128)S(1)} %pad_add_fusion.natural), custom_call_target="tpu_custom_call" | custom-call | tf_op jit(solution)/shard_map/pallas_call | solution.py:87
  1.8 3.1 %collective-permute-start = (f32[13,16,384]{2,1,0:T(8,128)S(1)}, f32[13,16,384]{2,1,0:T(8,128)S(1)}, u32[]{:S(2)}, u32[]{:S(2)}) collective-permute-start(f32[13,16,384]{2,1,0:T(8,128)S(1)} %get-tuple-element.20), channel_id=1, source_target_pairs={{0,4},{1,5},{2,6},{3,7},{4,0},{5,1},{6,2},{7,3},{8,12},{9,13},{10,... | collective-permute-start | bytes 958472 | tf_op jit(solution)/shard_map/ppermute | solution.py:43
  4.9 1.5 %collective-permute-start.2 = (f32[16,8,384]{2,1,0:T(8,128)S(1)}, f32[16,8,384]{2,1,0:T(8,128)S(1)}, u32[]{:S(2)}, u32[]{:S(2)}) collective-permute-start(f32[16,8,384]{2,1,0:T(8,128)S(1)} %get-tuple-element.22), channel_id=1, source_target_pairs={{0,16},{1,2},{2,1},{3,19},{4,20},{5,6},{6,5},{7,23},{8,24},{9,10},... | collective-permute-start | bytes 589832 | tf_op jit(solution)/shard_map/ppermute | solution.py:43
  6.4 0.5 %collective-permute-start.3 = (f32[6,8,384]{2,1,0:T(8,128)S(1)}, f32[6,8,384]{2,1,0:T(8,128)S(1)}, u32[]{:S(2)}, u32[]{:S(2)}) collective-permute-start(f32[6,8,384]{2,1,0:T(8,128)S(1)} %get-tuple-element.23), channel_id=1, source_target_pairs={{0,16},{1,6},{2,5},{3,19},{4,20},{5,2},{6,1},{7,23},{8,24},{9,14},... | collective-permute-start | bytes 221192 | tf_op jit(solution)/shard_map/ppermute | solution.py:43
  7.0 2.2 %collective-permute-start.4 = (f32[6,8,384]{2,1,0:T(8,128)S(1)}, f32[6,8,384]{2,1,0:T(8,128)S(1)}, u32[]{:S(2)}, u32[]{:S(2)}) collective-permute-start(f32[6,8,384]{2,1,0:T(8,128)S(1)} %get-tuple-element.24), channel_id=1, source_target_pairs={{0,1},{1,0},{2,3},{3,2},{4,20},{5,10},{6,9},{7,23},{8,24},{9,6},{1... | collective-permute-start | bytes 221192 | tf_op jit(solution)/shard_map/ppermute | solution.py:43
  9.1 2.3 %collective-permute-done.3.d_even = f32[6,8,384]{2,1,0:T(8,128)S(1)} collective-permute-done((f32[6,8,384]{2,1,0:T(8,128)S(1)}, f32[6,8,384]{2,1,0:T(8,128)S(1)}, u32[]{:S(2)}, u32[]{:S(2)}) %collective-permute-start.3) | collective-permute-done | bytes 73760 | tf_op jit(solution)/shard_map/ppermute | solution.py:43
  11.4 0.0 collective-permute-done.4.d_odd
  11.4 0.0 collective-permute-done.2.y_odd
  11.4 1.9 %collective-permute-done.z_even = f32[13,16,384]{2,1,0:T(8,128)S(1)} collective-permute-done((f32[13,16,384]{2,1,0:T(8,128)S(1)}, f32[13,16,384]{2,1,0:T(8,128)S(1)}, u32[]{:S(2)}, u32[]{:S(2)}) %collective-permute-start) | collective-permute-done | bytes 319520 | tf_op jit(solution)/shard_map/ppermute | solution.py:43
  13.3 0.0 collective-permute-done.1.z_odd
  13.3 0.1 shard_map.47
  13.4 1.0 %collective-permute-start.5 = (f32[27,8,384]{2,1,0:T(8,128)S(1)}, f32[27,8,384]{2,1,0:T(8,128)S(1)}, u32[]{:S(2)}, u32[]{:S(2)}) collective-permute-start(f32[27,8,384]{2,1,0:T(8,128)S(1)} %get-tuple-element.30), channel_id=1, source_target_pairs={{0,1},{1,0},{2,3},{3,2},{4,5},{5,4},{6,7},{7,6},{8,9},{9,8},{10,11... | collective-permute-start | bytes 995336 | tf_op jit(solution)/shard_map/ppermute | solution.py:43
  14.4 1.3 %collective-permute-done.5.relay = f32[27,8,384]{2,1,0:T(8,128)S(1)} collective-permute-done((f32[27,8,384]{2,1,0:T(8,128)S(1)}, f32[27,8,384]{2,1,0:T(8,128)S(1)}, u32[]{:S(2)}, u32[]{:S(2)}) %collective-permute-start.5) | collective-permute-done | bytes 331808 | tf_op jit(solution)/shard_map/ppermute | solution.py:43
  15.7 4.5 %shard_map.48 = (f32[3,4,8,16,384]{4,3,2,1,0:T(8,128)S(1)}, f32[8,128]{1,0:T(8,128)S(1)}) custom-call(f32[4,8,16,384]{3,2,1,0:T(8,128)S(1)} %get-tuple-element.19.arrays, f32[13,16,384]{2,1,0:T(8,128)S(1)} %get-tuple-element.25.before, f32[13,16,384]{2,1,0:T(8,128)S(1)} %get-tuple-element.26.after, f32[32,8,384]{2,1,0:T(8,128)S(1)} %get-tuple-element.27.ring_odd, ...), custom_call_target="tpu_custom_call" | custom-call | tf_op jit(solution)/shard_map/pallas_call | solution.py:402
  20.2 0.4 %collective-permute-start.6 = (f32[8,128]{1,0:T(8,128)S(1)}, f32[8,128]{1,0:T(8,128)S(1)}, u32[]{:S(2)}, u32[]{:S(2)}) collective-permute-start(f32[8,128]{1,0:T(8,128)S(1)} %get-tuple-element.31), channel_id=1, source_target_pairs={{0,1},{1,0},{2,3},{3,2},{4,5},{5,4},{6,7},{7,6},{8,9},{9,8},{10,11... | collective-permute-start | bytes 12296 | tf_op jit(solution)/shard_map/ppermute | solution.py:43
  20.6 0.8 %collective-permute-done.6 = f32[8,128]{1,0:T(8,128)S(1)} collective-permute-done((f32[8,128]{1,0:T(8,128)S(1)}, f32[8,128]{1,0:T(8,128)S(1)}, u32[]{:S(2)}, u32[]{:S(2)}) %collective-permute-start.6) | collective-permute-done | bytes 4128 | tf_op jit(solution)/shard_map/ppermute | solution.py:43
  21.4 0.6 %collective-permute-start.7 = (f32[8,128]{1,0:T(8,128)S(1)}, f32[8,128]{1,0:T(8,128)S(1)}, u32[]{:S(2)}, u32[]{:S(2)}) collective-permute-start(f32[8,128]{1,0:T(8,128)S(1)} %add.9), channel_id=1, source_target_pairs={{0,3},{1,2},{2,1},{3,0},{4,7},{5,6},{6,5},{7,4},{8,11},{9,10},{10,... | collective-permute-start | bytes 12296 | tf_op jit(solution)/shard_map/ppermute | solution.py:43
  22.0 2.4 %collective-permute-done.7 = f32[8,128]{1,0:T(8,128)S(1)} collective-permute-done((f32[8,128]{1,0:T(8,128)S(1)}, f32[8,128]{1,0:T(8,128)S(1)}, u32[]{:S(2)}, u32[]{:S(2)}) %collective-permute-start.7) | collective-permute-done | bytes 4128 | tf_op jit(solution)/shard_map/ppermute | solution.py:43
  24.4 2.6 %collective-permute-start.8 = (f32[8,128]{1,0:T(8,128)S(1)}, f32[8,128]{1,0:T(8,128)S(1)}, u32[]{:S(2)}, u32[]{:S(2)}) collective-permute-start(f32[8,128]{1,0:T(8,128)S(1)} %add.10), channel_id=1, source_target_pairs={{0,5},{1,4},{2,7},{3,6},{4,1},{5,0},{6,3},{7,2},{8,13},{9,12},{10,... | collective-permute-start | bytes 12296 | tf_op jit(solution)/shard_map/ppermute | solution.py:43
  27.1 1.3 %collective-permute-done.8 = f32[8,128]{1,0:T(8,128)S(1)} collective-permute-done((f32[8,128]{1,0:T(8,128)S(1)}, f32[8,128]{1,0:T(8,128)S(1)}, u32[]{:S(2)}, u32[]{:S(2)}) %collective-permute-start.8) | collective-permute-done | bytes 4128 | tf_op jit(solution)/shard_map/ppermute | solution.py:43
  28.4 2.9 %collective-permute-start.9 = (f32[8,128]{1,0:T(8,128)S(1)}, f32[8,128]{1,0:T(8,128)S(1)}, u32[]{:S(2)}, u32[]{:S(2)}) collective-permute-start(f32[8,128]{1,0:T(8,128)S(1)} %add.11.mine), channel_id=1, source_target_pairs={{0,9},{1,8},{2,11},{3,10},{4,13},{5,12},{6,15},{7,14},{8,1},{9,0},... | collective-permute-start | bytes 12296 | tf_op jit(solution)/shard_map/ppermute | solution.py:43
  31.3 1.3 %collective-permute-done.9.theirs = f32[8,128]{1,0:T(8,128)S(1)} collective-permute-done((f32[8,128]{1,0:T(8,128)S(1)}, f32[8,128]{1,0:T(8,128)S(1)}, u32[]{:S(2)}, u32[]{:S(2)}) %collective-permute-start.9) | collective-permute-done | bytes 4128 | tf_op jit(solution)/shard_map/ppermute | solution.py:43
  32.6 3.4 %shard_map.49 = f32[4,8,16,384]{3,2,1,0:T(8,128)} custom-call(f32[8,128]{1,0:T(8,128)S(1)} %add.11.mine, f32[8,128]{1,0:T(8,128)S(1)} %collective-permute-done.9.theirs, f32[3,4,8,16,384]{4,3,2,1,0:T(8,128)S(1)} %get-tuple-element.32.fields, s32[4,8,16,384]{3,2,1,0:T(8,128)S(1)} %pad_add_fusion.natural), custom_call_target="tpu_custom_call" | custom-call | tf_op jit(solution)/shard_map/pallas_call | solution.py:501
  (4 shorter events, 0.0 us)
Async XLA Ops:
  1.8 11.4 %collective-permute-start = (f32[13,16,384]{2,1,0:T(8,128)S(1)}, f32[13,16,384]{2,1,0:T(8,128)S(1)}, u32[]{:S(2)}, u32[]{:S(2)}) collective-permute-start(f32[13,16,384]{2,1,0:T(8,128)S(1)} %get-tuple-element.20), channel_id=1, source_target_pairs={{0,4},{1,5},{2,6},{3,7},{4,0},{5,1},{6,2},{7,3},{8,12},{9,13},{10,... | collective-permute-start | bytes 958472 | tf_op jit(solution)/shard_map/ppermute | solution.py:43
  4.9 8.3 %collective-permute-start.1 = (f32[13,16,384]{2,1,0:T(8,128)S(1)}, f32[13,16,384]{2,1,0:T(8,128)S(1)}, u32[]{:S(2)}, u32[]{:S(2)}) collective-permute-start(f32[13,16,384]{2,1,0:T(8,128)S(1)} %get-tuple-element.21), channel_id=1, source_target_pairs={{0,1},{1,0},{2,3},{3,2},{4,8},{5,9},{6,10},{7,11},{8,4},{9,5},{10,... | collective-permute-start | bytes 958472 | tf_op jit(solution)/shard_map/ppermute | solution.py:43
  4.9 6.5 %collective-permute-start.2 = (f32[16,8,384]{2,1,0:T(8,128)S(1)}, f32[16,8,384]{2,1,0:T(8,128)S(1)}, u32[]{:S(2)}, u32[]{:S(2)}) collective-permute-start(f32[16,8,384]{2,1,0:T(8,128)S(1)} %get-tuple-element.22), channel_id=1, source_target_pairs={{0,16},{1,2},{2,1},{3,19},{4,20},{5,6},{6,5},{7,23},{8,24},{9,10},... | collective-permute-start | bytes 589832 | tf_op jit(solution)/shard_map/ppermute | solution.py:43
  6.4 4.9 %collective-permute-start.3 = (f32[6,8,384]{2,1,0:T(8,128)S(1)}, f32[6,8,384]{2,1,0:T(8,128)S(1)}, u32[]{:S(2)}, u32[]{:S(2)}) collective-permute-start(f32[6,8,384]{2,1,0:T(8,128)S(1)} %get-tuple-element.23), channel_id=1, source_target_pairs={{0,16},{1,6},{2,5},{3,19},{4,20},{5,2},{6,1},{7,23},{8,24},{9,14},... | collective-permute-start | bytes 221192 | tf_op jit(solution)/shard_map/ppermute | solution.py:43
  7.0 4.4 %collective-permute-start.4 = (f32[6,8,384]{2,1,0:T(8,128)S(1)}, f32[6,8,384]{2,1,0:T(8,128)S(1)}, u32[]{:S(2)}, u32[]{:S(2)}) collective-permute-start(f32[6,8,384]{2,1,0:T(8,128)S(1)} %get-tuple-element.24), channel_id=1, source_target_pairs={{0,1},{1,0},{2,3},{3,2},{4,20},{5,10},{6,9},{7,23},{8,24},{9,6},{1... | collective-permute-start | bytes 221192 | tf_op jit(solution)/shard_map/ppermute | solution.py:43
  13.4 2.3 %collective-permute-start.5 = (f32[27,8,384]{2,1,0:T(8,128)S(1)}, f32[27,8,384]{2,1,0:T(8,128)S(1)}, u32[]{:S(2)}, u32[]{:S(2)}) collective-permute-start(f32[27,8,384]{2,1,0:T(8,128)S(1)} %get-tuple-element.30), channel_id=1, source_target_pairs={{0,1},{1,0},{2,3},{3,2},{4,5},{5,4},{6,7},{7,6},{8,9},{9,8},{10,11... | collective-permute-start | bytes 995336 | tf_op jit(solution)/shard_map/ppermute | solution.py:43
  20.2 1.2 %collective-permute-start.6 = (f32[8,128]{1,0:T(8,128)S(1)}, f32[8,128]{1,0:T(8,128)S(1)}, u32[]{:S(2)}, u32[]{:S(2)}) collective-permute-start(f32[8,128]{1,0:T(8,128)S(1)} %get-tuple-element.31), channel_id=1, source_target_pairs={{0,1},{1,0},{2,3},{3,2},{4,5},{5,4},{6,7},{7,6},{8,9},{9,8},{10,11... | collective-permute-start | bytes 12296 | tf_op jit(solution)/shard_map/ppermute | solution.py:43
  21.4 3.0 %collective-permute-start.7 = (f32[8,128]{1,0:T(8,128)S(1)}, f32[8,128]{1,0:T(8,128)S(1)}, u32[]{:S(2)}, u32[]{:S(2)}) collective-permute-start(f32[8,128]{1,0:T(8,128)S(1)} %add.9), channel_id=1, source_target_pairs={{0,3},{1,2},{2,1},{3,0},{4,7},{5,6},{6,5},{7,4},{8,11},{9,10},{10,... | collective-permute-start | bytes 12296 | tf_op jit(solution)/shard_map/ppermute | solution.py:43
  24.4 4.0 %collective-permute-start.8 = (f32[8,128]{1,0:T(8,128)S(1)}, f32[8,128]{1,0:T(8,128)S(1)}, u32[]{:S(2)}, u32[]{:S(2)}) collective-permute-start(f32[8,128]{1,0:T(8,128)S(1)} %add.10), channel_id=1, source_target_pairs={{0,5},{1,4},{2,7},{3,6},{4,1},{5,0},{6,3},{7,2},{8,13},{9,12},{10,... | collective-permute-start | bytes 12296 | tf_op jit(solution)/shard_map/ppermute | solution.py:43
  28.4 4.2 %collective-permute-start.9 = (f32[8,128]{1,0:T(8,128)S(1)}, f32[8,128]{1,0:T(8,128)S(1)}, u32[]{:S(2)}, u32[]{:S(2)}) collective-permute-start(f32[8,128]{1,0:T(8,128)S(1)} %add.11.mine), channel_id=1, source_target_pairs={{0,9},{1,8},{2,11},{3,10},{4,13},{5,12},{6,15},{7,14},{8,1},{9,0},... | collective-permute-start | bytes 12296 | tf_op jit(solution)/shard_map/ppermute | solution.py:43

commit v4 on v3

--- a/solution.py
+++ b/solution.py
@@ -15,6 +15,7 @@
 CORNER_WIDTHS = (3, 3, 3, 2)
 CORNERS = [(a, i) for a, width in enumerate(CORNER_WIDTHS) for i in range(width)]
 PAIR = 4096.0
+CHUNKS = 4
 GROUP = 4
 VMEM = pltpu.VMEM
 
@@ -421,91 +422,118 @@
     )(arrays, *halos)
 
 
-def combine_kernel(mine, theirs, fields, natural, out, coeffs, mixed):
+def solved(moment, sides, floor):
+    n = 3 * LABELS
+    system = {
+        (i, j): moment(i // LABELS + j // LABELS + 1, i % LABELS, j % LABELS)
+        for i in range(n) for j in range(i + 1)
+    }
+    right = dict(enumerate(sides))
+    first = {k: system[k, k] for k in range(n)}
+    lower, inverse = {}, {}
+    for k in range(n):
+        pivot = system[k, k]
+        sound = pivot > floor * first[k]
+        inverse[k] = jnp.where(sound, 1.0 / jnp.where(sound, pivot, 1.0), 0.0)
+        for i in range(k + 1, n):
+            lower[i, k] = system[i, k] * inverse[k]
+        for i in range(k + 1, n):
+            for j in range(k + 1, i + 1):
+                system[i, j] = system[i, j] - lower[i, k] * system[j, k]
+            right[i] = right[i] - lower[i, k] * right[k]
+    for k in reversed(range(n)):
+        x = right[k] * inverse[k]
+        for i in range(k + 1, n):
+            x = x - lower[i, k] * right[i]
+        right[k] = x
+    return [right[k] for k in range(n)]
+
+
+def combine_kernel(mine, theirs, fields, natural, out, spread, coeffs, mixed, buffer, sems):
     f32 = jnp.float32
     _, depth, rows, cols = natural.shape
     sums = mine[...] + theirs[...]
-    lane = lax.broadcasted_iota(jnp.int32, (8, 128), 1)
-    row = lax.broadcasted_iota(jnp.int32, (8, 128), 0)
-
-    def splat(column):
-        return jnp.broadcast_to(column, (8, 128))
-
-    columns = {}
-    for k in range(6):
-        for h in range(2):
-            x = splat(sums[:, 2 * k + h : 2 * k + h + 1])
-            columns[k, 2 * h] = x
-            columns[k, 2 * h + 1] = pltpu.roll(x, 4, 0)
-    blocks = []
-    for i in range(3):
-        x = jnp.zeros((8, 128), f32)
-        for j, k in enumerate((i + 1, i + 2, i + 3, i)):
-            for b in range(LABELS):
-                x = jnp.where(lane == 4 * j + b, columns[k, b], x)
-        blocks.append(x)
-    system = [
-        jnp.where(row < 4, blocks[0], pltpu.roll(blocks[1], 4, 0)),
-        jnp.where(row < 4, blocks[2], 0.0),
-    ]
-    start = list(system)
-    for k in range(3 * LABELS):
-        n, r = divmod(k, 8)
-        pivot_row = system[n][r : r + 1, :]
-        pivot = pivot_row[:, k : k + 1]
-        sound = pivot > PIVOT_FLOOR * start[n][r : r + 1, k : k + 1]
-        scale = jnp.where(sound, 1.0 / jnp.where(sound, pivot, 1.0), 0.0)
-        pivot_row = pivot_row * scale
-        for m in range(2):
-            x = system[m] - system[m][:, k : k + 1] * pivot_row
-            system[m] = jnp.where(row == r, pivot_row, x) if m == n else x
-    for c in range(LABELS):
-        for m in range(2):
-            at = 3 * LABELS + c
-            coeffs[c, 8 * m : 8 * m + 8, :] = splat(system[m][:, at : at + 1])
-
-    for first in range(0, LABELS, 2):
-        weights = {
-            (c, k): jnp.broadcast_to(coeffs[c, k : k + 1, :], (8, 128))
-            for c in (first, first + 1)
-            for k in range(3 * LABELS)
-        }
-
-        def body(p, _):
-            for r in range(0, rows, 8):
-                for l in range(0, cols, 128):
-                    cut = (p, slice(r, r + 8), slice(l, l + 128))
-                    v = [fields[(k // LABELS, k % LABELS) + cut] for k in range(3 * LABELS)]
-                    for c in (first, first + 1):
-                        s = [v[k] * weights[c, k] for k in range(3 * LABELS)]
-                        while len(s) > 1:
-                            s = [x + y for x, y in zip(s[::2], s[1::2])] + (
-                                [s[-1]] if len(s) % 2 else []
-                            )
-                        mixed[(c,) + cut] = s[0]
-            return 0
-
-        lax.fori_loop(0, depth, body, 0)
+    columns = [jnp.broadcast_to(sums[:, g : g + 1], (8, 128)) for g in range(12)]
+    for g in range(12):
+        spread[g] = columns[g]
+
+    def moment(k, a, b):
+        a, b = min(a, b), max(a, b)
+        at = (b % 2) * 4 + a
+        return jnp.broadcast_to(spread[2 * k + b // 2, at : at + 1, :], (8, 128))
+
+    sides = []
+    for k in range(3):
+        for a in range(LABELS):
+            x = columns[2 * k + a // 2]
+            sides.append(pltpu.roll(x, 4, 0) if a % 2 else x)
+    for k, x in enumerate(solved(moment, sides, PIVOT_FLOOR)):
+        coeffs[k] = x
 
     back = interleave(cols, back=True)
-    for c in range(LABELS):
-        x = mixed[c].reshape(depth * rows, cols)
+    chunk = depth // CHUNKS
+
+    def combine(n):
+        for first in range(0, LABELS, 2):
+            weights = {
+                (k, c): jnp.broadcast_to(coeffs[k, c : c + 1, :], (8, 128))
+                for k in range(3 * LABELS) for c in (first, first + 1)
+            }
+            for p in range(n * chunk, n * chunk + chunk):
+                for r in range(0, rows, 8):
+                    for l in range(0, cols, 128):
+                        cut = (p, slice(r, r + 8), slice(l, l + 128))
+                        v = [fields[(k // LABELS, k % LABELS) + cut] for k in range(3 * LABELS)]
+                        for c in (first, first + 1):
+                            s = [v[k] * weights[k, c] for k in range(3 * LABELS)]
+                            while len(s) > 1:
+                                s = [x + y for x, y in zip(s[::2], s[1::2])] + (
+                                    [s[-1]] if len(s) % 2 else []
+                                )
+                            mixed[(c,) + cut] = s[0]
+
+    def turn_back(n):
+        planes = slice(n * chunk, n * chunk + chunk)
+        x = mixed[:, planes].reshape(LABELS * chunk * rows, cols)
         high = x.astype(jnp.bfloat16)
         low = (x - high.astype(f32)).astype(jnp.bfloat16)
         x = jnp.dot(high, back, preferred_element_type=f32)
         x = x + jnp.dot(low, back, preferred_element_type=f32)
-        out[c] = jnp.where(natural[0] == c, 1.0, x.reshape(depth, rows, cols))
+        x = x.reshape(LABELS, chunk, rows, cols)
+        for c in range(LABELS):
+            buffer[c, planes] = jnp.where(natural[0, planes] == c, 1.0, x[c])
+
+    copies = [
+        pltpu.make_async_copy(
+            buffer.at[:, n * chunk : (n + 1) * chunk], out.at[:, n * chunk : (n + 1) * chunk],
+            sems.at[n],
+        )
+        for n in range(CHUNKS)
+    ]
+    combine(0)
+    for n in range(CHUNKS):
+        if n + 1 < CHUNKS:
+            combine(n + 1)
+        turn_back(n)
+        copies[n].start()
+    for copy in copies:
+        copy.wait()
 
 
 def combined(mine, theirs, fields, natural):
+    _, depth, rows, cols = natural.shape
+    f32 = jnp.float32
     return pl.pallas_call(
         combine_kernel,
-        out_shape=jax.ShapeDtypeStruct((LABELS,) + natural.shape[1:], jnp.float32),
+        out_shape=jax.ShapeDtypeStruct((LABELS, depth, rows, cols), f32),
         in_specs=[pl.BlockSpec(memory_space=VMEM)] * 4,
-        out_specs=pl.BlockSpec(memory_space=VMEM),
+        out_specs=pl.BlockSpec(memory_space=pltpu.HBM),
         scratch_shapes=[
-            VMEM((LABELS, 16, 128), jnp.float32),
-            VMEM((LABELS,) + natural.shape[1:], jnp.float32),
+            VMEM((12, 8, 128), f32),
+            VMEM((3 * LABELS, 8, 128), f32),
+            VMEM((LABELS, depth, rows, cols), f32),
+            VMEM((LABELS, depth, rows, cols), f32),
+            pltpu.SemaphoreType.DMA((CHUNKS,)),
         ],
         compiler_params=pltpu.CompilerParams(vmem_limit_bytes=32 * 2**20),
     )(mine, theirs, fields, natural)

time: 36.1 us -> 35.2 us (0.975)
  Pallas kernels: 8.55 us -> 7.55 us
    pallas_call x1, Pallas kernels: 3.38 us -> 2.39 us  [combined(): pl.pallas_call(combine_kernel, out_shape=jax.ShapeDtypeStruct((LABELS, de...]
where the time goes in v4:
time: 35.2 us; the launch traced here: 35 us
  starting transfers between devices  14.9 us (42%)
  waiting for transfers between devices  11.3 us (32%)
  Pallas kernels  7.55 us (21%)
  other arithmetic  1.29 us (4%)
    ppermute x10, starting transfers between devices, exchanged(): return lax.ppermute(array, axes, route)  14.9 us
    ppermute x10, waiting for transfers between devices, exchanged(): return lax.ppermute(array, axes, route)  11.3 us
    pallas_call x1, Pallas kernels, krylov(): pl.pallas_call(functools.partial(krylov_kernel, counts), out_shape=[jax.S...  4.49 us
    pallas_call x1, Pallas kernels, combined(): pl.pallas_call(combine_kernel, out_shape=jax.ShapeDtypeStruct((LABELS, de...  2.39 us
    another operation x1, other arithmetic, per_device(): natural = jnp.stack([tags, depth_affinity, row_affinity, column_affinity])  1.28 us
  transfers between devices with their start and end apart: 10, of which 7 were waited for; matrix products, arithmetic and copies ran while one was open for 0% of the time, Pallas kernels for 0%

profile of v4, /device:TPU:0, one launch (start us, length us, event | category | flops | bytes accessed | tf_op | source)
XLA Modules:
  0.0 35.0 jit_solution(14720148432284719384)
XLA Ops:
  0.0 1.3 %pad_add_fusion.natural = s32[4,8,16,384]{3,2,1,0:T(8,128)S(1)} fusion(s32[1,8,16,384]{3,2,1,0:T(8,128)} %bitcast.4, s32[1,8,16,384]{3,2,1,0:T(8,128)} %bitcast.5, s32[1,8,16,384]{3,2,1,0:T(8,128)} %bitcast.6, s32[1,8,16,384]{3,2,1,0:T(8,128)} %bitcast.7), kind=kLoop, calls=%fused_computation | loop fusion | flops 589824 | bytes 1572864 | tf_op jit(solution)/shard_map/stack | solution.py:544
  1.3 0.5 %shard_map.46 = (f32[4,8,16,384]{3,2,1,0:T(8,128)S(1)}, f32[13,16,384]{2,1,0:T(8,128)S(1)}, f32[13,16,384]{2,1,0:T(8,128)S(1)}, f32[16,8,384]{2,1,0:T(8,128)S(1)...) custom-call(s32[4,8,16,384]{3,2,1,0:T(8,128)S(1)} %pad_add_fusion.natural), custom_call_target="tpu_custom_call" | custom-call | tf_op jit(solution)/shard_map/pallas_call | solution.py:88
  1.8 3.1 %collective-permute-start = (f32[13,16,384]{2,1,0:T(8,128)S(1)}, f32[13,16,384]{2,1,0:T(8,128)S(1)}, u32[]{:S(2)}, u32[]{:S(2)}) collective-permute-start(f32[13,16,384]{2,1,0:T(8,128)S(1)} %get-tuple-element.20), channel_id=1, source_target_pairs={{0,4},{1,5},{2,6},{3,7},{4,0},{5,1},{6,2},{7,3},{8,12},{9,13},{10,... | collective-permute-start | bytes 958472 | tf_op jit(solution)/shard_map/ppermute | solution.py:44
  4.9 0.0 collective-permute-start.1
  4.9 1.5 %collective-permute-start.2 = (f32[16,8,384]{2,1,0:T(8,128)S(1)}, f32[16,8,384]{2,1,0:T(8,128)S(1)}, u32[]{:S(2)}, u32[]{:S(2)}) collective-permute-start(f32[16,8,384]{2,1,0:T(8,128)S(1)} %get-tuple-element.22), channel_id=1, source_target_pairs={{0,16},{1,2},{2,1},{3,19},{4,20},{5,6},{6,5},{7,23},{8,24},{9,10},... | collective-permute-start | bytes 589832 | tf_op jit(solution)/shard_map/ppermute | solution.py:44
  6.4 0.5 %collective-permute-start.3 = (f32[6,8,384]{2,1,0:T(8,128)S(1)}, f32[6,8,384]{2,1,0:T(8,128)S(1)}, u32[]{:S(2)}, u32[]{:S(2)}) collective-permute-start(f32[6,8,384]{2,1,0:T(8,128)S(1)} %get-tuple-element.23), channel_id=1, source_target_pairs={{0,16},{1,6},{2,5},{3,19},{4,20},{5,2},{6,1},{7,23},{8,24},{9,14},... | collective-permute-start | bytes 221192 | tf_op jit(solution)/shard_map/ppermute | solution.py:44
  7.0 2.2 %collective-permute-start.4 = (f32[6,8,384]{2,1,0:T(8,128)S(1)}, f32[6,8,384]{2,1,0:T(8,128)S(1)}, u32[]{:S(2)}, u32[]{:S(2)}) collective-permute-start(f32[6,8,384]{2,1,0:T(8,128)S(1)} %get-tuple-element.24), channel_id=1, source_target_pairs={{0,1},{1,0},{2,3},{3,2},{4,20},{5,10},{6,9},{7,23},{8,24},{9,6},{1... | collective-permute-start | bytes 221192 | tf_op jit(solution)/shard_map/ppermute | solution.py:44
  9.1 2.3 %collective-permute-done.3.d_even = f32[6,8,384]{2,1,0:T(8,128)S(1)} collective-permute-done((f32[6,8,384]{2,1,0:T(8,128)S(1)}, f32[6,8,384]{2,1,0:T(8,128)S(1)}, u32[]{:S(2)}, u32[]{:S(2)}) %collective-permute-start.3) | collective-permute-done | bytes 73760 | tf_op jit(solution)/shard_map/ppermute | solution.py:44
  11.4 0.0 collective-permute-done.4.d_odd
  11.4 1.9 %collective-permute-done.z_even = f32[13,16,384]{2,1,0:T(8,128)S(1)} collective-permute-done((f32[13,16,384]{2,1,0:T(8,128)S(1)}, f32[13,16,384]{2,1,0:T(8,128)S(1)}, u32[]{:S(2)}, u32[]{:S(2)}) %collective-permute-start) | collective-permute-done | bytes 319520 | tf_op jit(solution)/shard_map/ppermute | solution.py:44
  13.3 0.0 collective-permute-done.1.z_odd
  13.3 0.1 shard_map.47
  13.4 1.0 %collective-permute-start.5 = (f32[27,8,384]{2,1,0:T(8,128)S(1)}, f32[27,8,384]{2,1,0:T(8,128)S(1)}, u32[]{:S(2)}, u32[]{:S(2)}) collective-permute-start(f32[27,8,384]{2,1,0:T(8,128)S(1)} %get-tuple-element.30), channel_id=1, source_target_pairs={{0,1},{1,0},{2,3},{3,2},{4,5},{5,4},{6,7},{7,6},{8,9},{9,8},{10,11... | collective-permute-start | bytes 995336 | tf_op jit(solution)/shard_map/ppermute | solution.py:44
  14.4 1.3 %collective-permute-done.5.relay = f32[27,8,384]{2,1,0:T(8,128)S(1)} collective-permute-done((f32[27,8,384]{2,1,0:T(8,128)S(1)}, f32[27,8,384]{2,1,0:T(8,128)S(1)}, u32[]{:S(2)}, u32[]{:S(2)}) %collective-permute-start.5) | collective-permute-done | bytes 331808 | tf_op jit(solution)/shard_map/ppermute | solution.py:44
  15.7 4.5 %shard_map.48 = (f32[3,4,8,16,384]{4,3,2,1,0:T(8,128)S(1)}, f32[8,128]{1,0:T(8,128)S(1)}) custom-call(f32[4,8,16,384]{3,2,1,0:T(8,128)S(1)} %get-tuple-element.19.arrays, f32[13,16,384]{2,1,0:T(8,128)S(1)} %get-tuple-element.25.before, f32[13,16,384]{2,1,0:T(8,128)S(1)} %get-tuple-element.26.after, f32[32,8,384]{2,1,0:T(8,128)S(1)} %get-tuple-element.27.ring_odd, ...), custom_call_target="tpu_custom_call" | custom-call | tf_op jit(solution)/shard_map/pallas_call | solution.py:403
  20.2 0.4 %collective-permute-start.6 = (f32[8,128]{1,0:T(8,128)S(1)}, f32[8,128]{1,0:T(8,128)S(1)}, u32[]{:S(2)}, u32[]{:S(2)}) collective-permute-start(f32[8,128]{1,0:T(8,128)S(1)} %get-tuple-element.31), channel_id=1, source_target_pairs={{0,1},{1,0},{2,3},{3,2},{4,5},{5,4},{6,7},{7,6},{8,9},{9,8},{10,11... | collective-permute-start | bytes 12296 | tf_op jit(solution)/shard_map/ppermute | solution.py:44
  20.6 0.8 %collective-permute-done.6 = f32[8,128]{1,0:T(8,128)S(1)} collective-permute-done((f32[8,128]{1,0:T(8,128)S(1)}, f32[8,128]{1,0:T(8,128)S(1)}, u32[]{:S(2)}, u32[]{:S(2)}) %collective-permute-start.6) | collective-permute-done | bytes 4128 | tf_op jit(solution)/shard_map/ppermute | solution.py:44
  21.4 0.6 %collective-permute-start.7 = (f32[8,128]{1,0:T(8,128)S(1)}, f32[8,128]{1,0:T(8,128)S(1)}, u32[]{:S(2)}, u32[]{:S(2)}) collective-permute-start(f32[8,128]{1,0:T(8,128)S(1)} %add.9), channel_id=1, source_target_pairs={{0,3},{1,2},{2,1},{3,0},{4,7},{5,6},{6,5},{7,4},{8,11},{9,10},{10,... | collective-permute-start | bytes 12296 | tf_op jit(solution)/shard_map/ppermute | solution.py:44
  22.0 2.4 %collective-permute-done.7 = f32[8,128]{1,0:T(8,128)S(1)} collective-permute-done((f32[8,128]{1,0:T(8,128)S(1)}, f32[8,128]{1,0:T(8,128)S(1)}, u32[]{:S(2)}, u32[]{:S(2)}) %collective-permute-start.7) | collective-permute-done | bytes 4128 | tf_op jit(solution)/shard_map/ppermute | solution.py:44
  24.4 2.6 %collective-permute-start.8 = (f32[8,128]{1,0:T(8,128)S(1)}, f32[8,128]{1,0:T(8,128)S(1)}, u32[]{:S(2)}, u32[]{:S(2)}) collective-permute-start(f32[8,128]{1,0:T(8,128)S(1)} %add.10), channel_id=1, source_target_pairs={{0,5},{1,4},{2,7},{3,6},{4,1},{5,0},{6,3},{7,2},{8,13},{9,12},{10,... | collective-permute-start | bytes 12296 | tf_op jit(solution)/shard_map/ppermute | solution.py:44
  27.1 1.3 %collective-permute-done.8 = f32[8,128]{1,0:T(8,128)S(1)} collective-permute-done((f32[8,128]{1,0:T(8,128)S(1)}, f32[8,128]{1,0:T(8,128)S(1)}, u32[]{:S(2)}, u32[]{:S(2)}) %collective-permute-start.8) | collective-permute-done | bytes 4128 | tf_op jit(solution)/shard_map/ppermute | solution.py:44
  28.4 2.9 %collective-permute-start.9 = (f32[8,128]{1,0:T(8,128)S(1)}, f32[8,128]{1,0:T(8,128)S(1)}, u32[]{:S(2)}, u32[]{:S(2)}) collective-permute-start(f32[8,128]{1,0:T(8,128)S(1)} %add.11.mine), channel_id=1, source_target_pairs={{0,9},{1,8},{2,11},{3,10},{4,13},{5,12},{6,15},{7,14},{8,1},{9,0},... | collective-permute-start | bytes 12296 | tf_op jit(solution)/shard_map/ppermute | solution.py:44
  31.3 1.3 %collective-permute-done.9.theirs = f32[8,128]{1,0:T(8,128)S(1)} collective-permute-done((f32[8,128]{1,0:T(8,128)S(1)}, f32[8,128]{1,0:T(8,128)S(1)}, u32[]{:S(2)}, u32[]{:S(2)}) %collective-permute-start.9) | collective-permute-done | bytes 4128 | tf_op jit(solution)/shard_map/ppermute | solution.py:44
  32.6 2.4 %shard_map.49 = f32[4,8,16,384]{3,2,1,0:T(8,128)} custom-call(f32[8,128]{1,0:T(8,128)S(1)} %add.11.mine, f32[8,128]{1,0:T(8,128)S(1)} %collective-permute-done.9.theirs, f32[3,4,8,16,384]{4,3,2,1,0:T(8,128)S(1)} %get-tuple-element.32.fields, s32[4,8,16,384]{3,2,1,0:T(8,128)S(1)} %pad_add_fusion.natural), custom_call_target="tpu_custom_call" | custom-call | tf_op jit(solution)/shard_map/pallas_call | solution.py:526
  (4 shorter events, 0.0 us)
Async XLA Ops:
  1.8 11.4 %collective-permute-start = (f32[13,16,384]{2,1,0:T(8,128)S(1)}, f32[13,16,384]{2,1,0:T(8,128)S(1)}, u32[]{:S(2)}, u32[]{:S(2)}) collective-permute-start(f32[13,16,384]{2,1,0:T(8,128)S(1)} %get-tuple-element.20), channel_id=1, source_target_pairs={{0,4},{1,5},{2,6},{3,7},{4,0},{5,1},{6,2},{7,3},{8,12},{9,13},{10,... | collective-permute-start | bytes 958472 | tf_op jit(solution)/shard_map/ppermute | solution.py:44
  4.9 8.3 %collective-permute-start.1 = (f32[13,16,384]{2,1,0:T(8,128)S(1)}, f32[13,16,384]{2,1,0:T(8,128)S(1)}, u32[]{:S(2)}, u32[]{:S(2)}) collective-permute-start(f32[13,16,384]{2,1,0:T(8,128)S(1)} %get-tuple-element.21), channel_id=1, source_target_pairs={{0,1},{1,0},{2,3},{3,2},{4,8},{5,9},{6,10},{7,11},{8,4},{9,5},{10,... | collective-permute-start | bytes 958472 | tf_op jit(solution)/shard_map/ppermute | solution.py:44
  4.9 6.5 %collective-permute-start.2 = (f32[16,8,384]{2,1,0:T(8,128)S(1)}, f32[16,8,384]{2,1,0:T(8,128)S(1)}, u32[]{:S(2)}, u32[]{:S(2)}) collective-permute-start(f32[16,8,384]{2,1,0:T(8,128)S(1)} %get-tuple-element.22), channel_id=1, source_target_pairs={{0,16},{1,2},{2,1},{3,19},{4,20},{5,6},{6,5},{7,23},{8,24},{9,10},... | collective-permute-start | bytes 589832 | tf_op jit(solution)/shard_map/ppermute | solution.py:44
  6.4 4.9 %collective-permute-start.3 = (f32[6,8,384]{2,1,0:T(8,128)S(1)}, f32[6,8,384]{2,1,0:T(8,128)S(1)}, u32[]{:S(2)}, u32[]{:S(2)}) collective-permute-start(f32[6,8,384]{2,1,0:T(8,128)S(1)} %get-tuple-element.23), channel_id=1, source_target_pairs={{0,16},{1,6},{2,5},{3,19},{4,20},{5,2},{6,1},{7,23},{8,24},{9,14},... | collective-permute-start | bytes 221192 | tf_op jit(solution)/shard_map/ppermute | solution.py:44
  7.0 4.4 %collective-permute-start.4 = (f32[6,8,384]{2,1,0:T(8,128)S(1)}, f32[6,8,384]{2,1,0:T(8,128)S(1)}, u32[]{:S(2)}, u32[]{:S(2)}) collective-permute-start(f32[6,8,384]{2,1,0:T(8,128)S(1)} %get-tuple-element.24), channel_id=1, source_target_pairs={{0,1},{1,0},{2,3},{3,2},{4,20},{5,10},{6,9},{7,23},{8,24},{9,6},{1... | collective-permute-start | bytes 221192 | tf_op jit(solution)/shard_map/ppermute | solution.py:44
  13.4 2.3 %collective-permute-start.5 = (f32[27,8,384]{2,1,0:T(8,128)S(1)}, f32[27,8,384]{2,1,0:T(8,128)S(1)}, u32[]{:S(2)}, u32[]{:S(2)}) collective-permute-start(f32[27,8,384]{2,1,0:T(8,128)S(1)} %get-tuple-element.30), channel_id=1, source_target_pairs={{0,1},{1,0},{2,3},{3,2},{4,5},{5,4},{6,7},{7,6},{8,9},{9,8},{10,11... | collective-permute-start | bytes 995336 | tf_op jit(solution)/shard_map/ppermute | solution.py:44
  20.2 1.2 %collective-permute-start.6 = (f32[8,128]{1,0:T(8,128)S(1)}, f32[8,128]{1,0:T(8,128)S(1)}, u32[]{:S(2)}, u32[]{:S(2)}) collective-permute-start(f32[8,128]{1,0:T(8,128)S(1)} %get-tuple-element.31), channel_id=1, source_target_pairs={{0,1},{1,0},{2,3},{3,2},{4,5},{5,4},{6,7},{7,6},{8,9},{9,8},{10,11... | collective-permute-start | bytes 12296 | tf_op jit(solution)/shard_map/ppermute | solution.py:44
  21.4 3.0 %collective-permute-start.7 = (f32[8,128]{1,0:T(8,128)S(1)}, f32[8,128]{1,0:T(8,128)S(1)}, u32[]{:S(2)}, u32[]{:S(2)}) collective-permute-start(f32[8,128]{1,0:T(8,128)S(1)} %add.9), channel_id=1, source_target_pairs={{0,3},{1,2},{2,1},{3,0},{4,7},{5,6},{6,5},{7,4},{8,11},{9,10},{10,... | collective-permute-start | bytes 12296 | tf_op jit(solution)/shard_map/ppermute | solution.py:44
  24.4 4.0 %collective-permute-start.8 = (f32[8,128]{1,0:T(8,128)S(1)}, f32[8,128]{1,0:T(8,128)S(1)}, u32[]{:S(2)}, u32[]{:S(2)}) collective-permute-start(f32[8,128]{1,0:T(8,128)S(1)} %add.10), channel_id=1, source_target_pairs={{0,5},{1,4},{2,7},{3,6},{4,1},{5,0},{6,3},{7,2},{8,13},{9,12},{10,... | collective-permute-start | bytes 12296 | tf_op jit(solution)/shard_map/ppermute | solution.py:44
  28.4 4.2 %collective-permute-start.9 = (f32[8,128]{1,0:T(8,128)S(1)}, f32[8,128]{1,0:T(8,128)S(1)}, u32[]{:S(2)}, u32[]{:S(2)}) collective-permute-start(f32[8,128]{1,0:T(8,128)S(1)} %add.11.mine), channel_id=1, source_target_pairs={{0,9},{1,8},{2,11},{3,10},{4,13},{5,12},{6,15},{7,14},{8,1},{9,0},... | collective-permute-start | bytes 12296 | tf_op jit(solution)/shard_map/ppermute | solution.py:44

commit v5 on v4

--- a/solution.py
+++ b/solution.py
@@ -1,4 +1,5 @@
 import functools
+import types
 
 import jax
 import jax.numpy as jnp
@@ -16,7 +17,6 @@
 CORNERS = [(a, i) for a, width in enumerate(CORNER_WIDTHS) for i in range(width)]
 PAIR = 4096.0
 CHUNKS = 4
-GROUP = 4
 VMEM = pltpu.VMEM
 
 
@@ -62,7 +62,7 @@
     return (i == tiles * (j % 128) + j // 128).astype(jnp.float32).astype(jnp.bfloat16)
 
 
-def pack_kernel(natural, arrays, z_even, z_odd, y_odd, d_even, d_odd):
+def pack_kernel(natural, arrays, z_even, z_odd, y_even, y_odd, d_even, d_odd):
     cols = natural.shape[-1]
     flat = natural[...].reshape(-1, cols).astype(jnp.float32).astype(jnp.bfloat16)
     turned = jnp.dot(flat, interleave(cols), preferred_element_type=jnp.float32)
@@ -76,7 +76,8 @@
         for n, (a, i) in enumerate(Z_PLANES):
             out[n] = arrays[a, up * (depth - Z_WIDTHS[a]) + i]
     planes = [(arrays, a, p) for a in range(4) for p in range(depth)]
-    tile_pairs(planes, y_ups[1], y_odd)
+    for up, out in zip(y_ups, (y_even, y_odd)):
+        tile_pairs(planes, up, out)
     for up, out in zip(z_ups, (d_even, d_odd)):
         corners = [(arrays, a, up * (depth - CORNER_WIDTHS[a]) + i) for a, i in CORNERS]
         tile_pairs(corners, y_ups[1], out)
@@ -84,19 +85,19 @@
 
 def pack(arrays):
     _, depth, rows, cols = arrays.shape
-    sizes = [(len(Z_PLANES), rows)] * 2 + [(2 * depth, 8)] + [(len(CORNERS) // 2 + 1, 8)] * 2
+    sizes = [(len(Z_PLANES), rows)] * 2 + [(2 * depth, 8)] * 2 + [(len(CORNERS) // 2 + 1, 8)] * 2
     return pl.pallas_call(
         pack_kernel,
         out_shape=[jax.ShapeDtypeStruct(arrays.shape, jnp.float32)]
         + [jax.ShapeDtypeStruct((*size, cols), jnp.float32) for size in sizes],
         in_specs=[pl.BlockSpec(memory_space=VMEM)],
-        out_specs=[pl.BlockSpec(memory_space=VMEM)] * 6,
+        out_specs=[pl.BlockSpec(memory_space=VMEM)] * 7,
         compiler_params=pltpu.CompilerParams(vmem_limit_bytes=16 * 2**20),
     )(arrays)
 
 
 def relay_kernel(
-    arrays, z_even, z_odd, y_odd, d_even, d_odd, before, after, ring, d_before, d_after, relay
+    z_even, z_odd, y_odd, d_even, d_odd, before, after, d_before, d_after, relay
 ):
     z_is_even = lax.axis_index("gz") % 2 == 0
     y_is_odd = lax.axis_index("gy") % 2
@@ -104,7 +105,7 @@
         e, o = z_even[n], z_odd[n]
         before[n] = jnp.where(z_is_even, o, e)
         after[n] = jnp.where(z_is_even, e, o)
-    sources = [(arrays, a, p) for a in range(4) for p in range(arrays.shape[1])]
+    sources = []
     for a, i in CORNERS:
         n = Z_PLANES.index((a, 0))
         sources += [(before, n + Z_WIDTHS[a] - CORNER_WIDTHS[a] + i), (after, n + i)]
@@ -115,42 +116,30 @@
         if n + 1 < out.shape[0]:
             out[n + 1] = pltpu.roll(pair, 4, 0)
 
-    for k in range(y_odd.shape[0]):
-        unpack(ring, 2 * k, y_odd[k])
     for k in range(d_even.shape[0]):
         e, o = d_even[k], d_odd[k]
         unpack(d_before, 2 * k, jnp.where(z_is_even, o, e))
         unpack(d_after, 2 * k, jnp.where(z_is_even, e, o))
 
 
-def relayed(arrays, z_even, z_odd, y_odd, d_even, d_odd):
+def relayed(z_even, z_odd, y_odd, d_even, d_odd):
     cols = z_even.shape[2]
-    own = 2 * y_odd.shape[0]
-    shapes = [z_even.shape] * 2 + [
-        (n, 8, cols) for n in (own, len(CORNERS), len(CORNERS), own // 2 + len(CORNERS))
-    ]
+    shapes = [z_even.shape] * 2 + [(len(CORNERS), 8, cols)] * 3
     return pl.pallas_call(
         relay_kernel,
         out_shape=[jax.ShapeDtypeStruct(shape, jnp.float32) for shape in shapes],
-        in_specs=[pl.BlockSpec(memory_space=VMEM)] * 6,
-        out_specs=[pl.BlockSpec(memory_space=VMEM)] * 6,
+        in_specs=[pl.BlockSpec(memory_space=VMEM)] * 5,
+        out_specs=[pl.BlockSpec(memory_space=VMEM)] * 5,
         compiler_params=pltpu.CompilerParams(vmem_limit_bytes=16 * 2**20),
-    )(arrays, z_even, z_odd, y_odd, d_even, d_odd)
-
-
-def krylov_kernel(
-    counts, arrays, before, after, ring_odd, d_before, d_after, relay,
-    fields, moments,
-    m_pad, w_pad, free, b_pad, v1, v2, acc, sums,
-):
+    )(z_even, z_odd, y_odd, d_even, d_odd)
+
+
+def krylov_steps(counts, depth, rows, cols, m_pad, w_pad, free, b_pad, v1, v2, acc, fields, loops):
     _, nz, ny = counts
     zi, yi = lax.axis_index("gz"), lax.axis_index("gy")
-    _, depth, rows, cols = arrays.shape
-    z_is_even, y_is_even = zi % 2 == 0, yi % 2 == 0
     wide = rows + 8
     f32 = jnp.float32
     ring_row = lax.broadcasted_iota(jnp.int32, (8, cols), 0)
-    half = ring_row < 4
     own = slice(0, rows)
     ring = slice(rows, wide)
 
@@ -165,40 +154,19 @@
         else:
             w_pad[a - 1, plane, where, :] = values
 
-    for a in range(4):
-        for p in range(depth):
-            put(a, LO + p, own, arrays[a, p])
-    for n, (a, i) in enumerate(Z_PLANES):
-        put(a, LO + depth + i, own, after[n])
-        if LO - Z_WIDTHS[a] + i >= 0:
-            put(a, LO - Z_WIDTHS[a] + i, own, before[n])
-
-    from_even = half == y_is_even
-    for k in range(2 * depth):
-        pair = relay[k]
-        for j, tile_even in enumerate((pair, pltpu.roll(pair, 4, 0))):
-            a, p = divmod(2 * k + j, depth)
-            put(a, LO + p, ring, jnp.where(from_even, tile_even, ring_odd[2 * k + j]))
-    for n, (a, i) in enumerate(CORNERS):
-        pair = relay[2 * depth + n]
-        put(a, LO - CORNER_WIDTHS[a] + i, ring, jnp.where(from_even, pair, d_before[n]))
-        put(a, LO + depth + i, ring, jnp.where(from_even, pltpu.roll(pair, 4, 0), d_after[n]))
-    zero_tile = jnp.zeros((8, cols), f32)
-    put(0, LO + depth + 3, ring, zero_tile)
-    put(3, LO + depth + 2, ring, zero_tile)
-    put(3, 0, ring, zero_tile)
-
-    w_pad[0, LO + depth - 1] = jnp.where(zi == nz - 1, 0.0, w_pad[0, LO + depth - 1])
-    w_pad[0, LO - 1] = jnp.where(zi == 0, 0.0, w_pad[0, LO - 1])
-    x_end = slice(cols - 128, cols)
-    last_x = lax.broadcasted_iota(jnp.int32, (wide, 128), 1) == 127
-    at_end = (yi == ny - 1) & (ring_row == 7)
-    at_start = (yi == 0) & (ring_row == 7)
-    for p in range(LO + depth + 3):
-        here = slice(rows - 8, rows)
-        w_pad[1, p, here, :] = jnp.where(at_end, 0.0, w_pad[1, p, here, :])
-        w_pad[1, p, ring, :] = jnp.where(at_start, 0.0, w_pad[1, p, ring, :])
-        w_pad[2, p, :, x_end] = jnp.where(last_x, 0.0, w_pad[2, p, :, x_end])
+    def cut_edges(planes):
+        for p, at_rim in ((LO + depth - 1, zi == nz - 1), (LO - 1, zi == 0)):
+            if p in planes:
+                w_pad[0, p] = jnp.where(at_rim, 0.0, w_pad[0, p])
+        x_end = slice(cols - 128, cols)
+        last_x = lax.broadcasted_iota(jnp.int32, (wide, 128), 1) == 127
+        at_end = (yi == ny - 1) & (ring_row == 7)
+        at_start = (yi == 0) & (ring_row == 7)
+        for p in planes:
+            here = slice(rows - 8, rows)
+            w_pad[1, p, here, :] = jnp.where(at_end, 0.0, w_pad[1, p, here, :])
+            w_pad[1, p, ring, :] = jnp.where(at_start, 0.0, w_pad[1, p, ring, :])
+            w_pad[2, p, :, x_end] = jnp.where(last_x, 0.0, w_pad[2, p, :, x_end])
 
     lanes = [slice(l, l + 128) for l in range(0, cols, 128)]
     lane = lax.broadcasted_iota(jnp.int32, (8, 128), 1)
@@ -240,57 +208,49 @@
     def times(x, y):
         return each(lambda a, b: a * b, x, y)
 
-    def in_groups(first, end, body):
-        steps, rest = divmod(end - first, GROUP)
-
-        def step(i, _):
-            body(first + GROUP * i, GROUP)
-            return 0
-
-        lax.fori_loop(0, steps, step, 0)
-        if rest:
-            body(end - rest, rest)
-
-    def prepare(start, count):
-        for h in range(2):
-            m = [plane(m_pad, h, start + j) for j in (-1, 0)]
-            from_behind = times(plane(w_pad, 0, start - 1), m[0])
-            here = m[1]
-            for j in range(count):
-                p = start + j
-                ahead = plane(m_pad, h, p + 1)
-                w_z, w_y, w_x = (plane(w_pad, i, p) for i in range(3))
-                sums_ = each(
-                    lambda a, b, c, d, e, f: (a + b) + (c + d) + (e + f),
-                    times(w_z, ahead), from_behind,
-                    times(w_y, next_y(here)), prev_y(times(w_y, here)),
-                    times(w_x, next_x(here)), prev_x(times(w_x, here)),
-                )
-                if h == 0:
-                    other = plane(m_pad, 1, p)
+    def repeated(count, body):
+        if loops:
+            lax.fori_loop(0, count, body, 0)
+        else:
+            for n in range(count):
+                body(n, 0)
+
+    def prepare(*ranges):
+        def body(h, _):
+            for start, count in ranges:
+                here = plane(m_pad, h, start)
+                from_behind = times(plane(w_pad, 0, start - 1), plane(m_pad, h, start - 1))
+                for p in range(start, start + count):
+                    ahead = plane(m_pad, h, p + 1)
+                    w_z, w_y, w_x = (plane(w_pad, i, p) for i in range(3))
+                    sums_ = each(
+                        lambda a, b, c, d, e, f: (a + b) + (c + d) + (e + f),
+                        times(w_z, ahead), from_behind,
+                        times(w_y, next_y(here)), prev_y(times(w_y, here)),
+                        times(w_x, next_x(here)), prev_x(times(w_x, here)),
+                    )
+                    other = plane(m_pad, 1 - h, p)
                     u = each(lambda a, b: jnp.where(a + b == 0.0, 1.0, 0.0), here, other)
                     store_plane(free, (p,), u)
-                else:
-                    u = plane(free, p)
-                sums_ = times(sums_, u)
-                second = each(lambda x: jnp.floor(x * (1.0 / PAIR)), sums_)
-                store_plane(b_pad, (2 * h, p), each(lambda x, y: x - PAIR * y, sums_, second))
-                store_plane(b_pad, (2 * h + 1, p), second)
-                from_behind = times(w_z, here)
-                here = ahead
-
-    in_groups(1, LO + depth + 3, prepare)
+                    sums_ = times(sums_, u)
+                    second = each(lambda x: jnp.floor(x * (1.0 / PAIR)), sums_)
+                    store_plane(b_pad, (2 * h, p), each(lambda x, y: x - PAIR * y, sums_, second))
+                    store_plane(b_pad, (2 * h + 1, p), second)
+                    from_behind = times(w_z, here)
+                    here = ahead
+            return 0
+
+        repeated(2, body)
 
     def flow(w, x, y):
         return each(lambda a, b, c: a * (b - c), w, x, y)
 
-    def apply(source, target):
-        def body(start, count):
-            for c in range(LABELS):
+    def apply(source, target, *ranges):
+        def body(c, _):
+            for start, count in ranges:
                 here = plane(source, c, start)
                 from_behind = flow(plane(w_pad, 0, start - 1), here, plane(source, c, start - 1))
-                for j in range(count):
-                    p = start + j
+                for p in range(start, start + count):
                     ahead = plane(source, c, p + 1)
                     f_z = flow(plane(w_pad, 0, p), ahead, here)
                     f_y = flow(plane(w_pad, 1, p), next_y(here), here)
@@ -300,10 +260,9 @@
                         plane(free, p), from_behind, f_z, prev_y(f_y), f_y, prev_x(f_x), f_x,
                     ))
                     from_behind, here = f_z, ahead
-        return body
-
-    in_groups(2, LO + depth + 2, apply(b_pad, v1))
-    in_groups(3, LO + depth + 1, apply(v1, v2))
+            return 0
+
+        repeated(LABELS, body)
 
     half_pairs = [(a, b) for a in range(LABELS) for b in range(a, LABELS)]
     all_pairs = [(a, b) for a in range(LABELS) for b in range(LABELS)]
@@ -334,8 +293,9 @@
                 for part, product in zip(parts, products):
                     part.append(product)
             for c in range(LABELS):
-                store(fields, (0, c, p - LO), r, bs[c])
-                store(fields, (1, c, p - LO), r, abs_[c])
+                if fields is not None:
+                    store(fields, (0, c, p - LO), r, bs[c])
+                    store(fields, (1, c, p - LO), r, abs_[c])
         add_up(0, parts)
         return 0
 
@@ -365,15 +325,115 @@
                 for part, product in zip(parts, products):
                     part.append(product)
             for c in range(LABELS):
-                store(fields, (2, c, p - LO), r, aabs_[c][t])
+                if fields is not None:
+                    store(fields, (2, c, p - LO), r, aabs_[c][t])
         add_up(30, parts)
         return 0
 
-    zero = jnp.zeros((8, 128), f32)
+    return types.SimpleNamespace(
+        put=put, cut_edges=cut_edges, prepare=prepare,
+        first=functools.partial(apply, b_pad, v1), second=functools.partial(apply, v1, v2), accumulate=accumulate, accumulate_last=accumulate_last,
+        half_pairs=half_pairs, all_pairs=all_pairs, own=own, ring=ring,
+    )
+
+
+def unpacked(even, odd, y_is_even):
+    half = lax.broadcasted_iota(jnp.int32, even.shape, 0) < 4
+    from_even = half == y_is_even
+    return jnp.where(from_even, even, odd), pltpu.roll(jnp.where(from_even, odd, even), 4, 0)
+
+
+def inner_kernel(
+    counts, arrays, y_even, y_odd, m_pad, w_pad, free, b_pad, v1, v2, acc
+):
+    _, depth, rows, cols = arrays.shape
+    y_is_even = lax.axis_index("gy") % 2 == 0
+    do = krylov_steps(counts, depth, rows, cols, m_pad, w_pad, free, b_pad, v1, v2, acc, None, False)
+    for a in range(4):
+        for p in range(depth):
+            do.put(a, LO + p, do.own, arrays[a, p])
+    for k in range(2 * depth):
+        for j, x in enumerate(unpacked(y_even[k], y_odd[k], y_is_even)):
+            a, p = divmod(2 * k + j, depth)
+            do.put(a, LO + p, do.ring, x)
+    do.cut_edges(range(LO, LO + depth))
+    do.prepare((LO + 1, depth - 2))
+    do.first((LO + 2, depth - 4))
+    do.second((LO + 3, depth - 6))
     for n in range(66):
-        acc[n] = zero
-    lax.fori_loop(LO, LO + depth, accumulate, 0)
-    lax.fori_loop(LO, LO + depth, accumulate_last, 0)
+        acc[n] = jnp.zeros((8, 128), jnp.float32)
+    lax.fori_loop(LO + 2, LO + depth - 2, do.accumulate, 0)
+    lax.fori_loop(LO + 3, LO + depth - 4, do.accumulate_last, 0)
+
+
+def padded_shapes(depth, rows, cols):
+    planes, wide = depth + LO + HI, rows + 8
+    sizes = [(2,), (3,), (), (LABELS,), (LABELS,), (LABELS,)]
+    return [(*size, planes, wide, cols) for size in sizes] + [(66, 8, 128)]
+
+
+def inner(counts, arrays, y_even, y_odd):
+    _, depth, rows, cols = arrays.shape
+    f32 = jnp.float32
+    return pl.pallas_call(
+        functools.partial(inner_kernel, counts),
+        out_shape=[jax.ShapeDtypeStruct(x, f32) for x in padded_shapes(depth, rows, cols)],
+        in_specs=[pl.BlockSpec(memory_space=VMEM)] * 3,
+        out_specs=[pl.BlockSpec(memory_space=VMEM)] * 7,
+        cost_estimate=pl.CostEstimate(flops=10**7, bytes_accessed=10**6, transcendentals=0),
+        compiler_params=pltpu.CompilerParams(vmem_limit_bytes=20 * 2**20),
+    )(arrays, y_even, y_odd)
+
+
+def outer_kernel(
+    counts, before, after, d_before, d_after, relay,
+    m_in, w_in, free_in, b_in, v1_in, v2_in, acc_in,
+    fields, moments,
+    m_pad, w_pad, free, b_pad, v1, v2, acc, sums,
+):
+    depth, rows, cols = fields.shape[2:]
+    f32 = jnp.float32
+    y_is_even = lax.axis_index("gy") % 2 == 0
+    do = krylov_steps(counts, depth, rows, cols, m_pad, w_pad, free, b_pad, v1, v2, acc, fields, True)
+    for n, (a, i) in enumerate(Z_PLANES):
+        do.put(a, LO + depth + i, do.own, after[n])
+        if LO - Z_WIDTHS[a] + i >= 0:
+            do.put(a, LO - Z_WIDTHS[a] + i, do.own, before[n])
+    for n, (a, i) in enumerate(CORNERS):
+        even = relay[n]
+        even_after = pltpu.roll(even, 4, 0)
+        do.put(a, LO - CORNER_WIDTHS[a] + i, do.ring, unpacked(even, d_before[n], y_is_even)[0])
+        do.put(a, LO + depth + i, do.ring, unpacked(even_after, d_after[n], y_is_even)[0])
+    zero_tile = jnp.zeros((8, cols), f32)
+    do.put(0, LO + depth + 3, do.ring, zero_tile)
+    do.put(3, LO + depth + 2, do.ring, zero_tile)
+    do.put(3, 0, do.ring, zero_tile)
+    low, high = LO, LO + depth
+    for source, target, planes in (
+        (m_in, m_pad, (low, low + 1, high - 2, high - 1)),
+        (w_in, w_pad, range(low, high)),
+        (b_in, b_pad, (low + 1, low + 2, high - 3, high - 2)),
+        (v1_in, v1, (low + 2, low + 3, high - 4, high - 3)),
+        (v2_in, v2, (low + 3, high - 4)),
+    ):
+        for p in planes:
+            for c in range(source.shape[0]):
+                target[c, p] = source[c, p]
+    for p in (low + 1, low + 2, high - 3, high - 2):
+        free[p] = free_in[p]
+    for n in range(66):
+        acc[n] = acc_in[n]
+    do.cut_edges([p for p in range(high + 3) if p not in range(low, high)])
+
+    do.prepare((1, low), (high - 1, 4))
+    do.first((2, low), (high - 2, 4))
+    do.second((3, low), (high - 3, 4))
+    lax.fori_loop(0, 4, lambda i, x: do.accumulate(low + i + (i // 2) * (depth - 4), x), 0)
+    lax.fori_loop(
+        0, depth - 1, lambda i, x: do.accumulate_last(low + i + jnp.where(i >= 3, 1, 0), x), 0
+    )
+
+    half_pairs, all_pairs = do.half_pairs, do.all_pairs
     low, high = [acc[n] for n in range(30)], [acc[30 + n] for n in range(36)]
     kept = {}
     for k in range(5):
@@ -389,37 +449,29 @@
             for i, j in {(a, b), (b, a)}:
                 at = (2 * k + j // 2) * 8 + (j % 2) * 4 + i
                 sums[at : at + 1, :] = x
-    packed = zero
+    lane = lax.broadcasted_iota(jnp.int32, (8, 128), 1)
+    packed = jnp.zeros((8, 128), f32)
     for g in range(12):
         x = jnp.sum(sums[8 * g : 8 * g + 8, :], axis=1, keepdims=True)
         packed = jnp.where(lane == g, x, packed)
     moments[...] = packed
 
 
-def krylov(counts, arrays, halos):
-    _, depth, rows, cols = arrays.shape
-    planes, wide = depth + LO + HI, rows + 8
+def outer(counts, shape, halos, insides):
+    _, depth, rows, cols = shape
     f32 = jnp.float32
     return pl.pallas_call(
-        functools.partial(krylov_kernel, counts),
+        functools.partial(outer_kernel, counts),
         out_shape=[
             jax.ShapeDtypeStruct((3, LABELS, depth, rows, cols), f32),
             jax.ShapeDtypeStruct((8, 128), f32),
         ],
-        in_specs=[pl.BlockSpec(memory_space=VMEM)] * 7,
+        in_specs=[pl.BlockSpec(memory_space=VMEM)] * 12,
         out_specs=[pl.BlockSpec(memory_space=VMEM)] * 2,
-        scratch_shapes=[
-            VMEM((2, planes, wide, cols), f32),
-            VMEM((3, planes, wide, cols), f32),
-            VMEM((planes, wide, cols), f32),
-            VMEM((LABELS, planes, wide, cols), f32),
-            VMEM((LABELS, planes, wide, cols), f32),
-            VMEM((LABELS, planes, wide, cols), f32),
-            VMEM((66, 8, 128), f32),
-            VMEM((96, 128), f32),
-        ],
-        compiler_params=pltpu.CompilerParams(vmem_limit_bytes=48 * 2**20),
-    )(arrays, *halos)
+        scratch_shapes=[VMEM(x, f32) for x in padded_shapes(depth, rows, cols)]
+        + [VMEM((96, 128), f32)],
+        compiler_params=pltpu.CompilerParams(vmem_limit_bytes=28 * 2**20),
+    )(*halos, *insides)
 
 
 def solved(moment, sides, floor):
@@ -449,7 +501,9 @@
     return [right[k] for k in range(n)]
 
 
-def combine_kernel(mine, theirs, fields, natural, out, spread, coeffs, mixed, buffer, sems):
+def combine_kernel(
+    mine, theirs, fields, b_in, v1_in, v2_in, natural, out, spread, coeffs, mixed, buffer, sems
+):
     f32 = jnp.float32
     _, depth, rows, cols = natural.shape
     sums = mine[...] + theirs[...]
@@ -472,6 +526,13 @@
 
     back = interleave(cols, back=True)
     chunk = depth // CHUNKS
+
+    def field(k, p, cut):
+        n, c = divmod(k, LABELS)
+        inside = range(2, depth - 2) if n < 2 else range(3, depth - 4)
+        if p in inside:
+            return (b_in, v1_in, v2_in)[n][(c, LO + p) + cut]
+        return fields[(n, c, p) + cut]
 
     def combine(n):
         for first in range(0, LABELS, 2):
@@ -482,15 +543,15 @@
             for p in range(n * chunk, n * chunk + chunk):
                 for r in range(0, rows, 8):
                     for l in range(0, cols, 128):
-                        cut = (p, slice(r, r + 8), slice(l, l + 128))
-                        v = [fields[(k // LABELS, k % LABELS) + cut] for k in range(3 * LABELS)]
+                        cut = (slice(r, r + 8), slice(l, l + 128))
+                        v = [field(k, p, cut) for k in range(3 * LABELS)]
                         for c in (first, first + 1):
                             s = [v[k] * weights[k, c] for k in range(3 * LABELS)]
                             while len(s) > 1:
                                 s = [x + y for x, y in zip(s[::2], s[1::2])] + (
                                     [s[-1]] if len(s) % 2 else []
                                 )
-                            mixed[(c,) + cut] = s[0]
+                            mixed[(c, p) + cut] = s[0]
 
     def turn_back(n):
         planes = slice(n * chunk, n * chunk + chunk)
@@ -520,13 +581,13 @@
         copy.wait()
 
 
-def combined(mine, theirs, fields, natural):
+def combined(mine, theirs, fields, insides, natural):
     _, depth, rows, cols = natural.shape
     f32 = jnp.float32
     return pl.pallas_call(
         combine_kernel,
         out_shape=jax.ShapeDtypeStruct((LABELS, depth, rows, cols), f32),
-        in_specs=[pl.BlockSpec(memory_space=VMEM)] * 4,
+        in_specs=[pl.BlockSpec(memory_space=VMEM)] * 7,
         out_specs=pl.BlockSpec(memory_space=pltpu.HBM),
         scratch_shapes=[
             VMEM((12, 8, 128), f32),
@@ -536,7 +597,7 @@
             pltpu.SemaphoreType.DMA((CHUNKS,)),
         ],
         compiler_params=pltpu.CompilerParams(vmem_limit_bytes=32 * 2**20),
-    )(mine, theirs, fields, natural)
+    )(mine, theirs, fields, *insides, natural)
 
 
 def per_device(counts, tags, depth_affinity, row_affinity, column_affinity):
@@ -555,13 +616,15 @@
             return pz(z) if pz else z, py(y) if py else y
         return exchanged(array, axes, counts, pair)
 
-    arrays, z_even, z_odd, y_odd, d_even, d_odd = pack(natural)
-    *sorted_halos, relay = relayed(
-        arrays, swap(z_even, ze, None), swap(z_odd, zo, None), swap(y_odd, None, yo),
-        swap(d_even, ze, yo), swap(d_odd, zo, yo),
+    arrays, z_even, z_odd, y_even, y_odd, d_even, d_odd = pack(natural)
+    y_odd = swap(y_odd, None, yo)
+    insides = inner(counts, arrays, swap(y_even, None, ye), y_odd)
+    *halos, relay = relayed(
+        swap(z_even, ze, None), swap(z_odd, zo, None), y_odd, swap(d_even, ze, yo),
+        swap(d_odd, zo, yo),
     )
-    halos = [*sorted_halos, swap(relay, None, ye)]
-    fields, moments = krylov(counts, arrays, halos)
+    halos = [*halos, swap(relay, None, ye)]
+    fields, moments = outer(counts, arrays.shape, halos, insides)
 
     steps = [lambda z, y: (z, y ^ 1)]
     steps += [lambda z, y, d=d: (z, y ^ d ^ 1) for d in powers(ny)[1:]]
@@ -570,7 +633,7 @@
         theirs = exchanged(moments, axes, counts, pair)
         if n < len(steps) - 1:
             moments = moments + theirs
-    return combined(moments, theirs, fields, natural)
+    return combined(moments, theirs, fields, insides[3:6], natural)
 
 
 def powers(count):

time: 35.2 us -> 33.9 us (0.963)
  waiting for transfers between devices: 11.3 us -> 9.17 us
  starting transfers between devices: 14.9 us -> 15.5 us
    ppermute x10 -> x11, waiting for transfers between devices: 11.3 us -> 9.17 us  [exchanged(): return lax.ppermute(array, axes, route)]
    ppermute x10 -> x11, starting transfers between devices: 14.9 us -> 15.5 us  [exchanged(): return lax.ppermute(array, axes, route)]
    pallas_call x1 -> x2, Pallas kernels: 4.49 us -> 4.74 us  [the longest x1 3.42 us: outer(): pl.pallas_call(functools.partial(outer_kernel, counts), out_shape=[jax.Sh...]
  transfers between devices with their start and end apart: 10 -> 11, of which waited for: 7 -> 6; matrix products, arithmetic and copies ran while one was open for 0% -> 0% of each run, Pallas kernels for 0% -> 4%
where the time goes in v5:
time: 33.9 us; the launch traced here: 33.7 us
  starting transfers between devices  15.5 us (46%)
  waiting for transfers between devices  9.17 us (27%)
  Pallas kernels  7.77 us (23%)
  other arithmetic  1.29 us (4%)
    ppermute x11, starting transfers between devices, exchanged(): return lax.ppermute(array, axes, route)  15.5 us
    ppermute x11, waiting for transfers between devices, exchanged(): return lax.ppermute(array, axes, route)  9.17 us
    pallas_call x1, Pallas kernels, outer(): pl.pallas_call(functools.partial(outer_kernel, counts), out_shape=[jax.Sh...  3.42 us
    pallas_call x1, Pallas kernels, combined(): pl.pallas_call(combine_kernel, out_shape=jax.ShapeDtypeStruct((LABELS, de...  2.34 us
    pallas_call x1, Pallas kernels, inner(): pl.pallas_call(functools.partial(inner_kernel, counts), out_shape=[jax.Sh...  1.32 us
    another operation x1, other arithmetic, per_device(): natural = jnp.stack([tags, depth_affinity, row_affinity, column_affinity])  1.28 us
  transfers between devices with their start and end apart: 11, of which 6 were waited for; matrix products, arithmetic and copies ran while one was open for 0% of the time, Pallas kernels for 4%

profile of v5, /device:TPU:0, one launch (start us, length us, event | category | flops | bytes accessed | tf_op | source)
XLA Modules:
  0.0 33.7 jit_solution(15437237789382472885)
XLA Ops:
  0.0 1.3 %pad_add_fusion.natural = s32[4,8,16,384]{3,2,1,0:T(8,128)S(1)} fusion(s32[1,8,16,384]{3,2,1,0:T(8,128)} %bitcast.4, s32[1,8,16,384]{3,2,1,0:T(8,128)} %bitcast.5, s32[1,8,16,384]{3,2,1,0:T(8,128)} %bitcast.6, s32[1,8,16,384]{3,2,1,0:T(8,128)} %bitcast.7), kind=kLoop, calls=%fused_computation | loop fusion | flops 589824 | bytes 1572864 | tf_op jit(solution)/shard_map/stack | solution.py:605
  1.3 0.6 %shard_map.46 = (f32[4,8,16,384]{3,2,1,0:T(8,128)S(1)}, f32[13,16,384]{2,1,0:T(8,128)S(1)}, f32[13,16,384]{2,1,0:T(8,128)S(1)}, f32[16,8,384]{2,1,0:T(8,128)S(1)...) custom-call(s32[4,8,16,384]{3,2,1,0:T(8,128)S(1)} %pad_add_fusion.natural), custom_call_target="tpu_custom_call" | custom-call | tf_op jit(solution)/shard_map/pallas_call | solution.py:89
  1.9 3.1 %collective-permute-start = (f32[13,16,384]{2,1,0:T(8,128)S(1)}, f32[13,16,384]{2,1,0:T(8,128)S(1)}, u32[]{:S(2)}, u32[]{:S(2)}) collective-permute-start(f32[13,16,384]{2,1,0:T(8,128)S(1)} %get-tuple-element.26), channel_id=1, source_target_pairs={{0,4},{1,5},{2,6},{3,7},{4,0},{5,1},{6,2},{7,3},{8,12},{9,13},{10,... | collective-permute-start | bytes 958472 | tf_op jit(solution)/shard_map/ppermute | solution.py:44
  5.0 0.0 collective-permute-start.1
  5.0 1.5 %collective-permute-start.2 = (f32[16,8,384]{2,1,0:T(8,128)S(1)}, f32[16,8,384]{2,1,0:T(8,128)S(1)}, u32[]{:S(2)}, u32[]{:S(2)}) collective-permute-start(f32[16,8,384]{2,1,0:T(8,128)S(1)} %get-tuple-element.28), channel_id=1, source_target_pairs={{0,16},{1,2},{2,1},{3,19},{4,20},{5,6},{6,5},{7,23},{8,24},{9,10},... | collective-permute-start | bytes 589832 | tf_op jit(solution)/shard_map/ppermute | solution.py:44
  6.5 0.5 %collective-permute-start.3 = (f32[6,8,384]{2,1,0:T(8,128)S(1)}, f32[6,8,384]{2,1,0:T(8,128)S(1)}, u32[]{:S(2)}, u32[]{:S(2)}) collective-permute-start(f32[6,8,384]{2,1,0:T(8,128)S(1)} %get-tuple-element.29), channel_id=1, source_target_pairs={{0,16},{1,6},{2,5},{3,19},{4,20},{5,2},{6,1},{7,23},{8,24},{9,14},... | collective-permute-start | bytes 221192 | tf_op jit(solution)/shard_map/ppermute | solution.py:44
  7.0 2.2 %collective-permute-start.4 = (f32[6,8,384]{2,1,0:T(8,128)S(1)}, f32[6,8,384]{2,1,0:T(8,128)S(1)}, u32[]{:S(2)}, u32[]{:S(2)}) collective-permute-start(f32[6,8,384]{2,1,0:T(8,128)S(1)} %get-tuple-element.30), channel_id=1, source_target_pairs={{0,1},{1,0},{2,3},{3,2},{4,20},{5,10},{6,9},{7,23},{8,24},{9,6},{1... | collective-permute-start | bytes 221192 | tf_op jit(solution)/shard_map/ppermute | solution.py:44
  9.2 2.3 %collective-permute-done.3.d_even = f32[6,8,384]{2,1,0:T(8,128)S(1)} collective-permute-done((f32[6,8,384]{2,1,0:T(8,128)S(1)}, f32[6,8,384]{2,1,0:T(8,128)S(1)}, u32[]{:S(2)}, u32[]{:S(2)}) %collective-permute-start.3) | collective-permute-done | bytes 73760 | tf_op jit(solution)/shard_map/ppermute | solution.py:44
  11.4 2.8 %collective-permute-start.6 = (f32[16,8,384]{2,1,0:T(8,128)S(1)}, f32[16,8,384]{2,1,0:T(8,128)S(1)}, u32[]{:S(2)}, u32[]{:S(2)}) collective-permute-start(f32[16,8,384]{2,1,0:T(8,128)S(1)} %get-tuple-element.37), channel_id=1, source_target_pairs={{0,1},{1,0},{2,3},{3,2},{4,5},{5,4},{6,7},{7,6},{8,9},{9,8},{10,11... | collective-permute-start | bytes 589832 | tf_op jit(solution)/shard_map/ppermute | solution.py:44
  14.2 0.0 collective-permute-done.4.d_odd
  14.2 0.1 shard_map.47
  14.3 0.1 collective-permute-start.5
  14.4 0.9 %collective-permute-done.6.y_even = f32[16,8,384]{2,1,0:T(8,128)S(1)} collective-permute-done((f32[16,8,384]{2,1,0:T(8,128)S(1)}, f32[16,8,384]{2,1,0:T(8,128)S(1)}, u32[]{:S(2)}, u32[]{:S(2)}) %collective-permute-start.6) | collective-permute-done | bytes 196640 | tf_op jit(solution)/shard_map/ppermute | solution.py:44
  15.3 1.3 %shard_map.48 = (f32[2,15,24,384]{3,2,1,0:T(8,128)S(1)}, f32[3,15,24,384]{3,2,1,0:T(8,128)S(1)}, f32[15,24,384]{2,1,0:T(8,128)S(1)}, f32[4,15,24,384]{3,2,1,0:T(...) custom-call(f32[4,8,16,384]{3,2,1,0:T(8,128)S(1)} %get-tuple-element.36.arrays, ...), custom_call_target="tpu_custom_call" | custom-call | flops 10000000 | bytes 1000000 | tf_op jit(solution)/shard_map/pallas_call | solution.py:378
  16.6 3.4 %shard_map.49 = (f32[3,4,8,16,384]{4,3,2,1,0:T(8,128)S(1)}, f32[8,128]{1,0:T(8,128)S(1)}) custom-call(f32[13,16,384]{2,1,0:T(8,128)S(1)} %get-tuple-element.31.before, f32[13,16,384]{2,1,0:T(8,128)S(1)} %get-tuple-element.32.after, f32[11,8,384]{2,1,0:T(8,128)S(1)} %get-tuple-element.33.d_before, f32[11,8,384]{2,1,0:T(8,128)S(1)} %get-tuple-element.34.d_after, ...), custom_call_target="tpu_custom_call" | custom-call | tf_op jit(solution)/shard_map/pallas_call | solution.py:463
  20.0 0.4 %collective-permute-start.7 = (f32[8,128]{1,0:T(8,128)S(1)}, f32[8,128]{1,0:T(8,128)S(1)}, u32[]{:S(2)}, u32[]{:S(2)}) collective-permute-start(f32[8,128]{1,0:T(8,128)S(1)} %get-tuple-element.45), channel_id=1, source_target_pairs={{0,1},{1,0},{2,3},{3,2},{4,5},{5,4},{6,7},{7,6},{8,9},{9,8},{10,11... | collective-permute-start | bytes 12296 | tf_op jit(solution)/shard_map/ppermute | solution.py:44
  20.4 0.8 %collective-permute-done.7 = f32[8,128]{1,0:T(8,128)S(1)} collective-permute-done((f32[8,128]{1,0:T(8,128)S(1)}, f32[8,128]{1,0:T(8,128)S(1)}, u32[]{:S(2)}, u32[]{:S(2)}) %collective-permute-start.7) | collective-permute-done | bytes 4128 | tf_op jit(solution)/shard_map/ppermute | solution.py:44
  21.3 0.6 %collective-permute-start.8 = (f32[8,128]{1,0:T(8,128)S(1)}, f32[8,128]{1,0:T(8,128)S(1)}, u32[]{:S(2)}, u32[]{:S(2)}) collective-permute-start(f32[8,128]{1,0:T(8,128)S(1)} %add.9), channel_id=1, source_target_pairs={{0,3},{1,2},{2,1},{3,0},{4,7},{5,6},{6,5},{7,4},{8,11},{9,10},{10,... | collective-permute-start | bytes 12296 | tf_op jit(solution)/shard_map/ppermute | solution.py:44
  21.9 2.4 %collective-permute-done.8 = f32[8,128]{1,0:T(8,128)S(1)} collective-permute-done((f32[8,128]{1,0:T(8,128)S(1)}, f32[8,128]{1,0:T(8,128)S(1)}, u32[]{:S(2)}, u32[]{:S(2)}) %collective-permute-start.8) | collective-permute-done | bytes 4128 | tf_op jit(solution)/shard_map/ppermute | solution.py:44
  24.3 1.6 %collective-permute-start.9 = (f32[8,128]{1,0:T(8,128)S(1)}, f32[8,128]{1,0:T(8,128)S(1)}, u32[]{:S(2)}, u32[]{:S(2)}) collective-permute-start(f32[8,128]{1,0:T(8,128)S(1)} %add.10), channel_id=1, source_target_pairs={{0,5},{1,4},{2,7},{3,6},{4,1},{5,0},{6,3},{7,2},{8,13},{9,12},{10,... | collective-permute-start | bytes 12296 | tf_op jit(solution)/shard_map/ppermute | solution.py:44
  25.9 1.5 %collective-permute-done.9 = f32[8,128]{1,0:T(8,128)S(1)} collective-permute-done((f32[8,128]{1,0:T(8,128)S(1)}, f32[8,128]{1,0:T(8,128)S(1)}, u32[]{:S(2)}, u32[]{:S(2)}) %collective-permute-start.9) | collective-permute-done | bytes 4128 | tf_op jit(solution)/shard_map/ppermute | solution.py:44
  27.3 2.7 %collective-permute-start.10 = (f32[8,128]{1,0:T(8,128)S(1)}, f32[8,128]{1,0:T(8,128)S(1)}, u32[]{:S(2)}, u32[]{:S(2)}) collective-permute-start(f32[8,128]{1,0:T(8,128)S(1)} %add.11.mine), channel_id=1, source_target_pairs={{0,9},{1,8},{2,11},{3,10},{4,13},{5,12},{6,15},{7,14},{8,1},{9,0},... | collective-permute-start | bytes 12296 | tf_op jit(solution)/shard_map/ppermute | solution.py:44
  30.1 1.3 %collective-permute-done.10.theirs = f32[8,128]{1,0:T(8,128)S(1)} collective-permute-done((f32[8,128]{1,0:T(8,128)S(1)}, f32[8,128]{1,0:T(8,128)S(1)}, u32[]{:S(2)}, u32[]{:S(2)}) %collective-permute-start.10) | collective-permute-done | bytes 4128 | tf_op jit(solution)/shard_map/ppermute | solution.py:44
  31.4 2.3 %shard_map.50 = f32[4,8,16,384]{3,2,1,0:T(8,128)} custom-call(f32[8,128]{1,0:T(8,128)S(1)} %add.11.mine, f32[8,128]{1,0:T(8,128)S(1)} %collective-permute-done.10.theirs, f32[3,4,8,16,384]{4,3,2,1,0:T(8,128)S(1)} %get-tuple-element.46.fields, f32[4,15,24,384]{3,2,1,0:T(8,128)S(1)} %get-tuple-element.41.b_in, f32[4,15,24,384]{3,2,1,0:T(8,128)S(1)} %get-tuple-element.42.v1_in, ...), custom_call_target="tpu_custom_call" | custom-call | tf_op jit(solution)/shard_map/pallas_call | solution.py:587
  (7 shorter events, 0.0 us)
Async XLA Ops:
  1.9 12.3 %collective-permute-start = (f32[13,16,384]{2,1,0:T(8,128)S(1)}, f32[13,16,384]{2,1,0:T(8,128)S(1)}, u32[]{:S(2)}, u32[]{:S(2)}) collective-permute-start(f32[13,16,384]{2,1,0:T(8,128)S(1)} %get-tuple-element.26), channel_id=1, source_target_pairs={{0,4},{1,5},{2,6},{3,7},{4,0},{5,1},{6,2},{7,3},{8,12},{9,13},{10,... | collective-permute-start | bytes 958472 | tf_op jit(solution)/shard_map/ppermute | solution.py:44
  5.0 9.2 %collective-permute-start.1 = (f32[13,16,384]{2,1,0:T(8,128)S(1)}, f32[13,16,384]{2,1,0:T(8,128)S(1)}, u32[]{:S(2)}, u32[]{:S(2)}) collective-permute-start(f32[13,16,384]{2,1,0:T(8,128)S(1)} %get-tuple-element.27), channel_id=1, source_target_pairs={{0,1},{1,0},{2,3},{3,2},{4,8},{5,9},{6,10},{7,11},{8,4},{9,5},{10,... | collective-permute-start | bytes 958472 | tf_op jit(solution)/shard_map/ppermute | solution.py:44
  5.0 9.2 %collective-permute-start.2 = (f32[16,8,384]{2,1,0:T(8,128)S(1)}, f32[16,8,384]{2,1,0:T(8,128)S(1)}, u32[]{:S(2)}, u32[]{:S(2)}) collective-permute-start(f32[16,8,384]{2,1,0:T(8,128)S(1)} %get-tuple-element.28), channel_id=1, source_target_pairs={{0,16},{1,2},{2,1},{3,19},{4,20},{5,6},{6,5},{7,23},{8,24},{9,10},... | collective-permute-start | bytes 589832 | tf_op jit(solution)/shard_map/ppermute | solution.py:44
  6.5 4.9 %collective-permute-start.3 = (f32[6,8,384]{2,1,0:T(8,128)S(1)}, f32[6,8,384]{2,1,0:T(8,128)S(1)}, u32[]{:S(2)}, u32[]{:S(2)}) collective-permute-start(f32[6,8,384]{2,1,0:T(8,128)S(1)} %get-tuple-element.29), channel_id=1, source_target_pairs={{0,16},{1,6},{2,5},{3,19},{4,20},{5,2},{6,1},{7,23},{8,24},{9,14},... | collective-permute-start | bytes 221192 | tf_op jit(solution)/shard_map/ppermute | solution.py:44
  7.0 7.2 %collective-permute-start.4 = (f32[6,8,384]{2,1,0:T(8,128)S(1)}, f32[6,8,384]{2,1,0:T(8,128)S(1)}, u32[]{:S(2)}, u32[]{:S(2)}) collective-permute-start(f32[6,8,384]{2,1,0:T(8,128)S(1)} %get-tuple-element.30), channel_id=1, source_target_pairs={{0,1},{1,0},{2,3},{3,2},{4,20},{5,10},{6,9},{7,23},{8,24},{9,6},{1... | collective-permute-start | bytes 221192 | tf_op jit(solution)/shard_map/ppermute | solution.py:44
  11.4 3.8 %collective-permute-start.6 = (f32[16,8,384]{2,1,0:T(8,128)S(1)}, f32[16,8,384]{2,1,0:T(8,128)S(1)}, u32[]{:S(2)}, u32[]{:S(2)}) collective-permute-start(f32[16,8,384]{2,1,0:T(8,128)S(1)} %get-tuple-element.37), channel_id=1, source_target_pairs={{0,1},{1,0},{2,3},{3,2},{4,5},{5,4},{6,7},{7,6},{8,9},{9,8},{10,11... | collective-permute-start | bytes 589832 | tf_op jit(solution)/shard_map/ppermute | solution.py:44
  14.3 2.3 %collective-permute-start.5 = (f32[11,8,384]{2,1,0:T(8,128)S(1)}, f32[11,8,384]{2,1,0:T(8,128)S(1)}, u32[]{:S(2)}, u32[]{:S(2)}) collective-permute-start(f32[11,8,384]{2,1,0:T(8,128)S(1)} %get-tuple-element.35), channel_id=1, source_target_pairs={{0,1},{1,0},{2,3},{3,2},{4,5},{5,4},{6,7},{7,6},{8,9},{9,8},{10,11... | collective-permute-start | bytes 405512 | tf_op jit(solution)/shard_map/ppermute | solution.py:44
  20.0 1.2 %collective-permute-start.7 = (f32[8,128]{1,0:T(8,128)S(1)}, f32[8,128]{1,0:T(8,128)S(1)}, u32[]{:S(2)}, u32[]{:S(2)}) collective-permute-start(f32[8,128]{1,0:T(8,128)S(1)} %get-tuple-element.45), channel_id=1, source_target_pairs={{0,1},{1,0},{2,3},{3,2},{4,5},{5,4},{6,7},{7,6},{8,9},{9,8},{10,11... | collective-permute-start | bytes 12296 | tf_op jit(solution)/shard_map/ppermute | solution.py:44
  21.3 3.0 %collective-permute-start.8 = (f32[8,128]{1,0:T(8,128)S(1)}, f32[8,128]{1,0:T(8,128)S(1)}, u32[]{:S(2)}, u32[]{:S(2)}) collective-permute-start(f32[8,128]{1,0:T(8,128)S(1)} %add.9), channel_id=1, source_target_pairs={{0,3},{1,2},{2,1},{3,0},{4,7},{5,6},{6,5},{7,4},{8,11},{9,10},{10,... | collective-permute-start | bytes 12296 | tf_op jit(solution)/shard_map/ppermute | solution.py:44
  24.3 3.0 %collective-permute-start.9 = (f32[8,128]{1,0:T(8,128)S(1)}, f32[8,128]{1,0:T(8,128)S(1)}, u32[]{:S(2)}, u32[]{:S(2)}) collective-permute-start(f32[8,128]{1,0:T(8,128)S(1)} %add.10), channel_id=1, source_target_pairs={{0,5},{1,4},{2,7},{3,6},{4,1},{5,0},{6,3},{7,2},{8,13},{9,12},{10,... | collective-permute-start | bytes 12296 | tf_op jit(solution)/shard_map/ppermute | solution.py:44
  27.3 4.1 %collective-permute-start.10 = (f32[8,128]{1,0:T(8,128)S(1)}, f32[8,128]{1,0:T(8,128)S(1)}, u32[]{:S(2)}, u32[]{:S(2)}) collective-permute-start(f32[8,128]{1,0:T(8,128)S(1)} %add.11.mine), channel_id=1, source_target_pairs={{0,9},{1,8},{2,11},{3,10},{4,13},{5,12},{6,15},{7,14},{8,1},{9,0},... | collective-permute-start | bytes 12296 | tf_op jit(solution)/shard_map/ppermute | solution.py:44

commit v6 on v5

--- a/solution.py
+++ b/solution.py
@@ -15,6 +15,10 @@
 Z_PLANES = [(a, i) for a, width in enumerate(Z_WIDTHS) for i in range(width)]
 CORNER_WIDTHS = (3, 3, 3, 2)
 CORNERS = [(a, i) for a, width in enumerate(CORNER_WIDTHS) for i in range(width)]
+SLOTS = [
+    (0, 0, 0, 1), (0, 4, 1, 1), (1, 0, 2, 1), (1, 4, 0, 2), (1, 6, 1, 2), (2, 0, 2, 2),
+    (2, 2, 3, 1), (2, 4, 0, 3), (2, 5, 1, 3), (2, 6, 2, 3), (2, 7, 3, 2),
+]
 PAIR = 4096.0
 CHUNKS = 4
 VMEM = pltpu.VMEM
@@ -60,6 +64,27 @@
     tiles = cols // 128
     i, j = (lax.broadcasted_iota(jnp.int32, (cols, cols), n) for n in ((1, 0) if back else (0, 1)))
     return (i == tiles * (j % 128) + j // 128).astype(jnp.float32).astype(jnp.bfloat16)
+
+
+def moved(tile, rows, up):
+    rows %= 8
+    if rows == 0:
+        return tile
+    return jnp.where(up == 1, pltpu.roll(tile, 8 - rows, 0), pltpu.roll(tile, rows, 0))
+
+
+def pack_corner(arrays, z_up, y_up, out):
+    _, depth, rows, cols = arrays.shape
+    row = lax.broadcasted_iota(jnp.int32, (8, cols), 0)
+    away = jnp.where(y_up == 1, 7 - row, row)
+    tile = pl.multiple_of(y_up * (rows - 8), 8)
+    packed = {}
+    for t, first, a, k in SLOTS:
+        x = arrays[a, z_up * (depth - 2 * k + 1) + k - 1, pl.ds(tile, 8), :]
+        x = moved(x, first, y_up)
+        packed[t] = jnp.where(away >= first, x, packed[t]) if first else x
+    for t, x in packed.items():
+        out[t] = x
 
 
 def pack_kernel(natural, arrays, z_even, z_odd, y_even, y_odd, d_even, d_odd):
@@ -79,13 +104,12 @@
     for up, out in zip(y_ups, (y_even, y_odd)):
         tile_pairs(planes, up, out)
     for up, out in zip(z_ups, (d_even, d_odd)):
-        corners = [(arrays, a, up * (depth - CORNER_WIDTHS[a]) + i) for a, i in CORNERS]
-        tile_pairs(corners, y_ups[1], out)
+        pack_corner(arrays, up, y_ups[1], out)
 
 
 def pack(arrays):
     _, depth, rows, cols = arrays.shape
-    sizes = [(len(Z_PLANES), rows)] * 2 + [(2 * depth, 8)] * 2 + [(len(CORNERS) // 2 + 1, 8)] * 2
+    sizes = [(len(Z_PLANES), rows)] * 2 + [(2 * depth, 8)] * 2 + [(3, 8)] * 2
     return pl.pallas_call(
         pack_kernel,
         out_shape=[jax.ShapeDtypeStruct(arrays.shape, jnp.float32)]
@@ -96,9 +120,7 @@
     )(arrays)
 
 
-def relay_kernel(
-    z_even, z_odd, y_odd, d_even, d_odd, before, after, d_before, d_after, relay
-):
+def relay_kernel(z_even, z_odd, y_odd, before, after, relay):
     z_is_even = lax.axis_index("gz") % 2 == 0
     y_is_odd = lax.axis_index("gy") % 2
     for n in range(len(Z_PLANES)):
@@ -111,27 +133,39 @@
         sources += [(before, n + Z_WIDTHS[a] - CORNER_WIDTHS[a] + i), (after, n + i)]
     tile_pairs(sources, 1 - y_is_odd, relay)
 
-    def unpack(out, n, pair):
-        out[n] = pair
-        if n + 1 < out.shape[0]:
-            out[n + 1] = pltpu.roll(pair, 4, 0)
-
-    for k in range(d_even.shape[0]):
-        e, o = d_even[k], d_odd[k]
-        unpack(d_before, 2 * k, jnp.where(z_is_even, o, e))
-        unpack(d_after, 2 * k, jnp.where(z_is_even, e, o))
-
-
-def relayed(z_even, z_odd, y_odd, d_even, d_odd):
+
+def corner_kernel(d_even, d_odd, d_before, d_after):
+    z_is_even = lax.axis_index("gz") % 2 == 0
+    y_is_odd = lax.axis_index("gy") % 2
+    for out, x, y in ((d_before, d_odd, d_even), (d_after, d_even, d_odd)):
+        tiles = [jnp.where(z_is_even, x[t], y[t]) for t in range(3)]
+        for t, first, a, k in SLOTS:
+            i = CORNER_WIDTHS[a] - k if out is d_before else k - 1
+            out[CORNERS.index((a, i))] = moved(tiles[t], -first, 1 - y_is_odd)
+
+
+def cornered(d_even, d_odd):
+    cols = d_even.shape[2]
+    return pl.pallas_call(
+        corner_kernel,
+        out_shape=[jax.ShapeDtypeStruct((len(CORNERS), 8, cols), jnp.float32)] * 2,
+        in_specs=[pl.BlockSpec(memory_space=VMEM)] * 2,
+        out_specs=[pl.BlockSpec(memory_space=VMEM)] * 2,
+        cost_estimate=pl.CostEstimate(flops=2 * 10**9, bytes_accessed=10**6, transcendentals=0),
+        compiler_params=pltpu.CompilerParams(vmem_limit_bytes=16 * 2**20),
+    )(d_even, d_odd)
+
+
+def relayed(z_even, z_odd, y_odd):
     cols = z_even.shape[2]
-    shapes = [z_even.shape] * 2 + [(len(CORNERS), 8, cols)] * 3
+    shapes = [z_even.shape] * 2 + [(len(CORNERS), 8, cols)]
     return pl.pallas_call(
         relay_kernel,
         out_shape=[jax.ShapeDtypeStruct(shape, jnp.float32) for shape in shapes],
-        in_specs=[pl.BlockSpec(memory_space=VMEM)] * 5,
-        out_specs=[pl.BlockSpec(memory_space=VMEM)] * 5,
+        in_specs=[pl.BlockSpec(memory_space=VMEM)] * 3,
+        out_specs=[pl.BlockSpec(memory_space=VMEM)] * 3,
         compiler_params=pltpu.CompilerParams(vmem_limit_bytes=16 * 2**20),
-    )(z_even, z_odd, y_odd, d_even, d_odd)
+    )(z_even, z_odd, y_odd)
 
 
 def krylov_steps(counts, depth, rows, cols, m_pad, w_pad, free, b_pad, v1, v2, acc, fields, loops):
@@ -619,11 +653,9 @@
     arrays, z_even, z_odd, y_even, y_odd, d_even, d_odd = pack(natural)
     y_odd = swap(y_odd, None, yo)
     insides = inner(counts, arrays, swap(y_even, None, ye), y_odd)
-    *halos, relay = relayed(
-        swap(z_even, ze, None), swap(z_odd, zo, None), y_odd, swap(d_even, ze, yo),
-        swap(d_odd, zo, yo),
-    )
-    halos = [*halos, swap(relay, None, ye)]
+    before, after, relay = relayed(swap(z_even, ze, None), swap(z_odd, zo, None), y_odd)
+    corners = cornered(swap(d_even, ze, yo), swap(d_odd, zo, yo))
+    halos = [before, after, *corners, swap(relay, None, ye)]
     fields, moments = outer(counts, arrays.shape, halos, insides)
 
     steps = [lambda z, y: (z, y ^ 1)]

time: 33.9 us -> 33.2 us (0.979)
  starting transfers between devices: 15.5 us -> 14.8 us
    ppermute x11, starting transfers between devices: 15.5 us -> 14.8 us  [exchanged(): return lax.ppermute(array, axes, route)]
where the time goes in v6:
time: 33.2 us; the launch traced here: 33.1 us
  starting transfers between devices  14.8 us (45%)
  waiting for transfers between devices  9.05 us (27%)
  Pallas kernels  7.79 us (23%)
  other arithmetic  1.29 us (4%)
    ppermute x11, starting transfers between devices, exchanged(): return lax.ppermute(array, axes, route)  14.8 us
    ppermute x11, waiting for transfers between devices, exchanged(): return lax.ppermute(array, axes, route)  9.05 us
    pallas_call x1, Pallas kernels, outer(): pl.pallas_call(functools.partial(outer_kernel, counts), out_shape=[jax.Sh...  3.42 us
    pallas_call x1, Pallas kernels, combined(): pl.pallas_call(combine_kernel, out_shape=jax.ShapeDtypeStruct((LABELS, de...  2.34 us
    pallas_call x1, Pallas kernels, inner(): pl.pallas_call(functools.partial(inner_kernel, counts), out_shape=[jax.Sh...  1.33 us
    another operation x1, other arithmetic, per_device(): natural = jnp.stack([tags, depth_affinity, row_affinity, column_affinity])  1.28 us
  transfers between devices with their start and end apart: 11, of which 6 were waited for; matrix products, arithmetic and copies ran while one was open for 0% of the time, Pallas kernels for 4%

profile of v6, /device:TPU:0, one launch (start us, length us, event | category | flops | bytes accessed | tf_op | source)
XLA Modules:
  0.0 33.1 jit_solution(10960372012805395348)
XLA Ops:
  0.0 1.3 %pad_add_fusion.natural = s32[4,8,16,384]{3,2,1,0:T(8,128)S(1)} fusion(s32[1,8,16,384]{3,2,1,0:T(8,128)} %bitcast.4, s32[1,8,16,384]{3,2,1,0:T(8,128)} %bitcast.5, s32[1,8,16,384]{3,2,1,0:T(8,128)} %bitcast.6, s32[1,8,16,384]{3,2,1,0:T(8,128)} %bitcast.7), kind=kLoop, calls=%fused_computation | loop fusion | flops 589824 | bytes 1572864 | tf_op jit(solution)/shard_map/stack | solution.py:639
  1.3 0.6 %shard_map.46 = (f32[4,8,16,384]{3,2,1,0:T(8,128)S(1)}, f32[13,16,384]{2,1,0:T(8,128)S(1)}, f32[13,16,384]{2,1,0:T(8,128)S(1)}, f32[16,8,384]{2,1,0:T(8,128)S(1)...) custom-call(s32[4,8,16,384]{3,2,1,0:T(8,128)S(1)} %pad_add_fusion.natural), custom_call_target="tpu_custom_call" | custom-call | tf_op jit(solution)/shard_map/pallas_call | solution.py:113
  1.9 3.1 %collective-permute-start = (f32[13,16,384]{2,1,0:T(8,128)S(1)}, f32[13,16,384]{2,1,0:T(8,128)S(1)}, u32[]{:S(2)}, u32[]{:S(2)}) collective-permute-start(f32[13,16,384]{2,1,0:T(8,128)S(1)} %get-tuple-element.26), channel_id=1, source_target_pairs={{0,4},{1,5},{2,6},{3,7},{4,0},{5,1},{6,2},{7,3},{8,12},{9,13},{10,... | collective-permute-start | bytes 958472 | tf_op jit(solution)/shard_map/ppermute | solution.py:48
  5.0 0.0 collective-permute-start.1
  5.0 1.5 %collective-permute-start.2 = (f32[16,8,384]{2,1,0:T(8,128)S(1)}, f32[16,8,384]{2,1,0:T(8,128)S(1)}, u32[]{:S(2)}, u32[]{:S(2)}) collective-permute-start(f32[16,8,384]{2,1,0:T(8,128)S(1)} %get-tuple-element.28), channel_id=1, source_target_pairs={{0,16},{1,2},{2,1},{3,19},{4,20},{5,6},{6,5},{7,23},{8,24},{9,10},... | collective-permute-start | bytes 589832 | tf_op jit(solution)/shard_map/ppermute | solution.py:48
  6.5 0.5 %collective-permute-start.3 = (f32[3,8,384]{2,1,0:T(8,128)S(1)}, f32[3,8,384]{2,1,0:T(8,128)S(1)}, u32[]{:S(2)}, u32[]{:S(2)}) collective-permute-start(f32[3,8,384]{2,1,0:T(8,128)S(1)} %get-tuple-element.31), channel_id=1, source_target_pairs={{0,16},{1,6},{2,5},{3,19},{4,20},{5,2},{6,1},{7,23},{8,24},{9,14},... | collective-permute-start | bytes 110600 | tf_op jit(solution)/shard_map/ppermute | solution.py:48
  7.0 2.2 %collective-permute-start.4 = (f32[3,8,384]{2,1,0:T(8,128)S(1)}, f32[3,8,384]{2,1,0:T(8,128)S(1)}, u32[]{:S(2)}, u32[]{:S(2)}) collective-permute-start(f32[3,8,384]{2,1,0:T(8,128)S(1)} %get-tuple-element.32), channel_id=1, source_target_pairs={{0,1},{1,0},{2,3},{3,2},{4,20},{5,10},{6,9},{7,23},{8,24},{9,6},{1... | collective-permute-start | bytes 110600 | tf_op jit(solution)/shard_map/ppermute | solution.py:48
  9.2 1.5 %collective-permute-done.2.y_odd = f32[16,8,384]{2,1,0:T(8,128)S(1)} collective-permute-done((f32[16,8,384]{2,1,0:T(8,128)S(1)}, f32[16,8,384]{2,1,0:T(8,128)S(1)}, u32[]{:S(2)}, u32[]{:S(2)}) %collective-permute-start.2) | collective-permute-done | bytes 196640 | tf_op jit(solution)/shard_map/ppermute | solution.py:48
  10.6 0.2 collective-permute-start.6
  10.9 2.0 %collective-permute-done.z_even = f32[13,16,384]{2,1,0:T(8,128)S(1)} collective-permute-done((f32[13,16,384]{2,1,0:T(8,128)S(1)}, f32[13,16,384]{2,1,0:T(8,128)S(1)}, u32[]{:S(2)}, u32[]{:S(2)}) %collective-permute-start) | collective-permute-done | bytes 319520 | tf_op jit(solution)/shard_map/ppermute | solution.py:48
  12.9 0.0 collective-permute-done.1.z_odd
  12.9 0.1 shard_map.47
  13.0 0.1 collective-permute-start.5
  13.1 1.3 %shard_map.49 = (f32[2,15,24,384]{3,2,1,0:T(8,128)S(1)}, f32[3,15,24,384]{3,2,1,0:T(8,128)S(1)}, f32[15,24,384]{2,1,0:T(8,128)S(1)}, f32[4,15,24,384]{3,2,1,0:T(...) custom-call(f32[4,8,16,384]{3,2,1,0:T(8,128)S(1)} %get-tuple-element.36.arrays, ...), custom_call_target="tpu_custom_call" | custom-call | flops 10000000 | bytes 1000000 | tf_op jit(solution)/shard_map/pallas_call | solution.py:412
  14.5 3.4 %shard_map.50 = (f32[3,4,8,16,384]{4,3,2,1,0:T(8,128)S(1)}, f32[8,128]{1,0:T(8,128)S(1)}) custom-call(f32[13,16,384]{2,1,0:T(8,128)S(1)} %get-tuple-element.29.before, f32[13,16,384]{2,1,0:T(8,128)S(1)} %get-tuple-element.30.after, f32[11,8,384]{2,1,0:T(8,128)S(1)} %get-tuple-element.33.d_before, f32[11,8,384]{2,1,0:T(8,128)S(1)} %get-tuple-element.34.d_after, ...), custom_call_target="tpu_custom_call" | custom-call | tf_op jit(solution)/shard_map/pallas_call | solution.py:497
  17.9 0.8 %collective-permute-start.7 = (f32[8,128]{1,0:T(8,128)S(1)}, f32[8,128]{1,0:T(8,128)S(1)}, u32[]{:S(2)}, u32[]{:S(2)}) collective-permute-start(f32[8,128]{1,0:T(8,128)S(1)} %get-tuple-element.45), channel_id=1, source_target_pairs={{0,1},{1,0},{2,3},{3,2},{4,5},{5,4},{6,7},{7,6},{8,9},{9,8},{10,11... | collective-permute-start | bytes 12296 | tf_op jit(solution)/shard_map/ppermute | solution.py:48
  18.7 0.8 %collective-permute-done.7 = f32[8,128]{1,0:T(8,128)S(1)} collective-permute-done((f32[8,128]{1,0:T(8,128)S(1)}, f32[8,128]{1,0:T(8,128)S(1)}, u32[]{:S(2)}, u32[]{:S(2)}) %collective-permute-start.7) | collective-permute-done | bytes 4128 | tf_op jit(solution)/shard_map/ppermute | solution.py:48
  19.5 1.0 %collective-permute-start.8 = (f32[8,128]{1,0:T(8,128)S(1)}, f32[8,128]{1,0:T(8,128)S(1)}, u32[]{:S(2)}, u32[]{:S(2)}) collective-permute-start(f32[8,128]{1,0:T(8,128)S(1)} %add.9), channel_id=1, source_target_pairs={{0,3},{1,2},{2,1},{3,0},{4,7},{5,6},{6,5},{7,4},{8,11},{9,10},{10,... | collective-permute-start | bytes 12296 | tf_op jit(solution)/shard_map/ppermute | solution.py:48
  20.5 2.1 %collective-permute-done.8 = f32[8,128]{1,0:T(8,128)S(1)} collective-permute-done((f32[8,128]{1,0:T(8,128)S(1)}, f32[8,128]{1,0:T(8,128)S(1)}, u32[]{:S(2)}, u32[]{:S(2)}) %collective-permute-start.8) | collective-permute-done | bytes 4128 | tf_op jit(solution)/shard_map/ppermute | solution.py:48
  22.5 2.6 %collective-permute-start.9 = (f32[8,128]{1,0:T(8,128)S(1)}, f32[8,128]{1,0:T(8,128)S(1)}, u32[]{:S(2)}, u32[]{:S(2)}) collective-permute-start(f32[8,128]{1,0:T(8,128)S(1)} %add.10), channel_id=1, source_target_pairs={{0,5},{1,4},{2,7},{3,6},{4,1},{5,0},{6,3},{7,2},{8,13},{9,12},{10,... | collective-permute-start | bytes 12296 | tf_op jit(solution)/shard_map/ppermute | solution.py:48
  25.2 1.3 %collective-permute-done.9 = f32[8,128]{1,0:T(8,128)S(1)} collective-permute-done((f32[8,128]{1,0:T(8,128)S(1)}, f32[8,128]{1,0:T(8,128)S(1)}, u32[]{:S(2)}, u32[]{:S(2)}) %collective-permute-start.9) | collective-permute-done | bytes 4128 | tf_op jit(solution)/shard_map/ppermute | solution.py:48
  26.5 2.9 %collective-permute-start.10 = (f32[8,128]{1,0:T(8,128)S(1)}, f32[8,128]{1,0:T(8,128)S(1)}, u32[]{:S(2)}, u32[]{:S(2)}) collective-permute-start(f32[8,128]{1,0:T(8,128)S(1)} %add.11.mine), channel_id=1, source_target_pairs={{0,9},{1,8},{2,11},{3,10},{4,13},{5,12},{6,15},{7,14},{8,1},{9,0},... | collective-permute-start | bytes 12296 | tf_op jit(solution)/shard_map/ppermute | solution.py:48
  29.4 1.3 %collective-permute-done.10.theirs = f32[8,128]{1,0:T(8,128)S(1)} collective-permute-done((f32[8,128]{1,0:T(8,128)S(1)}, f32[8,128]{1,0:T(8,128)S(1)}, u32[]{:S(2)}, u32[]{:S(2)}) %collective-permute-start.10) | collective-permute-done | bytes 4128 | tf_op jit(solution)/shard_map/ppermute | solution.py:48
  30.7 2.3 %shard_map.51 = f32[4,8,16,384]{3,2,1,0:T(8,128)} custom-call(f32[8,128]{1,0:T(8,128)S(1)} %add.11.mine, f32[8,128]{1,0:T(8,128)S(1)} %collective-permute-done.10.theirs, f32[3,4,8,16,384]{4,3,2,1,0:T(8,128)S(1)} %get-tuple-element.46.fields, f32[4,15,24,384]{3,2,1,0:T(8,128)S(1)} %get-tuple-element.41.b_in, f32[4,15,24,384]{3,2,1,0:T(8,128)S(1)} %get-tuple-element.42.v1_in, ...), custom_call_target="tpu_custom_call" | custom-call | tf_op jit(solution)/shard_map/pallas_call | solution.py:621
  (8 shorter events, 0.1 us)
Async XLA Ops:
  1.9 11.0 %collective-permute-start = (f32[13,16,384]{2,1,0:T(8,128)S(1)}, f32[13,16,384]{2,1,0:T(8,128)S(1)}, u32[]{:S(2)}, u32[]{:S(2)}) collective-permute-start(f32[13,16,384]{2,1,0:T(8,128)S(1)} %get-tuple-element.26), channel_id=1, source_target_pairs={{0,4},{1,5},{2,6},{3,7},{4,0},{5,1},{6,2},{7,3},{8,12},{9,13},{10,... | collective-permute-start | bytes 958472 | tf_op jit(solution)/shard_map/ppermute | solution.py:48
  5.0 7.9 %collective-permute-start.1 = (f32[13,16,384]{2,1,0:T(8,128)S(1)}, f32[13,16,384]{2,1,0:T(8,128)S(1)}, u32[]{:S(2)}, u32[]{:S(2)}) collective-permute-start(f32[13,16,384]{2,1,0:T(8,128)S(1)} %get-tuple-element.27), channel_id=1, source_target_pairs={{0,1},{1,0},{2,3},{3,2},{4,8},{5,9},{6,10},{7,11},{8,4},{9,5},{10,... | collective-permute-start | bytes 958472 | tf_op jit(solution)/shard_map/ppermute | solution.py:48
  5.0 5.7 %collective-permute-start.2 = (f32[16,8,384]{2,1,0:T(8,128)S(1)}, f32[16,8,384]{2,1,0:T(8,128)S(1)}, u32[]{:S(2)}, u32[]{:S(2)}) collective-permute-start(f32[16,8,384]{2,1,0:T(8,128)S(1)} %get-tuple-element.28), channel_id=1, source_target_pairs={{0,16},{1,2},{2,1},{3,19},{4,20},{5,6},{6,5},{7,23},{8,24},{9,10},... | collective-permute-start | bytes 589832 | tf_op jit(solution)/shard_map/ppermute | solution.py:48
  6.5 6.6 %collective-permute-start.3 = (f32[3,8,384]{2,1,0:T(8,128)S(1)}, f32[3,8,384]{2,1,0:T(8,128)S(1)}, u32[]{:S(2)}, u32[]{:S(2)}) collective-permute-start(f32[3,8,384]{2,1,0:T(8,128)S(1)} %get-tuple-element.31), channel_id=1, source_target_pairs={{0,16},{1,6},{2,5},{3,19},{4,20},{5,2},{6,1},{7,23},{8,24},{9,14},... | collective-permute-start | bytes 110600 | tf_op jit(solution)/shard_map/ppermute | solution.py:48
  7.0 6.1 %collective-permute-start.4 = (f32[3,8,384]{2,1,0:T(8,128)S(1)}, f32[3,8,384]{2,1,0:T(8,128)S(1)}, u32[]{:S(2)}, u32[]{:S(2)}) collective-permute-start(f32[3,8,384]{2,1,0:T(8,128)S(1)} %get-tuple-element.32), channel_id=1, source_target_pairs={{0,1},{1,0},{2,3},{3,2},{4,20},{5,10},{6,9},{7,23},{8,24},{9,6},{1... | collective-permute-start | bytes 110600 | tf_op jit(solution)/shard_map/ppermute | solution.py:48
  10.6 2.5 %collective-permute-start.6 = (f32[16,8,384]{2,1,0:T(8,128)S(1)}, f32[16,8,384]{2,1,0:T(8,128)S(1)}, u32[]{:S(2)}, u32[]{:S(2)}) collective-permute-start(f32[16,8,384]{2,1,0:T(8,128)S(1)} %get-tuple-element.37), channel_id=1, source_target_pairs={{0,1},{1,0},{2,3},{3,2},{4,5},{5,4},{6,7},{7,6},{8,9},{9,8},{10,11... | collective-permute-start | bytes 589832 | tf_op jit(solution)/shard_map/ppermute | solution.py:48
  13.0 1.5 %collective-permute-start.5 = (f32[11,8,384]{2,1,0:T(8,128)S(1)}, f32[11,8,384]{2,1,0:T(8,128)S(1)}, u32[]{:S(2)}, u32[]{:S(2)}) collective-permute-start(f32[11,8,384]{2,1,0:T(8,128)S(1)} %get-tuple-element.35), channel_id=1, source_target_pairs={{0,1},{1,0},{2,3},{3,2},{4,5},{5,4},{6,7},{7,6},{8,9},{9,8},{10,11... | collective-permute-start | bytes 405512 | tf_op jit(solution)/shard_map/ppermute | solution.py:48
  17.9 1.6 %collective-permute-start.7 = (f32[8,128]{1,0:T(8,128)S(1)}, f32[8,128]{1,0:T(8,128)S(1)}, u32[]{:S(2)}, u32[]{:S(2)}) collective-permute-start(f32[8,128]{1,0:T(8,128)S(1)} %get-tuple-element.45), channel_id=1, source_target_pairs={{0,1},{1,0},{2,3},{3,2},{4,5},{5,4},{6,7},{7,6},{8,9},{9,8},{10,11... | collective-permute-start | bytes 12296 | tf_op jit(solution)/shard_map/ppermute | solution.py:48
  19.5 3.0 %collective-permute-start.8 = (f32[8,128]{1,0:T(8,128)S(1)}, f32[8,128]{1,0:T(8,128)S(1)}, u32[]{:S(2)}, u32[]{:S(2)}) collective-permute-start(f32[8,128]{1,0:T(8,128)S(1)} %add.9), channel_id=1, source_target_pairs={{0,3},{1,2},{2,1},{3,0},{4,7},{5,6},{6,5},{7,4},{8,11},{9,10},{10,... | collective-permute-start | bytes 12296 | tf_op jit(solution)/shard_map/ppermute | solution.py:48
  22.5 4.0 %collective-permute-start.9 = (f32[8,128]{1,0:T(8,128)S(1)}, f32[8,128]{1,0:T(8,128)S(1)}, u32[]{:S(2)}, u32[]{:S(2)}) collective-permute-start(f32[8,128]{1,0:T(8,128)S(1)} %add.10), channel_id=1, source_target_pairs={{0,5},{1,4},{2,7},{3,6},{4,1},{5,0},{6,3},{7,2},{8,13},{9,12},{10,... | collective-permute-start | bytes 12296 | tf_op jit(solution)/shard_map/ppermute | solution.py:48
  26.5 4.2 %collective-permute-start.10 = (f32[8,128]{1,0:T(8,128)S(1)}, f32[8,128]{1,0:T(8,128)S(1)}, u32[]{:S(2)}, u32[]{:S(2)}) collective-permute-start(f32[8,128]{1,0:T(8,128)S(1)} %add.11.mine), channel_id=1, source_target_pairs={{0,9},{1,8},{2,11},{3,10},{4,13},{5,12},{6,15},{7,14},{8,1},{9,0},... | collective-permute-start | bytes 12296 | tf_op jit(solution)/shard_map/ppermute | solution.py:48

commit v7 on v6

--- a/solution.py
+++ b/solution.py
@@ -20,7 +20,7 @@
     (2, 2, 3, 1), (2, 4, 0, 3), (2, 5, 1, 3), (2, 6, 2, 3), (2, 7, 3, 2),
 ]
 PAIR = 4096.0
-CHUNKS = 4
+CHUNKS = 8
 VMEM = pltpu.VMEM
 
 
@@ -87,19 +87,25 @@
         out[t] = x
 
 
-def pack_kernel(natural, arrays, z_even, z_odd, y_even, y_odd, d_even, d_odd):
+def pack_kernel(natural, arrays, z_even, z_odd):
     cols = natural.shape[-1]
     flat = natural[...].reshape(-1, cols).astype(jnp.float32).astype(jnp.bfloat16)
     turned = jnp.dot(flat, interleave(cols), preferred_element_type=jnp.float32)
     turned = turned.reshape(arrays.shape)
     arrays[0] = turned[0]
     arrays[1:] = turned[1:] + 1.0
+    z_is_odd = lax.axis_index("gz") % 2
+    depth = arrays.shape[1]
+    z_ups = (1 - z_is_odd, z_is_odd)
+    for up, out in zip(z_ups, (z_even, z_odd)):
+        for n, (a, i) in enumerate(Z_PLANES):
+            out[n] = arrays[a, up * (depth - Z_WIDTHS[a]) + i]
+
+
+def pack_rest_kernel(arrays, y_even, y_odd, d_even, d_odd):
     z_is_odd, y_is_odd = lax.axis_index("gz") % 2, lax.axis_index("gy") % 2
     depth = arrays.shape[1]
     z_ups, y_ups = (1 - z_is_odd, z_is_odd), (1 - y_is_odd, y_is_odd)
-    for up, out in zip(z_ups, (z_even, z_odd)):
-        for n, (a, i) in enumerate(Z_PLANES):
-            out[n] = arrays[a, up * (depth - Z_WIDTHS[a]) + i]
     planes = [(arrays, a, p) for a in range(4) for p in range(depth)]
     for up, out in zip(y_ups, (y_even, y_odd)):
         tile_pairs(planes, up, out)
@@ -107,17 +113,23 @@
         pack_corner(arrays, up, y_ups[1], out)
 
 
-def pack(arrays):
-    _, depth, rows, cols = arrays.shape
-    sizes = [(len(Z_PLANES), rows)] * 2 + [(2 * depth, 8)] * 2 + [(3, 8)] * 2
+def packed(kernel, shapes, arrays):
     return pl.pallas_call(
-        pack_kernel,
-        out_shape=[jax.ShapeDtypeStruct(arrays.shape, jnp.float32)]
-        + [jax.ShapeDtypeStruct((*size, cols), jnp.float32) for size in sizes],
+        kernel,
+        out_shape=[jax.ShapeDtypeStruct(shape, jnp.float32) for shape in shapes],
         in_specs=[pl.BlockSpec(memory_space=VMEM)],
-        out_specs=[pl.BlockSpec(memory_space=VMEM)] * 7,
+        out_specs=[pl.BlockSpec(memory_space=VMEM)] * len(shapes),
         compiler_params=pltpu.CompilerParams(vmem_limit_bytes=16 * 2**20),
     )(arrays)
+
+
+def pack(natural):
+    _, depth, rows, cols = natural.shape
+    arrays, *z = packed(
+        pack_kernel, [natural.shape] + [(len(Z_PLANES), rows, cols)] * 2, natural
+    )
+    shapes = [(2 * depth, 8, cols)] * 2 + [(3, 8, cols)] * 2
+    return arrays, *z, *packed(pack_rest_kernel, shapes, arrays)
 
 
 def relay_kernel(z_even, z_odd, y_odd, before, after, relay):
@@ -168,7 +180,22 @@
     )(z_even, z_odd, y_odd)
 
 
-def krylov_steps(counts, depth, rows, cols, m_pad, w_pad, free, b_pad, v1, v2, acc, fields, loops):
+def krylov_steps(
+    counts, depth, rows, cols, m_pad, w_pad, free, b_pad, v1, v2, acc, fields, loops, given=None
+):
+    def at(p, ref, n, margin):
+        inside = LO + margin <= p < LO + depth - margin
+        return given[n] if given is not None and inside else ref
+
+    def m_at(p):
+        return at(p, m_pad, 0, 0)
+
+    def w_at(p):
+        return at(p, w_pad, 1, 0)
+
+    def free_at(p):
+        return at(p, free, 2, 1)
+
     _, nz, ny = counts
     zi, yi = lax.axis_index("gz"), lax.axis_index("gy")
     wide = rows + 8
@@ -252,18 +279,20 @@
     def prepare(*ranges):
         def body(h, _):
             for start, count in ranges:
-                here = plane(m_pad, h, start)
-                from_behind = times(plane(w_pad, 0, start - 1), plane(m_pad, h, start - 1))
+                here = plane(m_at(start), h, start)
+                from_behind = times(
+                    plane(w_at(start - 1), 0, start - 1), plane(m_at(start - 1), h, start - 1)
+                )
                 for p in range(start, start + count):
-                    ahead = plane(m_pad, h, p + 1)
-                    w_z, w_y, w_x = (plane(w_pad, i, p) for i in range(3))
+                    ahead = plane(m_at(p + 1), h, p + 1)
+                    w_z, w_y, w_x = (plane(w_at(p), i, p) for i in range(3))
                     sums_ = each(
                         lambda a, b, c, d, e, f: (a + b) + (c + d) + (e + f),
                         times(w_z, ahead), from_behind,
                         times(w_y, next_y(here)), prev_y(times(w_y, here)),
                         times(w_x, next_x(here)), prev_x(times(w_x, here)),
                     )
-                    other = plane(m_pad, 1 - h, p)
+                    other = plane(m_at(p), 1 - h, p)
                     u = each(lambda a, b: jnp.where(a + b == 0.0, 1.0, 0.0), here, other)
                     store_plane(free, (p,), u)
                     sums_ = times(sums_, u)
@@ -279,19 +308,23 @@
     def flow(w, x, y):
         return each(lambda a, b, c: a * (b - c), w, x, y)
 
-    def apply(source, target, *ranges):
+    def apply(source, n, margin, target, *ranges):
+        def v_at(p):
+            return at(p, source, n, margin)
+
         def body(c, _):
             for start, count in ranges:
-                here = plane(source, c, start)
-                from_behind = flow(plane(w_pad, 0, start - 1), here, plane(source, c, start - 1))
+                here = plane(v_at(start), c, start)
+                behind = plane(v_at(start - 1), c, start - 1)
+                from_behind = flow(plane(w_at(start - 1), 0, start - 1), here, behind)
                 for p in range(start, start + count):
-                    ahead = plane(source, c, p + 1)
-                    f_z = flow(plane(w_pad, 0, p), ahead, here)
-                    f_y = flow(plane(w_pad, 1, p), next_y(here), here)
-                    f_x = flow(plane(w_pad, 2, p), next_x(here), here)
+                    ahead = plane(v_at(p + 1), c, p + 1)
+                    f_z = flow(plane(w_at(p), 0, p), ahead, here)
+                    f_y = flow(plane(w_at(p), 1, p), next_y(here), here)
+                    f_x = flow(plane(w_at(p), 2, p), next_x(here), here)
                     store_plane(target, (c, p), each(
                         lambda u, a, b, c, d, e, f: u * ((a - b) + (c - d) + (e - f)),
-                        plane(free, p), from_behind, f_z, prev_y(f_y), f_y, prev_x(f_x), f_x,
+                        plane(free_at(p), p), from_behind, f_z, prev_y(f_y), f_y, prev_x(f_x), f_x,
                     ))
                     from_behind, here = f_z, ahead
             return 0
@@ -335,10 +368,14 @@
 
     def accumulate_last(p, _):
         parts = [[] for _ in range(36)]
-        w_z, w_y, w_x = (plane(w_pad, i, p) for i in range(3))
+        own_w = w_pad if given is None else given[1]
+        w_z, w_y, w_x = (plane(own_w, i, p) for i in range(3))
+        w_zb = plane(own_w, 0, jnp.maximum(p - 1, LO))
+        if given is not None:
+            w_zb = each(lambda a, b: jnp.where(p == LO, a, b), plane(w_pad, 0, LO - 1), w_zb)
         degree = each(
             lambda a, b, c, d, e, f: (a + b) + (c + d) + (e + f),
-            w_z, plane(w_pad, 0, p - 1), w_y, prev_y(w_y), w_x, prev_x(w_x),
+            w_z, w_zb, w_y, prev_y(w_y), w_x, prev_x(w_x),
         )
         qs, aabs_ = [], []
         for c in range(LABELS):
@@ -366,7 +403,8 @@
 
     return types.SimpleNamespace(
         put=put, cut_edges=cut_edges, prepare=prepare,
-        first=functools.partial(apply, b_pad, v1), second=functools.partial(apply, v1, v2), accumulate=accumulate, accumulate_last=accumulate_last,
+        first=functools.partial(apply, b_pad, 3, 1, v1),
+        second=functools.partial(apply, v1, 4, 2, v2), accumulate=accumulate, accumulate_last=accumulate_last,
         half_pairs=half_pairs, all_pairs=all_pairs, own=own, ring=ring,
     )
 
@@ -428,7 +466,10 @@
     depth, rows, cols = fields.shape[2:]
     f32 = jnp.float32
     y_is_even = lax.axis_index("gy") % 2 == 0
-    do = krylov_steps(counts, depth, rows, cols, m_pad, w_pad, free, b_pad, v1, v2, acc, fields, True)
+    given = (m_in, w_in, free_in, b_in, v1_in)
+    do = krylov_steps(
+        counts, depth, rows, cols, m_pad, w_pad, free, b_pad, v1, v2, acc, fields, True, given
+    )
     for n, (a, i) in enumerate(Z_PLANES):
         do.put(a, LO + depth + i, do.own, after[n])
         if LO - Z_WIDTHS[a] + i >= 0:
@@ -444,17 +485,13 @@
     do.put(3, 0, do.ring, zero_tile)
     low, high = LO, LO + depth
     for source, target, planes in (
-        (m_in, m_pad, (low, low + 1, high - 2, high - 1)),
-        (w_in, w_pad, range(low, high)),
-        (b_in, b_pad, (low + 1, low + 2, high - 3, high - 2)),
-        (v1_in, v1, (low + 2, low + 3, high - 4, high - 3)),
+        (b_in, b_pad, (low + 1, high - 2)),
+        (v1_in, v1, (low + 2, high - 4, high - 3)),
         (v2_in, v2, (low + 3, high - 4)),
     ):
         for p in planes:
-            for c in range(source.shape[0]):
+            for c in range(LABELS):
                 target[c, p] = source[c, p]
-    for p in (low + 1, low + 2, high - 3, high - 2):
-        free[p] = free_in[p]
     for n in range(66):
         acc[n] = acc_in[n]
     do.cut_edges([p for p in range(high + 3) if p not in range(low, high)])
@@ -520,7 +557,7 @@
     for k in range(n):
         pivot = system[k, k]
         sound = pivot > floor * first[k]
-        inverse[k] = jnp.where(sound, 1.0 / jnp.where(sound, pivot, 1.0), 0.0)
+        inverse[k] = jnp.where(sound, 1.0 / pivot, 0.0)
         for i in range(k + 1, n):
             lower[i, k] = system[i, k] * inverse[k]
         for i in range(k + 1, n):
@@ -559,6 +596,7 @@
         coeffs[k] = x
 
     back = interleave(cols, back=True)
+    back = jnp.concatenate([back, back], axis=0)
     chunk = depth // CHUNKS
 
     def field(k, p, cut):
@@ -592,8 +630,7 @@
         x = mixed[:, planes].reshape(LABELS * chunk * rows, cols)
         high = x.astype(jnp.bfloat16)
         low = (x - high.astype(f32)).astype(jnp.bfloat16)
-        x = jnp.dot(high, back, preferred_element_type=f32)
-        x = x + jnp.dot(low, back, preferred_element_type=f32)
+        x = jnp.dot(jnp.concatenate([high, low], axis=1), back, preferred_element_type=f32)
         x = x.reshape(LABELS, chunk, rows, cols)
         for c in range(LABELS):
             buffer[c, planes] = jnp.where(natural[0, planes] == c, 1.0, x[c])

time: 33.2 us -> 33 us (level)
  transfers between devices with their start and end apart: 11 -> 11, of which waited for: 6 -> 6; matrix products, arithmetic and copies ran while one was open for 0% -> 0% of each run, Pallas kernels for 4% -> 5%
where the time goes in v7:
time: 33 us; the launch traced here: 32.9 us
  starting transfers between devices  15 us (45%)
  waiting for transfers between devices  8.84 us (27%)
  Pallas kernels  7.65 us (23%)
  other arithmetic  1.29 us (4%)
    ppermute x11, starting transfers between devices, exchanged(): return lax.ppermute(array, axes, route)  15 us
    ppermute x11, waiting for transfers between devices, exchanged(): return lax.ppermute(array, axes, route)  8.84 us
    pallas_call x1, Pallas kernels, outer(): pl.pallas_call(functools.partial(outer_kernel, counts), out_shape=[jax.Sh...  3.39 us
    pallas_call x1, Pallas kernels, combined(): pl.pallas_call(combine_kernel, out_shape=jax.ShapeDtypeStruct((LABELS, de...  2.26 us
    pallas_call x1, Pallas kernels, inner(): pl.pallas_call(functools.partial(inner_kernel, counts), out_shape=[jax.Sh...  1.33 us
    another operation x1, other arithmetic, per_device(): natural = jnp.stack([tags, depth_affinity, row_affinity, column_affinity])  1.28 us
  transfers between devices with their start and end apart: 11, of which 6 were waited for; matrix products, arithmetic and copies ran while one was open for 0% of the time, Pallas kernels for 5%

profile of v7, /device:TPU:0, one launch (start us, length us, event | category | flops | bytes accessed | tf_op | source)
XLA Modules:
  0.0 32.9 jit_solution(11865689868919811005)
XLA Ops:
  0.0 1.3 %pad_add_fusion.natural = s32[4,8,16,384]{3,2,1,0:T(8,128)S(1)} fusion(s32[1,8,16,384]{3,2,1,0:T(8,128)} %bitcast.4, s32[1,8,16,384]{3,2,1,0:T(8,128)} %bitcast.5, s32[1,8,16,384]{3,2,1,0:T(8,128)} %bitcast.6, s32[1,8,16,384]{3,2,1,0:T(8,128)} %bitcast.7), kind=kLoop, calls=%fused_computation | loop fusion | flops 589824 | bytes 1572864 | tf_op jit(solution)/shard_map/stack | solution.py:676
  1.3 0.5 %shard_map.46 = (f32[4,8,16,384]{3,2,1,0:T(8,128)S(1)}, f32[13,16,384]{2,1,0:T(8,128)S(1)}, f32[13,16,384]{2,1,0:T(8,128)S(1)}) custom-call(s32[4,8,16,384]{3,2,1,0:T(8,128)S(1)} %pad_add_fusion.natural), custom_call_target="tpu_custom_call" | custom-call | tf_op jit(solution)/shard_map/pallas_call | solution.py:117
  1.8 3.1 %collective-permute-start = (f32[13,16,384]{2,1,0:T(8,128)S(1)}, f32[13,16,384]{2,1,0:T(8,128)S(1)}, u32[]{:S(2)}, u32[]{:S(2)}) collective-permute-start(f32[13,16,384]{2,1,0:T(8,128)S(1)} %get-tuple-element.26), channel_id=1, source_target_pairs={{0,4},{1,5},{2,6},{3,7},{4,0},{5,1},{6,2},{7,3},{8,12},{9,13},{10,... | collective-permute-start | bytes 958472 | tf_op jit(solution)/shard_map/ppermute | solution.py:48
  4.9 0.0 collective-permute-start.1
  4.9 0.1 shard_map.47
  4.9 1.6 %collective-permute-start.2 = (f32[16,8,384]{2,1,0:T(8,128)S(1)}, f32[16,8,384]{2,1,0:T(8,128)S(1)}, u32[]{:S(2)}, u32[]{:S(2)}) collective-permute-start(f32[16,8,384]{2,1,0:T(8,128)S(1)} %get-tuple-element.29), channel_id=1, source_target_pairs={{0,16},{1,2},{2,1},{3,19},{4,20},{5,6},{6,5},{7,23},{8,24},{9,10},... | collective-permute-start | bytes 589832 | tf_op jit(solution)/shard_map/ppermute | solution.py:48
  6.5 0.5 %collective-permute-start.3 = (f32[3,8,384]{2,1,0:T(8,128)S(1)}, f32[3,8,384]{2,1,0:T(8,128)S(1)}, u32[]{:S(2)}, u32[]{:S(2)}) collective-permute-start(f32[3,8,384]{2,1,0:T(8,128)S(1)} %get-tuple-element.32), channel_id=1, source_target_pairs={{0,16},{1,6},{2,5},{3,19},{4,20},{5,2},{6,1},{7,23},{8,24},{9,14},... | collective-permute-start | bytes 110600 | tf_op jit(solution)/shard_map/ppermute | solution.py:48
  7.0 2.2 %collective-permute-start.4 = (f32[3,8,384]{2,1,0:T(8,128)S(1)}, f32[3,8,384]{2,1,0:T(8,128)S(1)}, u32[]{:S(2)}, u32[]{:S(2)}) collective-permute-start(f32[3,8,384]{2,1,0:T(8,128)S(1)} %get-tuple-element.33), channel_id=1, source_target_pairs={{0,1},{1,0},{2,3},{3,2},{4,20},{5,10},{6,9},{7,23},{8,24},{9,6},{1... | collective-permute-start | bytes 110600 | tf_op jit(solution)/shard_map/ppermute | solution.py:48
  9.3 1.4 %collective-permute-done.2.y_odd = f32[16,8,384]{2,1,0:T(8,128)S(1)} collective-permute-done((f32[16,8,384]{2,1,0:T(8,128)S(1)}, f32[16,8,384]{2,1,0:T(8,128)S(1)}, u32[]{:S(2)}, u32[]{:S(2)}) %collective-permute-start.2) | collective-permute-done | bytes 196640 | tf_op jit(solution)/shard_map/ppermute | solution.py:48
  10.7 0.2 collective-permute-start.6
  10.9 1.9 %collective-permute-done.z_even = f32[13,16,384]{2,1,0:T(8,128)S(1)} collective-permute-done((f32[13,16,384]{2,1,0:T(8,128)S(1)}, f32[13,16,384]{2,1,0:T(8,128)S(1)}, u32[]{:S(2)}, u32[]{:S(2)}) %collective-permute-start) | collective-permute-done | bytes 319520 | tf_op jit(solution)/shard_map/ppermute | solution.py:48
  12.8 0.1 shard_map.48
  12.9 0.1 collective-permute-start.5
  13.0 1.3 %shard_map.50 = (f32[2,15,24,384]{3,2,1,0:T(8,128)S(1)}, f32[3,15,24,384]{3,2,1,0:T(8,128)S(1)}, f32[15,24,384]{2,1,0:T(8,128)S(1)}, f32[4,15,24,384]{3,2,1,0:T(...) custom-call(f32[4,8,16,384]{3,2,1,0:T(8,128)S(1)} %get-tuple-element.28.arrays, ...), custom_call_target="tpu_custom_call" | custom-call | flops 10000000 | bytes 1000000 | tf_op jit(solution)/shard_map/pallas_call | solution.py:450
  14.4 3.4 %shard_map.51 = (f32[3,4,8,16,384]{4,3,2,1,0:T(8,128)S(1)}, f32[8,128]{1,0:T(8,128)S(1)}) custom-call(f32[13,16,384]{2,1,0:T(8,128)S(1)} %get-tuple-element.30.before, f32[13,16,384]{2,1,0:T(8,128)S(1)} %get-tuple-element.31.after, f32[11,8,384]{2,1,0:T(8,128)S(1)} %get-tuple-element.34.d_before, f32[11,8,384]{2,1,0:T(8,128)S(1)} %get-tuple-element.35.d_after, ...), custom_call_target="tpu_custom_call" | custom-call | tf_op jit(solution)/shard_map/pallas_call | solution.py:534
  17.8 0.8 %collective-permute-start.7 = (f32[8,128]{1,0:T(8,128)S(1)}, f32[8,128]{1,0:T(8,128)S(1)}, u32[]{:S(2)}, u32[]{:S(2)}) collective-permute-start(f32[8,128]{1,0:T(8,128)S(1)} %get-tuple-element.45), channel_id=1, source_target_pairs={{0,1},{1,0},{2,3},{3,2},{4,5},{5,4},{6,7},{7,6},{8,9},{9,8},{10,11... | collective-permute-start | bytes 12296 | tf_op jit(solution)/shard_map/ppermute | solution.py:48
  18.5 0.8 %collective-permute-done.7 = f32[8,128]{1,0:T(8,128)S(1)} collective-permute-done((f32[8,128]{1,0:T(8,128)S(1)}, f32[8,128]{1,0:T(8,128)S(1)}, u32[]{:S(2)}, u32[]{:S(2)}) %collective-permute-start.7) | collective-permute-done | bytes 4128 | tf_op jit(solution)/shard_map/ppermute | solution.py:48
  19.4 1.0 %collective-permute-start.8 = (f32[8,128]{1,0:T(8,128)S(1)}, f32[8,128]{1,0:T(8,128)S(1)}, u32[]{:S(2)}, u32[]{:S(2)}) collective-permute-start(f32[8,128]{1,0:T(8,128)S(1)} %add.9), channel_id=1, source_target_pairs={{0,3},{1,2},{2,1},{3,0},{4,7},{5,6},{6,5},{7,4},{8,11},{9,10},{10,... | collective-permute-start | bytes 12296 | tf_op jit(solution)/shard_map/ppermute | solution.py:48
  20.3 2.1 %collective-permute-done.8 = f32[8,128]{1,0:T(8,128)S(1)} collective-permute-done((f32[8,128]{1,0:T(8,128)S(1)}, f32[8,128]{1,0:T(8,128)S(1)}, u32[]{:S(2)}, u32[]{:S(2)}) %collective-permute-start.8) | collective-permute-done | bytes 4128 | tf_op jit(solution)/shard_map/ppermute | solution.py:48
  22.4 2.6 %collective-permute-start.9 = (f32[8,128]{1,0:T(8,128)S(1)}, f32[8,128]{1,0:T(8,128)S(1)}, u32[]{:S(2)}, u32[]{:S(2)}) collective-permute-start(f32[8,128]{1,0:T(8,128)S(1)} %add.10), channel_id=1, source_target_pairs={{0,5},{1,4},{2,7},{3,6},{4,1},{5,0},{6,3},{7,2},{8,13},{9,12},{10,... | collective-permute-start | bytes 12296 | tf_op jit(solution)/shard_map/ppermute | solution.py:48
  25.0 1.3 %collective-permute-done.9 = f32[8,128]{1,0:T(8,128)S(1)} collective-permute-done((f32[8,128]{1,0:T(8,128)S(1)}, f32[8,128]{1,0:T(8,128)S(1)}, u32[]{:S(2)}, u32[]{:S(2)}) %collective-permute-start.9) | collective-permute-done | bytes 4128 | tf_op jit(solution)/shard_map/ppermute | solution.py:48
  26.4 2.9 %collective-permute-start.10 = (f32[8,128]{1,0:T(8,128)S(1)}, f32[8,128]{1,0:T(8,128)S(1)}, u32[]{:S(2)}, u32[]{:S(2)}) collective-permute-start(f32[8,128]{1,0:T(8,128)S(1)} %add.11.mine), channel_id=1, source_target_pairs={{0,9},{1,8},{2,11},{3,10},{4,13},{5,12},{6,15},{7,14},{8,1},{9,0},... | collective-permute-start | bytes 12296 | tf_op jit(solution)/shard_map/ppermute | solution.py:48
  29.3 1.3 %collective-permute-done.10.theirs = f32[8,128]{1,0:T(8,128)S(1)} collective-permute-done((f32[8,128]{1,0:T(8,128)S(1)}, f32[8,128]{1,0:T(8,128)S(1)}, u32[]{:S(2)}, u32[]{:S(2)}) %collective-permute-start.10) | collective-permute-done | bytes 4128 | tf_op jit(solution)/shard_map/ppermute | solution.py:48
  30.6 2.3 %shard_map.52 = f32[4,8,16,384]{3,2,1,0:T(8,128)} custom-call(f32[8,128]{1,0:T(8,128)S(1)} %add.11.mine, f32[8,128]{1,0:T(8,128)S(1)} %collective-permute-done.10.theirs, f32[3,4,8,16,384]{4,3,2,1,0:T(8,128)S(1)} %get-tuple-element.46.fields, f32[4,15,24,384]{3,2,1,0:T(8,128)S(1)} %get-tuple-element.41.b_in, f32[4,15,24,384]{3,2,1,0:T(8,128)S(1)} %get-tuple-element.42.v1_in, ...), custom_call_target="tpu_custom_call" | custom-call | tf_op jit(solution)/shard_map/pallas_call | solution.py:658
  (9 shorter events, 0.1 us)
Async XLA Ops:
  1.8 11.0 %collective-permute-start = (f32[13,16,384]{2,1,0:T(8,128)S(1)}, f32[13,16,384]{2,1,0:T(8,128)S(1)}, u32[]{:S(2)}, u32[]{:S(2)}) collective-permute-start(f32[13,16,384]{2,1,0:T(8,128)S(1)} %get-tuple-element.26), channel_id=1, source_target_pairs={{0,4},{1,5},{2,6},{3,7},{4,0},{5,1},{6,2},{7,3},{8,12},{9,13},{10,... | collective-permute-start | bytes 958472 | tf_op jit(solution)/shard_map/ppermute | solution.py:48
  4.9 7.9 %collective-permute-start.1 = (f32[13,16,384]{2,1,0:T(8,128)S(1)}, f32[13,16,384]{2,1,0:T(8,128)S(1)}, u32[]{:S(2)}, u32[]{:S(2)}) collective-permute-start(f32[13,16,384]{2,1,0:T(8,128)S(1)} %get-tuple-element.27), channel_id=1, source_target_pairs={{0,1},{1,0},{2,3},{3,2},{4,8},{5,9},{6,10},{7,11},{8,4},{9,5},{10,... | collective-permute-start | bytes 958472 | tf_op jit(solution)/shard_map/ppermute | solution.py:48
  4.9 5.7 %collective-permute-start.2 = (f32[16,8,384]{2,1,0:T(8,128)S(1)}, f32[16,8,384]{2,1,0:T(8,128)S(1)}, u32[]{:S(2)}, u32[]{:S(2)}) collective-permute-start(f32[16,8,384]{2,1,0:T(8,128)S(1)} %get-tuple-element.29), channel_id=1, source_target_pairs={{0,16},{1,2},{2,1},{3,19},{4,20},{5,6},{6,5},{7,23},{8,24},{9,10},... | collective-permute-start | bytes 589832 | tf_op jit(solution)/shard_map/ppermute | solution.py:48
  6.5 6.4 %collective-permute-start.3 = (f32[3,8,384]{2,1,0:T(8,128)S(1)}, f32[3,8,384]{2,1,0:T(8,128)S(1)}, u32[]{:S(2)}, u32[]{:S(2)}) collective-permute-start(f32[3,8,384]{2,1,0:T(8,128)S(1)} %get-tuple-element.32), channel_id=1, source_target_pairs={{0,16},{1,6},{2,5},{3,19},{4,20},{5,2},{6,1},{7,23},{8,24},{9,14},... | collective-permute-start | bytes 110600 | tf_op jit(solution)/shard_map/ppermute | solution.py:48
  7.0 5.9 %collective-permute-start.4 = (f32[3,8,384]{2,1,0:T(8,128)S(1)}, f32[3,8,384]{2,1,0:T(8,128)S(1)}, u32[]{:S(2)}, u32[]{:S(2)}) collective-permute-start(f32[3,8,384]{2,1,0:T(8,128)S(1)} %get-tuple-element.33), channel_id=1, source_target_pairs={{0,1},{1,0},{2,3},{3,2},{4,20},{5,10},{6,9},{7,23},{8,24},{9,6},{1... | collective-permute-start | bytes 110600 | tf_op jit(solution)/shard_map/ppermute | solution.py:48
  10.7 2.4 %collective-permute-start.6 = (f32[16,8,384]{2,1,0:T(8,128)S(1)}, f32[16,8,384]{2,1,0:T(8,128)S(1)}, u32[]{:S(2)}, u32[]{:S(2)}) collective-permute-start(f32[16,8,384]{2,1,0:T(8,128)S(1)} %get-tuple-element.37), channel_id=1, source_target_pairs={{0,1},{1,0},{2,3},{3,2},{4,5},{5,4},{6,7},{7,6},{8,9},{9,8},{10,11... | collective-permute-start | bytes 589832 | tf_op jit(solution)/shard_map/ppermute | solution.py:48
  12.9 1.5 %collective-permute-start.5 = (f32[11,8,384]{2,1,0:T(8,128)S(1)}, f32[11,8,384]{2,1,0:T(8,128)S(1)}, u32[]{:S(2)}, u32[]{:S(2)}) collective-permute-start(f32[11,8,384]{2,1,0:T(8,128)S(1)} %get-tuple-element.36), channel_id=1, source_target_pairs={{0,1},{1,0},{2,3},{3,2},{4,5},{5,4},{6,7},{7,6},{8,9},{9,8},{10,11... | collective-permute-start | bytes 405512 | tf_op jit(solution)/shard_map/ppermute | solution.py:48
  17.8 1.6 %collective-permute-start.7 = (f32[8,128]{1,0:T(8,128)S(1)}, f32[8,128]{1,0:T(8,128)S(1)}, u32[]{:S(2)}, u32[]{:S(2)}) collective-permute-start(f32[8,128]{1,0:T(8,128)S(1)} %get-tuple-element.45), channel_id=1, source_target_pairs={{0,1},{1,0},{2,3},{3,2},{4,5},{5,4},{6,7},{7,6},{8,9},{9,8},{10,11... | collective-permute-start | bytes 12296 | tf_op jit(solution)/shard_map/ppermute | solution.py:48
  19.4 3.0 %collective-permute-start.8 = (f32[8,128]{1,0:T(8,128)S(1)}, f32[8,128]{1,0:T(8,128)S(1)}, u32[]{:S(2)}, u32[]{:S(2)}) collective-permute-start(f32[8,128]{1,0:T(8,128)S(1)} %add.9), channel_id=1, source_target_pairs={{0,3},{1,2},{2,1},{3,0},{4,7},{5,6},{6,5},{7,4},{8,11},{9,10},{10,... | collective-permute-start | bytes 12296 | tf_op jit(solution)/shard_map/ppermute | solution.py:48
  22.4 4.0 %collective-permute-start.9 = (f32[8,128]{1,0:T(8,128)S(1)}, f32[8,128]{1,0:T(8,128)S(1)}, u32[]{:S(2)}, u32[]{:S(2)}) collective-permute-start(f32[8,128]{1,0:T(8,128)S(1)} %add.10), channel_id=1, source_target_pairs={{0,5},{1,4},{2,7},{3,6},{4,1},{5,0},{6,3},{7,2},{8,13},{9,12},{10,... | collective-permute-start | bytes 12296 | tf_op jit(solution)/shard_map/ppermute | solution.py:48
  26.4 4.2 %collective-permute-start.10 = (f32[8,128]{1,0:T(8,128)S(1)}, f32[8,128]{1,0:T(8,128)S(1)}, u32[]{:S(2)}, u32[]{:S(2)}) collective-permute-start(f32[8,128]{1,0:T(8,128)S(1)} %add.11.mine), channel_id=1, source_target_pairs={{0,9},{1,8},{2,11},{3,10},{4,13},{5,12},{6,15},{7,14},{8,1},{9,0},... | collective-permute-start | bytes 12296 | tf_op jit(solution)/shard_map/ppermute | solution.py:48

commit v8 on v7

--- a/solution.py
+++ b/solution.py
@@ -303,7 +303,8 @@
                     here = ahead
             return 0
 
-        repeated(2, body)
+        for n in range(2):
+            body(n, 0)
 
     def flow(w, x, y):
         return each(lambda a, b, c: a * (b - c), w, x, y)
@@ -329,7 +330,7 @@
                     from_behind, here = f_z, ahead
             return 0
 
-        repeated(LABELS, body)
+        repeated(LABELS // 2, lambda n, x: body(2 * n + 1, body(2 * n, x)))
 
     half_pairs = [(a, b) for a in range(LABELS) for b in range(a, LABELS)]
     all_pairs = [(a, b) for a in range(LABELS) for b in range(LABELS)]

time: 33 us -> 32.7 us (level)
  no operation moved by 1% of the time
where the time goes in v8:
time: 32.7 us; the launch traced here: 32.5 us
  starting transfers between devices  15 us (46%)
  waiting for transfers between devices  8.84 us (27%)
  Pallas kernels  7.35 us (22%)
  other arithmetic  1.29 us (4%)
    ppermute x11, starting transfers between devices, exchanged(): return lax.ppermute(array, axes, route)  15 us
    ppermute x11, waiting for transfers between devices, exchanged(): return lax.ppermute(array, axes, route)  8.84 us
    pallas_call x1, Pallas kernels, outer(): pl.pallas_call(functools.partial(outer_kernel, counts), out_shape=[jax.Sh...  3.09 us
    pallas_call x1, Pallas kernels, combined(): pl.pallas_call(combine_kernel, out_shape=jax.ShapeDtypeStruct((LABELS, de...  2.26 us
    pallas_call x1, Pallas kernels, inner(): pl.pallas_call(functools.partial(inner_kernel, counts), out_shape=[jax.Sh...  1.33 us
    another operation x1, other arithmetic, per_device(): natural = jnp.stack([tags, depth_affinity, row_affinity, column_affinity])  1.28 us
  transfers between devices with their start and end apart: 11, of which 6 were waited for; matrix products, arithmetic and copies ran while one was open for 0% of the time, Pallas kernels for 5%

profile of v8, /device:TPU:0, one launch (start us, length us, event | category | flops | bytes accessed | tf_op | source)
XLA Modules:
  0.0 32.5 jit_solution(4868547799299482231)
XLA Ops:
  0.0 1.3 %pad_add_fusion.natural = s32[4,8,16,384]{3,2,1,0:T(8,128)S(1)} fusion(s32[1,8,16,384]{3,2,1,0:T(8,128)} %bitcast.4, s32[1,8,16,384]{3,2,1,0:T(8,128)} %bitcast.5, s32[1,8,16,384]{3,2,1,0:T(8,128)} %bitcast.6, s32[1,8,16,384]{3,2,1,0:T(8,128)} %bitcast.7), kind=kLoop, calls=%fused_computation | loop fusion | flops 589824 | bytes 1572864 | tf_op jit(solution)/shard_map/stack | solution.py:677
  1.3 0.5 %shard_map.46 = (f32[4,8,16,384]{3,2,1,0:T(8,128)S(1)}, f32[13,16,384]{2,1,0:T(8,128)S(1)}, f32[13,16,384]{2,1,0:T(8,128)S(1)}) custom-call(s32[4,8,16,384]{3,2,1,0:T(8,128)S(1)} %pad_add_fusion.natural), custom_call_target="tpu_custom_call" | custom-call | tf_op jit(solution)/shard_map/pallas_call | solution.py:117
  1.8 3.1 %collective-permute-start = (f32[13,16,384]{2,1,0:T(8,128)S(1)}, f32[13,16,384]{2,1,0:T(8,128)S(1)}, u32[]{:S(2)}, u32[]{:S(2)}) collective-permute-start(f32[13,16,384]{2,1,0:T(8,128)S(1)} %get-tuple-element.26), channel_id=1, source_target_pairs={{0,4},{1,5},{2,6},{3,7},{4,0},{5,1},{6,2},{7,3},{8,12},{9,13},{10,... | collective-permute-start | bytes 958472 | tf_op jit(solution)/shard_map/ppermute | solution.py:48
  4.9 0.0 collective-permute-start.1
  4.9 0.1 shard_map.47
  4.9 1.6 %collective-permute-start.2 = (f32[16,8,384]{2,1,0:T(8,128)S(1)}, f32[16,8,384]{2,1,0:T(8,128)S(1)}, u32[]{:S(2)}, u32[]{:S(2)}) collective-permute-start(f32[16,8,384]{2,1,0:T(8,128)S(1)} %get-tuple-element.29), channel_id=1, source_target_pairs={{0,16},{1,2},{2,1},{3,19},{4,20},{5,6},{6,5},{7,23},{8,24},{9,10},... | collective-permute-start | bytes 589832 | tf_op jit(solution)/shard_map/ppermute | solution.py:48
  6.5 0.5 %collective-permute-start.3 = (f32[3,8,384]{2,1,0:T(8,128)S(1)}, f32[3,8,384]{2,1,0:T(8,128)S(1)}, u32[]{:S(2)}, u32[]{:S(2)}) collective-permute-start(f32[3,8,384]{2,1,0:T(8,128)S(1)} %get-tuple-element.32), channel_id=1, source_target_pairs={{0,16},{1,6},{2,5},{3,19},{4,20},{5,2},{6,1},{7,23},{8,24},{9,14},... | collective-permute-start | bytes 110600 | tf_op jit(solution)/shard_map/ppermute | solution.py:48
  7.0 2.2 %collective-permute-start.4 = (f32[3,8,384]{2,1,0:T(8,128)S(1)}, f32[3,8,384]{2,1,0:T(8,128)S(1)}, u32[]{:S(2)}, u32[]{:S(2)}) collective-permute-start(f32[3,8,384]{2,1,0:T(8,128)S(1)} %get-tuple-element.33), channel_id=1, source_target_pairs={{0,1},{1,0},{2,3},{3,2},{4,20},{5,10},{6,9},{7,23},{8,24},{9,6},{1... | collective-permute-start | bytes 110600 | tf_op jit(solution)/shard_map/ppermute | solution.py:48
  9.3 1.4 %collective-permute-done.2.y_odd = f32[16,8,384]{2,1,0:T(8,128)S(1)} collective-permute-done((f32[16,8,384]{2,1,0:T(8,128)S(1)}, f32[16,8,384]{2,1,0:T(8,128)S(1)}, u32[]{:S(2)}, u32[]{:S(2)}) %collective-permute-start.2) | collective-permute-done | bytes 196640 | tf_op jit(solution)/shard_map/ppermute | solution.py:48
  10.7 0.2 collective-permute-start.6
  10.9 1.9 %collective-permute-done.z_even = f32[13,16,384]{2,1,0:T(8,128)S(1)} collective-permute-done((f32[13,16,384]{2,1,0:T(8,128)S(1)}, f32[13,16,384]{2,1,0:T(8,128)S(1)}, u32[]{:S(2)}, u32[]{:S(2)}) %collective-permute-start) | collective-permute-done | bytes 319520 | tf_op jit(solution)/shard_map/ppermute | solution.py:48
  12.8 0.1 shard_map.48
  12.9 0.1 collective-permute-start.5
  13.0 1.3 %shard_map.50 = (f32[2,15,24,384]{3,2,1,0:T(8,128)S(1)}, f32[3,15,24,384]{3,2,1,0:T(8,128)S(1)}, f32[15,24,384]{2,1,0:T(8,128)S(1)}, f32[4,15,24,384]{3,2,1,0:T(...) custom-call(f32[4,8,16,384]{3,2,1,0:T(8,128)S(1)} %get-tuple-element.28.arrays, ...), custom_call_target="tpu_custom_call" | custom-call | flops 10000000 | bytes 1000000 | tf_op jit(solution)/shard_map/pallas_call | solution.py:451
  14.4 3.1 %shard_map.51 = (f32[3,4,8,16,384]{4,3,2,1,0:T(8,128)S(1)}, f32[8,128]{1,0:T(8,128)S(1)}) custom-call(f32[13,16,384]{2,1,0:T(8,128)S(1)} %get-tuple-element.30.before, f32[13,16,384]{2,1,0:T(8,128)S(1)} %get-tuple-element.31.after, f32[11,8,384]{2,1,0:T(8,128)S(1)} %get-tuple-element.34.d_before, f32[11,8,384]{2,1,0:T(8,128)S(1)} %get-tuple-element.35.d_after, ...), custom_call_target="tpu_custom_call" | custom-call | tf_op jit(solution)/shard_map/pallas_call | solution.py:535
  17.5 0.8 %collective-permute-start.7 = (f32[8,128]{1,0:T(8,128)S(1)}, f32[8,128]{1,0:T(8,128)S(1)}, u32[]{:S(2)}, u32[]{:S(2)}) collective-permute-start(f32[8,128]{1,0:T(8,128)S(1)} %get-tuple-element.45), channel_id=1, source_target_pairs={{0,1},{1,0},{2,3},{3,2},{4,5},{5,4},{6,7},{7,6},{8,9},{9,8},{10,11... | collective-permute-start | bytes 12296 | tf_op jit(solution)/shard_map/ppermute | solution.py:48
  18.2 0.8 %collective-permute-done.7 = f32[8,128]{1,0:T(8,128)S(1)} collective-permute-done((f32[8,128]{1,0:T(8,128)S(1)}, f32[8,128]{1,0:T(8,128)S(1)}, u32[]{:S(2)}, u32[]{:S(2)}) %collective-permute-start.7) | collective-permute-done | bytes 4128 | tf_op jit(solution)/shard_map/ppermute | solution.py:48
  19.1 1.0 %collective-permute-start.8 = (f32[8,128]{1,0:T(8,128)S(1)}, f32[8,128]{1,0:T(8,128)S(1)}, u32[]{:S(2)}, u32[]{:S(2)}) collective-permute-start(f32[8,128]{1,0:T(8,128)S(1)} %add.9), channel_id=1, source_target_pairs={{0,3},{1,2},{2,1},{3,0},{4,7},{5,6},{6,5},{7,4},{8,11},{9,10},{10,... | collective-permute-start | bytes 12296 | tf_op jit(solution)/shard_map/ppermute | solution.py:48
  20.0 2.1 %collective-permute-done.8 = f32[8,128]{1,0:T(8,128)S(1)} collective-permute-done((f32[8,128]{1,0:T(8,128)S(1)}, f32[8,128]{1,0:T(8,128)S(1)}, u32[]{:S(2)}, u32[]{:S(2)}) %collective-permute-start.8) | collective-permute-done | bytes 4128 | tf_op jit(solution)/shard_map/ppermute | solution.py:48
  22.1 2.6 %collective-permute-start.9 = (f32[8,128]{1,0:T(8,128)S(1)}, f32[8,128]{1,0:T(8,128)S(1)}, u32[]{:S(2)}, u32[]{:S(2)}) collective-permute-start(f32[8,128]{1,0:T(8,128)S(1)} %add.10), channel_id=1, source_target_pairs={{0,5},{1,4},{2,7},{3,6},{4,1},{5,0},{6,3},{7,2},{8,13},{9,12},{10,... | collective-permute-start | bytes 12296 | tf_op jit(solution)/shard_map/ppermute | solution.py:48
  24.7 1.3 %collective-permute-done.9 = f32[8,128]{1,0:T(8,128)S(1)} collective-permute-done((f32[8,128]{1,0:T(8,128)S(1)}, f32[8,128]{1,0:T(8,128)S(1)}, u32[]{:S(2)}, u32[]{:S(2)}) %collective-permute-start.9) | collective-permute-done | bytes 4128 | tf_op jit(solution)/shard_map/ppermute | solution.py:48
  26.1 2.9 %collective-permute-start.10 = (f32[8,128]{1,0:T(8,128)S(1)}, f32[8,128]{1,0:T(8,128)S(1)}, u32[]{:S(2)}, u32[]{:S(2)}) collective-permute-start(f32[8,128]{1,0:T(8,128)S(1)} %add.11.mine), channel_id=1, source_target_pairs={{0,9},{1,8},{2,11},{3,10},{4,13},{5,12},{6,15},{7,14},{8,1},{9,0},... | collective-permute-start | bytes 12296 | tf_op jit(solution)/shard_map/ppermute | solution.py:48
  29.0 1.3 %collective-permute-done.10.theirs = f32[8,128]{1,0:T(8,128)S(1)} collective-permute-done((f32[8,128]{1,0:T(8,128)S(1)}, f32[8,128]{1,0:T(8,128)S(1)}, u32[]{:S(2)}, u32[]{:S(2)}) %collective-permute-start.10) | collective-permute-done | bytes 4128 | tf_op jit(solution)/shard_map/ppermute | solution.py:48
  30.3 2.3 %shard_map.52 = f32[4,8,16,384]{3,2,1,0:T(8,128)} custom-call(f32[8,128]{1,0:T(8,128)S(1)} %add.11.mine, f32[8,128]{1,0:T(8,128)S(1)} %collective-permute-done.10.theirs, f32[3,4,8,16,384]{4,3,2,1,0:T(8,128)S(1)} %get-tuple-element.46.fields, f32[4,15,24,384]{3,2,1,0:T(8,128)S(1)} %get-tuple-element.41.b_in, f32[4,15,24,384]{3,2,1,0:T(8,128)S(1)} %get-tuple-element.42.v1_in, ...), custom_call_target="tpu_custom_call" | custom-call | tf_op jit(solution)/shard_map/pallas_call | solution.py:659
  (9 shorter events, 0.1 us)
Async XLA Ops:
  1.8 11.0 %collective-permute-start = (f32[13,16,384]{2,1,0:T(8,128)S(1)}, f32[13,16,384]{2,1,0:T(8,128)S(1)}, u32[]{:S(2)}, u32[]{:S(2)}) collective-permute-start(f32[13,16,384]{2,1,0:T(8,128)S(1)} %get-tuple-element.26), channel_id=1, source_target_pairs={{0,4},{1,5},{2,6},{3,7},{4,0},{5,1},{6,2},{7,3},{8,12},{9,13},{10,... | collective-permute-start | bytes 958472 | tf_op jit(solution)/shard_map/ppermute | solution.py:48
  4.9 7.9 %collective-permute-start.1 = (f32[13,16,384]{2,1,0:T(8,128)S(1)}, f32[13,16,384]{2,1,0:T(8,128)S(1)}, u32[]{:S(2)}, u32[]{:S(2)}) collective-permute-start(f32[13,16,384]{2,1,0:T(8,128)S(1)} %get-tuple-element.27), channel_id=1, source_target_pairs={{0,1},{1,0},{2,3},{3,2},{4,8},{5,9},{6,10},{7,11},{8,4},{9,5},{10,... | collective-permute-start | bytes 958472 | tf_op jit(solution)/shard_map/ppermute | solution.py:48
  4.9 5.7 %collective-permute-start.2 = (f32[16,8,384]{2,1,0:T(8,128)S(1)}, f32[16,8,384]{2,1,0:T(8,128)S(1)}, u32[]{:S(2)}, u32[]{:S(2)}) collective-permute-start(f32[16,8,384]{2,1,0:T(8,128)S(1)} %get-tuple-element.29), channel_id=1, source_target_pairs={{0,16},{1,2},{2,1},{3,19},{4,20},{5,6},{6,5},{7,23},{8,24},{9,10},... | collective-permute-start | bytes 589832 | tf_op jit(solution)/shard_map/ppermute | solution.py:48
  6.5 6.4 %collective-permute-start.3 = (f32[3,8,384]{2,1,0:T(8,128)S(1)}, f32[3,8,384]{2,1,0:T(8,128)S(1)}, u32[]{:S(2)}, u32[]{:S(2)}) collective-permute-start(f32[3,8,384]{2,1,0:T(8,128)S(1)} %get-tuple-element.32), channel_id=1, source_target_pairs={{0,16},{1,6},{2,5},{3,19},{4,20},{5,2},{6,1},{7,23},{8,24},{9,14},... | collective-permute-start | bytes 110600 | tf_op jit(solution)/shard_map/ppermute | solution.py:48
  7.0 5.9 %collective-permute-start.4 = (f32[3,8,384]{2,1,0:T(8,128)S(1)}, f32[3,8,384]{2,1,0:T(8,128)S(1)}, u32[]{:S(2)}, u32[]{:S(2)}) collective-permute-start(f32[3,8,384]{2,1,0:T(8,128)S(1)} %get-tuple-element.33), channel_id=1, source_target_pairs={{0,1},{1,0},{2,3},{3,2},{4,20},{5,10},{6,9},{7,23},{8,24},{9,6},{1... | collective-permute-start | bytes 110600 | tf_op jit(solution)/shard_map/ppermute | solution.py:48
  10.7 2.4 %collective-permute-start.6 = (f32[16,8,384]{2,1,0:T(8,128)S(1)}, f32[16,8,384]{2,1,0:T(8,128)S(1)}, u32[]{:S(2)}, u32[]{:S(2)}) collective-permute-start(f32[16,8,384]{2,1,0:T(8,128)S(1)} %get-tuple-element.37), channel_id=1, source_target_pairs={{0,1},{1,0},{2,3},{3,2},{4,5},{5,4},{6,7},{7,6},{8,9},{9,8},{10,11... | collective-permute-start | bytes 589832 | tf_op jit(solution)/shard_map/ppermute | solution.py:48
  12.9 1.5 %collective-permute-start.5 = (f32[11,8,384]{2,1,0:T(8,128)S(1)}, f32[11,8,384]{2,1,0:T(8,128)S(1)}, u32[]{:S(2)}, u32[]{:S(2)}) collective-permute-start(f32[11,8,384]{2,1,0:T(8,128)S(1)} %get-tuple-element.36), channel_id=1, source_target_pairs={{0,1},{1,0},{2,3},{3,2},{4,5},{5,4},{6,7},{7,6},{8,9},{9,8},{10,11... | collective-permute-start | bytes 405512 | tf_op jit(solution)/shard_map/ppermute | solution.py:48
  17.5 1.6 %collective-permute-start.7 = (f32[8,128]{1,0:T(8,128)S(1)}, f32[8,128]{1,0:T(8,128)S(1)}, u32[]{:S(2)}, u32[]{:S(2)}) collective-permute-start(f32[8,128]{1,0:T(8,128)S(1)} %get-tuple-element.45), channel_id=1, source_target_pairs={{0,1},{1,0},{2,3},{3,2},{4,5},{5,4},{6,7},{7,6},{8,9},{9,8},{10,11... | collective-permute-start | bytes 12296 | tf_op jit(solution)/shard_map/ppermute | solution.py:48
  19.1 3.0 %collective-permute-start.8 = (f32[8,128]{1,0:T(8,128)S(1)}, f32[8,128]{1,0:T(8,128)S(1)}, u32[]{:S(2)}, u32[]{:S(2)}) collective-permute-start(f32[8,128]{1,0:T(8,128)S(1)} %add.9), channel_id=1, source_target_pairs={{0,3},{1,2},{2,1},{3,0},{4,7},{5,6},{6,5},{7,4},{8,11},{9,10},{10,... | collective-permute-start | bytes 12296 | tf_op jit(solution)/shard_map/ppermute | solution.py:48
  22.1 4.0 %collective-permute-start.9 = (f32[8,128]{1,0:T(8,128)S(1)}, f32[8,128]{1,0:T(8,128)S(1)}, u32[]{:S(2)}, u32[]{:S(2)}) collective-permute-start(f32[8,128]{1,0:T(8,128)S(1)} %add.10), channel_id=1, source_target_pairs={{0,5},{1,4},{2,7},{3,6},{4,1},{5,0},{6,3},{7,2},{8,13},{9,12},{10,... | collective-permute-start | bytes 12296 | tf_op jit(solution)/shard_map/ppermute | solution.py:48
  26.1 4.2 %collective-permute-start.10 = (f32[8,128]{1,0:T(8,128)S(1)}, f32[8,128]{1,0:T(8,128)S(1)}, u32[]{:S(2)}, u32[]{:S(2)}) collective-permute-start(f32[8,128]{1,0:T(8,128)S(1)} %add.11.mine), channel_id=1, source_target_pairs={{0,9},{1,8},{2,11},{3,10},{4,13},{5,12},{6,15},{7,14},{8,1},{9,0},... | collective-permute-start | bytes 12296 | tf_op jit(solution)/shard_map/ppermute | solution.py:48
